TPU v7x, 128 devices: a whole 4x4x4 slice. The times are simulated.
128 devices in a mesh: sub: 8 (over x, core), slab: 16 (over y, z).
Axes of the slice: x: 4, y: 4, z: 4, core: 2. Of those that a mesh axis runs over, the one named last changes fastest.
Arguments:
- source: float32 [8, 256, 256, 256], P('sub', 'slab'), may hold values from -6 to 6
- coarse: float32 [2, 8, 256, 256, 256], P(None, 'sub', 'slab'), may hold values from -4 to 4
- rho: float32 [8], replicated, may hold values from 0.3 to 45, as said below
- basis_x: float32 [256, 256], replicated, may hold values from -0.375 to 0.375
- basis_y: float32 [256, 256], replicated, may hold values from -0.375 to 0.375
- basis_z: float32 [256, 256], replicated, may hold values from -0.375 to 0.375
- eigen_x: float32 [256], replicated, may hold values from 0.1 to 3
- eigen_y: float32 [256], replicated, may hold values from 0.1 to 3
- eigen_z: float32 [256], replicated, may hold values from 0.1 to 3
- face_stiff: float32 [256, 256], replicated, may hold values from 0.2 to 2
Outputs:
- solution: float32 [8, 256, 256, 256], P('sub', 'slab')
- multipliers: float32 [8, 256, 256], P('sub', 'slab')
- jump: float32 [8, 256, 256], P('sub', 'slab')
Inputs may be any that keep to these rules, and one draw needn't show every extreme that they name: `rho`: positive coefficient of each subdomain.
All inputs are finite; a program needn't handle non-finite values.
Results may differ from a plain program's by a relative error of at most 0.00014.
Values sent between devices are 32-bit elements; how exact they have to be, the bound alone decides.
No kernel may reach another device: no remote copies, remote signals or barrier semaphores. Data moves between devices by JAX's collectives and lax.ppermute only.
A program may use at most 128 MiB of HBM per device.

v0:
```python
import jax
import jax.numpy as jnp
from jax import lax
from jax.sharding import PartitionSpec as P

ITERS = 2


HI = lax.Precision.HIGHEST


def from_behind(block, axis, distance):
    devices = range(lax.axis_size(axis))
    route = [((i - distance) % len(devices), i) for i in devices]
    return lax.ppermute(block, axis, route)


def volume_tail(spread, basis_y, basis_z):
    slabs = lax.all_to_all(spread, "slab", split_axis=0, concat_axis=1, tiled=True)
    part = jnp.einsum("xjk,yj->xyk", slabs, basis_y, precision=HI)
    return jnp.einsum("xyk,zk->xyz", part, basis_z, precision=HI)


def on_device(
    source, coarse, rho, basis_x, basis_y, basis_z, eigen_x, eigen_y, eigen_z, face_stiff
):
    field = source[0]
    rows = field.shape[0]
    width = field.shape[1]
    sub_index = lax.axis_index("sub")
    slab_index = lax.axis_index("slab")
    subs = lax.axis_size("sub")
    own_rho = lax.dynamic_slice_in_dim(rho, sub_index, 1, 0)[0]
    next_rho = lax.dynamic_slice_in_dim(rho, (sub_index + 1) % subs, 1, 0)[0]
    weight = 0.5 * (own_rho + next_rho)
    start = slab_index * rows
    eigen_part = lax.dynamic_slice_in_dim(eigen_y, start, rows, 0)
    stiff_part = lax.dynamic_slice_in_dim(face_stiff, start, rows, 1)
    denom = (eigen_x[:, None, None] + eigen_part[None, :, None] + eigen_z[None, None, :]) * own_rho
    multipliers = jnp.zeros((rows, width), jnp.float32)
    solution = field
    jump = multipliers
    for step in range(ITERS):
        earlier = from_behind(multipliers, "sub", 1)
        load = field + coarse[step, 0]
        load = load.at[:, :, width - 1].add(-multipliers)
        load = load.at[:, :, 0].add(earlier)
        part = jnp.einsum("xyz,zk->xyk", load, basis_z, precision=HI)
        part = jnp.einsum("xyk,yj->xjk", part, basis_y, precision=HI)
        lines = lax.all_to_all(part, "slab", split_axis=1, concat_axis=0, tiled=True)
        modes = jnp.einsum("xjk,xi->ijk", lines, basis_x, precision=HI) / denom
        spread = jnp.einsum("ijk,xi->xjk", modes, basis_x, precision=HI)
        solution = volume_tail(spread, basis_y, basis_z)
        first = solution[:, :, 0]
        last = solution[:, :, width - 1]
        following = from_behind(first, "sub", -1)
        jump = last - following
        face = jnp.dot(jump, basis_y, precision=HI, preferred_element_type=jnp.float32)
        face = lax.all_to_all(face, "slab", split_axis=1, concat_axis=0, tiled=True)
        face = jnp.einsum("xj,xi->ij", face, basis_x, precision=HI) * stiff_part
        face = jnp.einsum("ij,xi->xj", face, basis_x, precision=HI)
        face = lax.all_to_all(face, "slab", split_axis=0, concat_axis=1, tiled=True)
        face = jnp.einsum("xj,yj->xy", face, basis_y, precision=HI)
        search = weight * face
        upper, lower = lax.psum((jnp.sum(jump * search), jnp.sum(search * search)), ("sub", "slab"))
        alpha = upper / (lower + 1e-06)
        multipliers = multipliers + alpha * search
    return (solution[None], multipliers[None], jump[None])


def solution(mesh):
    in_specs = (
        P("sub", "slab", None, None),
        P(None, "sub", "slab", None, None),
        P(),
        P(),
        P(),
        P(),
        P(),
        P(),
        P(),
        P(),
    )
    out_specs = (P("sub", "slab", None, None), P("sub", "slab", None), P("sub", "slab", None))
    return jax.shard_map(
        on_device, mesh=mesh, in_specs=in_specs, out_specs=out_specs, check_vma=False
    )
```

profile of v0, /device:TPU:6, one launch (start us, length us, event | category | flops | bytes accessed | tf_op | source)
XLA Modules:
  0.0 586.8 jit_solution(15697223355876928150)
XLA Ops:
  0.7 7.7 %fusion.49 = (f32[1,1,16,256,256]{4,3,2,1,0:T(8,128)}, f32[1,1,16,256,256]{4,3,2,1,0:T(8,128)}) fusion(f32[2,1,16,256,256]{4,3,2,1,0:T(8,128)} %param.19), kind=kLoop, calls=%fused_computation.76 | loop fusion | bytes 16777216 | tf_op jit(solution)/shard_map/slice | solution.py:45
  8.4 5.5 copy.88
  13.8 5.4 copy.39
  19.3 5.4 copy.89
  24.7 8.3 %bitcast_add_fusion = (f32[16,256,256]{1,0,2:T(8,128)S(1)}, f32[16,256,256]{1,0,2:T(8,128)}) fusion(f32[1,1,16,256,256]{3,2,4,1,0:T(8,128)} %copy.88, f32[1,16,256,256]{2,1,3,0:T(8,128)} %copy.39, f32[1,1,16,256,256]{3,2,4,1,0:T(8,128)} %copy.89), kind=kLoop, calls=%fused_computation.8 | loop fusion | flops 2097152 | bytes 20971520 | tf_op jit(solution)/shard_map/add | solution.py:45
  33.0 6.6 %fusion.12 = f32[16,256,256]{1,2,0:T(8,128)S(1)} fusion(f32[16,256,256]{1,0,2:T(8,128)S(1)} %fusion.39, f32[256,256]{1,0:T(8,128)S(1)} %copy-done.3), kind=kOutput, calls=%fused_computation.16 | convolution fusion | flops 3221225472 | bytes 8650752 | tf_op jit(solution)/shard_map/xyz,zk->xyk/dot_general | solution.py:48
  39.7 5.0 convolution_bitcast_fusion.1
  44.6 5.5 copy.44
  50.1 8.5 %all-to-all-start = ((f32[16,256,256]{2,0,1:T(8,128)}), f32[16,256,256]{2,0,1:T(8,128)}, u32[]{:S(2)}, u32[]{:S(2)}) async-start(f32[16,256,256]{2,0,1:T(8,128)} %copy.44), calls=%async_computation | async-start | bytes 8388608 | tf_op jit(solution)/shard_map/all_to_all | solution.py:50
  59.4 54.8 %all-to-all-done = f32[16,256,256]{2,0,1:T(8,128)} async-done(((f32[16,256,256]{2,0,1:T(8,128)}), f32[16,256,256]{2,0,1:T(8,128)}, u32[]{:S(2)}, u32[]{:S(2)}) %all-to-all-start) | async-done | bytes 4194336 | tf_op jit(solution)/shard_map/all_to_all | solution.py:50
  114.2 5.5 copy.46
  119.7 18.9 %fusion.10 = f32[16,256,256]{2,1,0:T(8,128)S(1)} fusion(f32[256,16,256]{2,1,0:T(8,128)S(1)} %bitcast.160, f32[256,256]{1,0:T(8,128)S(1)} %copy-done.2), kind=kOutput, calls=%fused_computation.14 | convolution fusion | flops 3221225472 | bytes 8650752 | tf_op jit(solution)/shard_map/xjk,xi->ijk/dot_general | solution.py:51
  138.7 5.8 fusion.14
  144.5 5.5 copy.48
  150.0 63.4 %all_to_all.148 = f32[256,16,256]{2,1,0:T(8,128)S(1)} all-to-all(f32[256,16,256]{2,1,0:T(8,128)} %copy.48), channel_id=1, replica_groups=mesh['sub'=8,'slab'=16] {'slab'}, dimensions={0} | all-to-all | bytes 8388608 | tf_op jit(solution)/shard_map/all_to_all | solution.py:19
  214.0 7.0 %fusion.31 = f32[16,256,256]{2,1,0:T(8,128)S(1)} fusion(f32[16,256,256]{2,1,0:T(8,128)S(1)} %bitcast.162, f32[256,256]{1,0:T(8,128)S(1)} %copy-done), kind=kOutput, calls=%fused_computation.44 | convolution fusion | flops 3221225472 | bytes 8650752 | tf_op jit(solution)/shard_map/xjk,yj->xyk/dot_general | solution.py:20
  221.0 4.3 fusion.3
  225.3 3.4 collective-permute-start.1
  228.7 1.4 collective-permute-done.1
  231.5 4.2 all-to-all-start.2
  235.9 7.4 %all-to-all-done.2 = f32[16,1,256]{2,1,0:T(1,128)S(1)} async-done(((f32[16,1,256]{2,1,0:T(1,128)}), f32[16,1,256]{2,1,0:T(1,128)S(1)}, u32[]{:S(2)}, u32[]{:S(2)}) %all-to-all-start.2) | async-done | bytes 16416 | tf_op jit(solution)/shard_map/all_to_all | solution.py:59
  246.3 3.5 all-to-all-start.3
  251.0 6.3 %all-to-all-done.3 = f32[16,1,256]{2,1,0:T(1,128)S(1)} async-done(((f32[16,1,256]{2,1,0:T(1,128)}), f32[16,1,256]{2,1,0:T(1,128)S(1)}, u32[]{:S(2)}, u32[]{:S(2)}) %all-to-all-start.3) | async-done | bytes 16416 | tf_op jit(solution)/shard_map/all_to_all | solution.py:62
  257.3 0.7 reduce.9
  258.3 0.9 multiply_reduce_fusion.2
  259.2 62.1 %all-reduce.1 = (f32[]{:T(128)}, f32[]{:T(128)}) all-reduce(f32[]{:T(128)} %get-tuple-element.63, f32[]{:T(128)} %get-tuple-element.62), channel_id=1, replica_groups=mesh['sub'=8,'slab'=16] {'sub','slab'}, use_global_device_ids=true, to_apply=%region_1.2 | all-reduce | flops 2 | bytes 16 | tf_op jit(solution)/shard_map/psum | solution.py:65
  322.7 1.3 fusion.41
  324.0 3.2 collective-permute-done.2
  327.2 1.3 fusion.38
  328.5 7.3 %fusion.8 = f32[16,256,256]{1,2,0:T(8,128)S(1)} fusion(f32[16,256,256]{1,0,2:T(8,128)} %fusion.38, f32[256,256]{1,0:T(8,128)S(1)} %copy-done.3), kind=kOutput, calls=%fused_computation.12 | convolution fusion | flops 3221225472 | bytes 8650752 | tf_op jit(solution)/shard_map/xyz,zk->xyk/dot_general | solution.py:48
  335.8 5.0 convolution_bitcast_fusion
  340.8 5.5 copy.60
  346.2 54.5 %all_to_all.149 = f32[16,256,256]{2,0,1:T(8,128)S(1)} all-to-all(f32[16,256,256]{2,0,1:T(8,128)} %copy.60), channel_id=1, replica_groups=mesh['sub'=8,'slab'=16] {'slab'}, dimensions={1} | all-to-all | bytes 8388608 | tf_op jit(solution)/shard_map/all_to_all | solution.py:50
  400.8 3.3 copy.62
  404.0 8.9 %fusion.6 = f32[16,256,256]{2,1,0:T(8,128)S(1)} fusion(f32[256,16,256]{2,1,0:T(8,128)S(1)} %bitcast.164, f32[256,256]{1,0:T(8,128)S(1)} %copy-done.2), kind=kOutput, calls=%fused_computation.10 | convolution fusion | flops 3221225472 | bytes 8650752 | tf_op jit(solution)/shard_map/xjk,xi->ijk/dot_general | solution.py:51
  412.9 5.8 fusion.15
  418.8 5.5 copy.64
  424.2 53.1 %all_to_all.150 = f32[256,16,256]{2,1,0:T(8,128)S(1)} all-to-all(f32[256,16,256]{2,1,0:T(8,128)} %copy.64), channel_id=1, replica_groups=mesh['sub'=8,'slab'=16] {'slab'}, dimensions={0} | all-to-all | bytes 8388608 | tf_op jit(solution)/shard_map/all_to_all | solution.py:19
  478.0 6.7 %fusion.28 = f32[16,256,256]{2,1,0:T(8,128)S(1)} fusion(f32[16,256,256]{2,1,0:T(8,128)S(1)} %bitcast.166, f32[256,256]{1,0:T(8,128)S(1)} %copy-done), kind=kOutput, calls=%fused_computation.41 | convolution fusion | flops 3221225472 | bytes 8650752 | tf_op jit(solution)/shard_map/xjk,yj->xyk/dot_general | solution.py:20
  484.7 4.3 fusion
  489.0 1.9 copy-done.1
  491.0 1.4 collective-permute-done.3
  493.2 11.9 %all_to_all.151 = f32[16,1,256]{2,1,0:T(1,128)S(1)} all-to-all(f32[16,1,256]{2,1,0:T(1,128)S(1)} %reshape.176), channel_id=1, replica_groups=mesh['sub'=8,'slab'=16] {'slab'}, dimensions={0} | all-to-all | bytes 32768 | tf_op jit(solution)/shard_map/all_to_all | solution.py:59
  507.4 3.5 all-to-all-start.7
  510.9 5.3 copy.74
  516.3 2.2 all-to-all-done.7
  519.7 1.3 multiply_reduce_fusion
  521.0 63.6 %all-reduce = (f32[]{:T(128)}, f32[]{:T(128)}) all-reduce(f32[]{:T(128)} %get-tuple-element.61, f32[]{:T(128)} %get-tuple-element.60), channel_id=1, replica_groups=mesh['sub'=8,'slab'=16] {'sub','slab'}, use_global_device_ids=true, to_apply=%region_5.6 | all-reduce | flops 2 | bytes 16 | tf_op jit(solution)/shard_map/psum | solution.py:65
  (67 shorter events, 11.7 us)
Async XLA Ops:
  0.6 39.0 %copy-start = (f32[256,256]{1,0:T(8,128)S(1)}, f32[256,256]{1,0:T(8,128)}, u32[]{:S(2)}) copy-start(f32[256,256]{1,0:T(8,128)} %param.22) | copy-start | bytes 786436
  0.7 32.3 %collective-permute-start = (f32[16,256]{1,0:T(8,128)S(1)}, f32[16,256]{1,0:T(8,128)S(1)}, u32[]{:S(2)}, u32[]{:S(2)}) collective-permute-start(f32[16,256]{1,0:T(8,128)S(1)} %broadcast_in_dim.15), channel_id=1, source_target_pairs={{112,0},{0,16},{16,32},{32,48},{48,64},{64,80},{80,96},{96,112},{1... | collective-permute-start | bytes 49160 | tf_op jit(solution)/shard_map/ppermute | solution.py:15
  24.7 8.3 %copy-start.3 = (f32[256,256]{1,0:T(8,128)S(1)}, f32[256,256]{1,0:T(8,128)}, u32[]{:S(2)}) copy-start(f32[256,256]{1,0:T(8,128)} %param.23) | copy-start | bytes 786436
  50.1 8.5 %copy-start.7 = (f32[256]{0:T(256)S(1)}, f32[256]{0:T(256)}, u32[]{:S(2)}) copy-start(f32[256]{0:T(256)} %param.25) | copy-start | bytes 3076
  50.1 8.6 %copy-start.5 = (f32[8]{0:T(128)S(1)}, f32[8]{0:T(128)}, u32[]{:S(2)}) copy-start(f32[8]{0:T(128)} %param.20) | copy-start | bytes 100
  50.1 9.2 %copy-start.6 = (f32[256]{0:T(256)S(1)}, f32[256]{0:T(256)}, u32[]{:S(2)}) copy-start(f32[256]{0:T(256)} %param.24) | copy-start | bytes 3076
  50.1 64.1 %all-to-all-start = ((f32[16,256,256]{2,0,1:T(8,128)}), f32[16,256,256]{2,0,1:T(8,128)}, u32[]{:S(2)}, u32[]{:S(2)}) async-start(f32[16,256,256]{2,0,1:T(8,128)} %copy.44), calls=%async_computation | async-start | bytes 8388608 | tf_op jit(solution)/shard_map/all_to_all | solution.py:50
  114.2 5.5 copy-start.2
  119.7 18.9 %copy-start.8 = (f32[256]{0:T(256)S(1)}, f32[256]{0:T(256)}, u32[]{:S(2)}) copy-start(f32[256]{0:T(256)} %param.26) | copy-start | bytes 3076
  221.0 14.7 %copy-start.4 = (f32[256,256]{1,0:T(8,128)S(1)}, f32[256,256]{1,0:T(8,128)}, u32[]{:S(2)}) copy-start(f32[256,256]{1,0:T(8,128)} %param.27) | copy-start | bytes 786436
  225.3 4.8 collective-permute-start.1
  231.5 11.8 %all-to-all-start.2 = ((f32[16,1,256]{2,1,0:T(1,128)}), f32[16,1,256]{2,1,0:T(1,128)S(1)}, u32[]{:S(2)}, u32[]{:S(2)}) async-start(f32[16,1,256]{2,1,0:T(1,128)} %reshape.172), calls=%async_computation.2 | async-start | bytes 32768 | tf_op jit(solution)/shard_map/all_to_all | solution.py:59
  246.3 11.0 %all-to-all-start.3 = ((f32[16,1,256]{2,1,0:T(1,128)}), f32[16,1,256]{2,1,0:T(1,128)S(1)}, u32[]{:S(2)}, u32[]{:S(2)}) async-start(f32[16,1,256]{2,1,0:T(1,128)} %reshape.174), calls=%async_computation.3 | async-start | bytes 32768 | tf_op jit(solution)/shard_map/all_to_all | solution.py:62
  324.0 3.2 collective-permute-start.2
  489.0 1.9 copy-start.1
  491.0 1.5 collective-permute-start.3
  507.4 11.0 %all-to-all-start.7 = ((f32[16,1,256]{2,1,0:T(1,128)}), f32[16,1,256]{2,1,0:T(1,128)S(1)}, u32[]{:S(2)}, u32[]{:S(2)}) async-start(f32[16,1,256]{2,1,0:T(1,128)} %reshape.178), calls=%async_computation.7 | async-start | bytes 32768 | tf_op jit(solution)/shard_map/all_to_all | solution.py:62
where the time goes:
time: 595 us; the launch traced here: 587 us
  blocking collectives  309 us (52%)
  matrix products  88.9 us (15%)
  waiting for transfers between devices  76.7 us (13%)
  local copies, waits for them, and re-layouts  68.4 us (11%)
  starting transfers between devices  23.1 us (4%)
  other arithmetic  15.8 us (3%)
    psum x2, blocking collectives, on_device(): lax.psum((jnp.sum(jump * search), jnp.sum(search * search)), ('sub', 'sla...  126 us
    all_to_all x2, blocking collectives, volume_tail(): lax.all_to_all(spread, 'slab', split_axis=0, concat_axis=1, tiled=True)  117 us
    all_to_all x1, waiting for transfers between devices, on_device(): lax.all_to_all(part, 'slab', split_axis=1, concat_axis=0, tiled=True)  54.8 us
    all_to_all x1, blocking collectives, on_device(): lax.all_to_all(part, 'slab', split_axis=1, concat_axis=0, tiled=True)  54.5 us
    dot_general x2, matrix products, on_device(): modes = jnp.einsum('xjk,xi->ijk', lines, basis_x, precision=HI) / denom  27.8 us
    unnamed x33, local copies, waits for them, and re-layouts  26.4 us
    dot_general x2, matrix products, on_device(): part = jnp.einsum('xyz,zk->xyk', load, basis_z, precision=HI)  13.9 us
    dot_general x2, matrix products, volume_tail(): part = jnp.einsum('xjk,yj->xyk', slabs, basis_y, precision=HI)  13.7 us
  transfers between devices with their start and end apart: 8, of which 7 were waited for; matrix products, arithmetic and copies ran while one was open for 7% of the time, Pallas kernels for 0%

commit v1 on v0

v1 whole, which is shorter than its diff:
```python
import functools

import jax
import jax.numpy as jnp
from jax import lax
from jax.experimental import pallas as pl
from jax.experimental.pallas import tpu as pltpu
from jax.sharding import PartitionSpec as P

HI = lax.Precision.HIGHEST
F32 = jnp.float32
BF16 = jnp.bfloat16
VMEM_LIMIT = 48 * 1024 * 1024
N = 256
ROWS = 16
SLABS = 16
LANES = 128
FIELD = (SLABS, 2, N // SLABS, ROWS, LANES)


def params():
    return pltpu.CompilerParams(vmem_limit_bytes=VMEM_LIMIT)


def split(a):
    high = a.astype(BF16)
    low = (a - high.astype(F32)).astype(BF16)
    return high, low


def dot(a, b):
    return jnp.dot(a, b, preferred_element_type=F32)


def dot3(a, b):
    return dot(a[0], b[0]) + (dot(a[0], b[1]) + dot(a[1], b[0]))


def put_split(scratch, a):
    scratch[0], scratch[1] = split(a)


def whole(shape):
    return pl.BlockSpec(shape, lambda *_: (0,) * len(shape))


def smem():
    return pl.BlockSpec(memory_space=pltpu.SMEM)


def forward_kernel(source, coarse, basis_y, basis_z, out, left, right):
    x = pl.program_id(0)

    @pl.when(x == 0)
    def _():
        put_split(left, basis_y[...].T)
        put_split(right, basis_z[...])

    load = source[0] + coarse[0, 0, 0]
    part = dot3(split(load), right)
    part = dot3(left, split(part))
    for slab in range(SLABS):
        for half in range(2):
            rows = out.at[slab, half].reshape(ROWS * 8, LANES)
            piece = part[slab * ROWS : slab * ROWS + ROWS, LANES * half : LANES * half + LANES]
            rows[pl.ds(x % 8, ROWS, stride=8), :] = piece


def forward(source, coarse, step, basis_y, basis_z):
    return pl.pallas_call(
        forward_kernel,
        grid=(ROWS,),
        in_specs=[
            pl.BlockSpec((1, N, N), lambda x: (x, 0, 0)),
            pl.BlockSpec((1, 1, 1, N, N), lambda x: (step, 0, x, 0, 0)),
            whole((N, N)),
            whole((N, N)),
        ],
        out_specs=pl.BlockSpec((SLABS, 2, ROWS, 8, LANES), lambda x: (0, 0, 0, x // 8, 0)),
        out_shape=jax.ShapeDtypeStruct(FIELD, F32),
        scratch_shapes=[pltpu.VMEM((2, N, N), BF16), pltpu.VMEM((2, N, N), BF16)],
        compiler_params=params(),
        cost_estimate=pl.CostEstimate(
            flops=12 * ROWS * N**3, bytes_accessed=12 * ROWS * N * N, transcendentals=0
        ),
        name="forward",
    )(source, coarse, basis_y, basis_z)


def middle_kernel(base, shift, basis_x, lines, out, left, right):
    j = pl.program_id(0)

    @pl.when(j == 0)
    def _():
        put_split(left, basis_x[...].T)
        put_split(right, basis_x[...])

    field = jnp.concatenate([lines[:, half, 0].reshape(N, LANES) for half in range(2)], axis=1)
    modes = dot3(left, split(field)) / (base[...] + shift[j])
    spread = dot3(right, split(modes))
    for half in range(2):
        piece = spread[:, LANES * half : LANES * half + LANES]
        out[:, half, 0] = piece.reshape(SLABS, ROWS, LANES)


def middle(base, shift, basis_x, lines):
    block = pl.BlockSpec((SLABS, 2, 1, ROWS, LANES), lambda j: (0, 0, j, 0, 0))
    return pl.pallas_call(
        middle_kernel,
        grid=(N // SLABS,),
        in_specs=[whole((N, N)), smem(), whole((N, N)), block],
        out_specs=block,
        out_shape=jax.ShapeDtypeStruct(FIELD, F32),
        scratch_shapes=[pltpu.VMEM((2, N, N), BF16), pltpu.VMEM((2, N, N), BF16)],
        compiler_params=params(),
        cost_estimate=pl.CostEstimate(
            flops=12 * ROWS * N**3, bytes_accessed=8 * ROWS * N * N, transcendentals=0
        ),
        name="middle",
    )(base, shift, basis_x, lines)


def backward_kernel(field, extra, basis_y, basis_z, out, left, right):
    x = pl.program_id(0)

    @pl.when(x == 0)
    def _():
        put_split(left, basis_y[...])
        put_split(right, basis_z[...].T)

    def rows(ref, slab, half):
        return ref.at[slab, half].reshape(ROWS * 8, LANES)[pl.ds(x % 8, ROWS, stride=8), :]

    halves = [
        jnp.concatenate(
            [rows(field, slab, half) + rows(extra, slab, half) for slab in range(SLABS)], axis=0
        )
        for half in range(2)
    ]
    part = dot3(left, split(jnp.concatenate(halves, axis=1)))
    out[0] = dot3(split(part), right)


def backward(field, extra, basis_y, basis_z):
    block = pl.BlockSpec((SLABS, 2, ROWS, 8, LANES), lambda x: (0, 0, 0, x // 8, 0))
    return pl.pallas_call(
        backward_kernel,
        grid=(ROWS,),
        in_specs=[block, block, whole((N, N)), whole((N, N))],
        out_specs=pl.BlockSpec((1, N, N), lambda x: (x, 0, 0)),
        out_shape=jax.ShapeDtypeStruct((ROWS, N, N), F32),
        scratch_shapes=[pltpu.VMEM((2, N, N), BF16), pltpu.VMEM((2, N, N), BF16)],
        compiler_params=params(),
        cost_estimate=pl.CostEstimate(
            flops=12 * ROWS * N**3, bytes_accessed=12 * ROWS * N * N, transcendentals=0
        ),
        name="backward",
    )(field, extra, basis_y, basis_z)


def inverse_parts(denom):
    high = pl.reciprocal(denom, approx=True).astype(BF16)
    wide = high.astype(F32)
    low = (wide * (1.0 - denom * wide)).astype(BF16)
    return high, low


def times_inverse(rows, denom):
    high, low = split(rows)
    count = rows.shape[0]
    w_high, w_low = inverse_parts(denom)
    both = dot(jnp.concatenate([high, low], axis=0), w_high)
    return both[:count] + (both[count:] + dot(high, w_low))


def faces_kernel(base, shift, own_x, ends, products, part0, part1, out):
    block = pl.program_id(0)
    first, last = ends[0:1], ends[1:2]
    for jj in range(8):
        a = jnp.concatenate([part0[0, 0, jj], part0[0, 1, jj]], axis=1)
        b = jnp.concatenate([part1[0, 0, jj], part1[0, 1, jj]], axis=1)
        rows = jnp.concatenate([a * last, b * last, a * first, b * first, products[...]], axis=0)
        result = times_inverse(rows, base[...] + shift[block * 8 + jj])
        for face in range(4):
            piece = result[16 * face : 16 * face + 16] * own_x[...]
            out[0, face, jj : jj + 1] = jnp.sum(piece, axis=0, keepdims=True)
        for pair in range(3):
            out[0, 4 + pair, jj : jj + 1] = result[64 + pair : 65 + pair]


def faces(base, shift, own_x, ends, products, part0, part1):
    block = pl.BlockSpec((1, 2, 8, ROWS, LANES), lambda j: (j // 2, 0, j % 2, 0, 0))
    return pl.pallas_call(
        faces_kernel,
        grid=(N // 8,),
        in_specs=[
            whole((N, N)),
            smem(),
            whole((ROWS, N)),
            whole((2, N)),
            whole((16, N)),
            block,
            block,
        ],
        out_specs=pl.BlockSpec((1, 7, 8, N), lambda j: (j // 2, 0, j % 2, 0)),
        out_shape=jax.ShapeDtypeStruct((SLABS, 7, N // SLABS, N), F32),
        compiler_params=params(),
        cost_estimate=pl.CostEstimate(
            flops=2 * 1000 * N**3, bytes_accessed=8 * ROWS * N * N, transcendentals=N**3
        ),
        name="faces",
    )(base, shift, own_x, ends, products, part0, part1)


def extra_kernel(base, shift, own_x, ends, faces_in, out):
    block = pl.program_id(0)
    first, last = ends[0:1], ends[1:2]
    for jj in range(8):
        upper = own_x[...] * faces_in[0, jj : jj + 1]
        lower = own_x[...] * faces_in[1, jj : jj + 1]
        rows = jnp.concatenate([upper, lower], axis=0)
        result = times_inverse(rows, base[...] + shift[block * 8 + jj])
        result = first * result[16:] - last * result[:16]
        for half in range(2):
            out[0, half, jj] = result[:, LANES * half : LANES * half + LANES]


def extra(base, shift, own_x, ends, faces_in):
    return pl.pallas_call(
        extra_kernel,
        grid=(N // 8,),
        in_specs=[
            whole((N, N)),
            smem(),
            whole((ROWS, N)),
            whole((2, N)),
            pl.BlockSpec((2, 8, N), lambda j: (0, j, 0)),
        ],
        out_specs=pl.BlockSpec((1, 2, 8, ROWS, LANES), lambda j: (j // 2, 0, j % 2, 0, 0)),
        out_shape=jax.ShapeDtypeStruct(FIELD, F32),
        compiler_params=params(),
        cost_estimate=pl.CostEstimate(
            flops=2 * 1000 * N**3, bytes_accessed=4 * ROWS * N * N, transcendentals=N**3
        ),
        name="extra",
    )(base, shift, own_x, ends, faces_in)


def exact(a, b):
    return jnp.dot(a, b, precision=HI, preferred_element_type=F32)


def exact_t(a, b):
    dims = (((1,), (1,)), ((), ()))
    return lax.dot_general(a, b, dims, precision=HI, preferred_element_type=F32)


def precondition(jump, gram_x, gram_y, stiff):
    seen = exact(exact(gram_y, jump), gram_x)
    search = stiff * seen
    image = exact(exact(gram_y, search), gram_x)
    return search, image, jnp.sum(seen * search), jnp.sum(image * search)


def scalars_block(upper, lower):
    at = lax.broadcasted_iota(jnp.int32, (8, 128), 0)
    return jnp.where(at == 0, upper, jnp.where(at == 1, lower, 0.0))


def chain0_kernel(jump, gram_x, gram_y, stiff, search, image, sums):
    search[...], image[...], upper, lower = precondition(
        jump[...], gram_x[...], gram_y[...], stiff[...]
    )
    sums[...] = scalars_block(upper, lower)


def chain0(jump, gram_x, gram_y, stiff):
    face = jax.ShapeDtypeStruct((N, N), F32)
    return pl.pallas_call(
        chain0_kernel,
        out_shape=(face, face, jax.ShapeDtypeStruct((8, 128), F32)),
        compiler_params=params(),
        cost_estimate=pl.CostEstimate(
            flops=48 * N**3, bytes_accessed=24 * N * N, transcendentals=0
        ),
        name="chain0",
    )(jump, gram_x, gram_y, stiff)


def chain1_kernel(
    scale, jump, image, before, after, table, gram_x, gram_y, stiff, own_x, basis_y, search, sums, out
):
    alpha, ratio = scale[0], scale[1]
    t = image[...]
    own = table[1] * before[...] - table[0] * t
    other = table[2] * t - table[1] * after[...]
    q = jump[...] + alpha * (own - ratio * other)
    search[...], _, upper, lower = precondition(q, gram_x[...], gram_y[...], stiff[...])
    sums[...] = scalars_block(upper, lower)
    out[...] = exact_t(exact_t(own_x[...], q), basis_y[...])


def chain1(*args):
    return pl.pallas_call(
        chain1_kernel,
        in_specs=[smem()] + [pl.BlockSpec(memory_space=pltpu.VMEM)] * 10,
        out_shape=(
            jax.ShapeDtypeStruct((N, N), F32),
            jax.ShapeDtypeStruct((8, 128), F32),
            jax.ShapeDtypeStruct((ROWS, N), F32),
        ),
        compiler_params=params(),
        cost_estimate=pl.CostEstimate(
            flops=50 * N**3, bytes_accessed=48 * N * N, transcendentals=0
        ),
        name="chain1",
    )(*args)


def final_kernel(scale, search0, search1, own_x, basis_y, out):
    total = scale[0] * search0[...] + scale[1] * search1[...]
    out[...] = exact_t(exact_t(own_x[...], total), basis_y[...])


def final(*args):
    return pl.pallas_call(
        final_kernel,
        in_specs=[smem()] + [pl.BlockSpec(memory_space=pltpu.VMEM)] * 4,
        out_shape=jax.ShapeDtypeStruct((ROWS, N), F32),
        compiler_params=params(),
        name="final",
    )(*args)


def gram_kernel(basis_x, basis_y, gram_x, gram_y):
    gram_x[...] = exact(basis_x[...].T, basis_x[...])
    gram_y[...] = exact(basis_y[...].T, basis_y[...])


def grams(basis_x, basis_y):
    face = jax.ShapeDtypeStruct((N, N), F32)
    return pl.pallas_call(
        gram_kernel, out_shape=(face, face), compiler_params=params(), name="grams"
    )(basis_x, basis_y)


def from_behind(block, axis, distance):
    count = lax.axis_size(axis)
    route = [((i - distance) % count, i) for i in range(count)]
    return lax.ppermute(block, axis, route)


def sum_over_subs(sums):
    for bit in (1, 2, 4):
        sums = sums + lax.ppermute(sums, "sub", [(i, i ^ bit) for i in range(8)])
    return sums


def step_length(sums):
    return sums[0, 0] / (sums[1, 0] + 1e-06)


def exchange(block):
    return lax.all_to_all(block, "slab", split_axis=0, concat_axis=0, tiled=True)


def on_device(
    source, coarse, rho, basis_x, basis_y, basis_z, eigen_x, eigen_y, eigen_z, face_stiff
):
    source = source[0]
    sub_index = lax.axis_index("sub")
    slab_index = lax.axis_index("slab")
    subs = lax.axis_size("sub")
    own_rho = lax.dynamic_slice_in_dim(rho, sub_index, 1, 0)[0]
    next_rho = lax.dynamic_slice_in_dim(rho, (sub_index + 1) % subs, 1, 0)[0]
    weight = 0.5 * (own_rho + next_rho)
    start = slab_index * ROWS
    own_x = lax.dynamic_slice_in_dim(basis_x, start, ROWS, 0)

    part1 = forward(source, coarse, 1, basis_y, basis_z)
    lines = exchange(part1)

    base_xz = own_rho * (eigen_x[:, None] + eigen_z[None, :])
    base_zx = own_rho * (eigen_z[:, None] + eigen_x[None, :])
    shift = own_rho * eigen_y
    own_shift = lax.dynamic_slice_in_dim(shift, start, ROWS, 0)
    ends = jnp.stack([basis_z[0], basis_z[N - 1]])
    products = jnp.stack([ends[1] * ends[1], ends[1] * ends[0], ends[0] * ends[0]])
    products = jnp.pad(products, ((0, 13), (0, 0)))
    stiff = weight * face_stiff.T
    gram_x, gram_y = grams(basis_x, basis_y)

    part0 = forward(source, coarse, 0, basis_y, basis_z)
    pieces = faces(base_zx, shift, own_x, ends, products, part0, part1)
    table = pieces[:, 4:].transpose(1, 0, 2, 3).reshape(3, N, N)
    following = from_behind(pieces[:, 2:4], "sub", -1)
    shares = exchange(pieces[:, 0:2] - following)
    jumps = jnp.sum(shares, axis=0)
    jumps = exchange(jnp.broadcast_to(jumps[None], (SLABS,) + jumps.shape))
    jumps = jumps.transpose(1, 0, 2, 3).reshape(2, N, N)

    search0, image0, sums0 = chain0(jumps[0], gram_x, gram_y, stiff)
    before = from_behind(image0, "sub", 1)
    after = from_behind(image0, "sub", -1)
    alpha0 = step_length(sum_over_subs(sums0))

    spread = exchange(middle(base_xz, own_shift, basis_x, lines))

    more = extra(base_xz, shift, own_x, ends, alpha0 * jnp.stack([image0, before]))
    scale = jnp.stack([alpha0, own_rho / next_rho])
    search1, sums1, jump = chain1(
        scale, jumps[1], image0, before, after, table, gram_x, gram_y, stiff, own_x, basis_y
    )
    alpha1 = step_length(sum_over_subs(sums1))
    multipliers = final(jnp.stack([alpha0, alpha1]), search0, search1, own_x, basis_y)
    solution = backward(spread, more, basis_y, basis_z)
    return (solution[None], multipliers[None], jump[None])


def solution(mesh):
    in_specs = (
        P("sub", "slab", None, None),
        P(None, "sub", "slab", None, None),
        P(),
        P(),
        P(),
        P(),
        P(),
        P(),
        P(),
        P(),
    )
    out_specs = (P("sub", "slab", None, None), P("sub", "slab", None), P("sub", "slab", None))
    return jax.shard_map(
        on_device, mesh=mesh, in_specs=in_specs, out_specs=out_specs, check_vma=False
    )
```

time: 595 us -> 283 us (0.48)
  blocking collectives: 309 us -> 35.6 us
  Pallas kernels: 0 us -> 127 us
  matrix products: 88.9 us -> 0 us
  local copies, waits for them, and re-layouts: 68.4 us -> 21 us
  waiting for transfers between devices: 76.7 us -> 63.8 us
  other arithmetic: 15.8 us -> 5.46 us
    all_to_all x4 -> x2, blocking collectives: 183 us -> 35.6 us  [exchange(): lax.all_to_all(block, 'slab', split_axis=0, concat_axis=0, tiled=True)]
    pallas_call x0 -> x10, Pallas kernels: none -> 127 us  [the longest x1 31.3 us: faces(): pl.pallas_call(faces_kernel, grid=(N // 8,), in_specs=[whole((N, N)), sme...]
    psum x2 -> x0, blocking collectives: 126 us -> none  [on_device(): lax.psum((jnp.sum(jump * search), jnp.sum(search * search)), ('sub', 'sla...]
    dot_general x18 -> x0, matrix products: 87.7 us -> none  [the longest x2 27.8 us: on_device(): modes = jnp.einsum('xjk,xi->ijk', lines, basis_x, precision=HI) / denom]
    all_to_all x4 -> x2, waiting for transfers between devices: 70.7 us -> 50.9 us  [exchange(): lax.all_to_all(block, 'slab', split_axis=0, concat_axis=0, tiled=True)]
    all_to_all x17 -> x0, local copies, waits for them, and re-layouts: 11.5 us -> none  [the longest x2 8.74 us: on_device(): lax.all_to_all(part, 'slab', split_axis=1, concat_axis=0, tiled=True)]
    dot_general x2 -> x0, local copies, waits for them, and re-layouts: 11 us -> none  [on_device(): spread = jnp.einsum('ijk,xi->xjk', modes, basis_x, precision=HI)]
    unnamed x33 -> x41, local copies, waits for them, and re-layouts: 26.4 us -> 16.2 us
  transfers between devices with their start and end apart: 8 -> 11, of which waited for: 7 -> 7; matrix products, arithmetic and copies ran while one was open for 7% -> 3% of each run, Pallas kernels for 0% -> 17%
where the time goes in v1:
time: 283 us; the launch traced here: 280 us
  Pallas kernels  127 us (45%)
  waiting for transfers between devices  63.8 us (23%)
  blocking collectives  35.6 us (13%)
  starting transfers between devices  21.6 us (8%)
  local copies, waits for them, and re-layouts  21 us (7%)
  between operations  6.14 us (2%)
  other arithmetic  5.46 us (2%)
    all_to_all x2, waiting for transfers between devices, exchange(): lax.all_to_all(block, 'slab', split_axis=0, concat_axis=0, tiled=True)  50.9 us
    all_to_all x2, blocking collectives, exchange(): lax.all_to_all(block, 'slab', split_axis=0, concat_axis=0, tiled=True)  35.6 us
    pallas_call x1, Pallas kernels, faces(): pl.pallas_call(faces_kernel, grid=(N // 8,), in_specs=[whole((N, N)), sme...  31.3 us
    pallas_call x2, Pallas kernels, forward(): pl.pallas_call(forward_kernel, grid=(ROWS,), in_specs=[pl.BlockSpec((1, N...  30.5 us
    pallas_call x1, Pallas kernels, extra(): pl.pallas_call(extra_kernel, grid=(N // 8,), in_specs=[whole((N, N)), sme...  24.9 us
    all_to_all x2, starting transfers between devices, exchange(): lax.all_to_all(block, 'slab', split_axis=0, concat_axis=0, tiled=True)  17.7 us
    pallas_call x1, Pallas kernels, backward(): pl.pallas_call(backward_kernel, grid=(ROWS,), in_specs=[block, block, who...  16.7 us
    unnamed x41, local copies, waits for them, and re-layouts  16.2 us
  transfers between devices with their start and end apart: 11, of which 7 were waited for; matrix products, arithmetic and copies ran while one was open for 3% of the time, Pallas kernels for 17%

profile of v1, /device:TPU:6, one launch (start us, length us, event | category | flops | bytes accessed | tf_op | source)
XLA Modules:
  0.0 280.4 jit_solution(13280780880756695227)
XLA Ops:
  0.6 0.7 slice_multiply_fusion.1
  1.4 0.9 copy-done.1
  2.3 0.9 copy-done.6
  3.3 15.2 %forward.2.part1 = f32[16,2,16,16,128]{4,3,2,1,0:T(8,128)S(1)} custom-call(f32[16,256,256]{2,1,0:T(8,128)} %bitcast.24, f32[2,1,16,256,256]{4,3,2,1,0:T(8,128)} %coarse.3, f32[256,256]{1,0:T(8,128)S(1)} %copy-done.1, f32[256,256]{1,0:T(8,128)S(1)} %copy-done.6), custom_call_target="tpu_custom_call" | custom-call | flops 3221225472 | bytes 12582912 | tf_op jit(solution)/shard_map/forward/pallas_call | solution.py:70
  18.5 2.0 copy-done
  20.5 15.3 %forward.3.part0 = f32[16,2,16,16,128]{4,3,2,1,0:T(8,128)S(1)} custom-call(f32[16,256,256]{2,1,0:T(8,128)} %bitcast.25, f32[2,1,16,256,256]{4,3,2,1,0:T(8,128)} %coarse.3, f32[256,256]{1,0:T(8,128)S(1)} %copy-done.1, f32[256,256]{1,0:T(8,128)S(1)} %copy-done.6), custom_call_target="tpu_custom_call" | custom-call | flops 3221225472 | bytes 12582912 | tf_op jit(solution)/shard_map/forward/pallas_call | solution.py:70
  35.8 2.0 copy-done.5
  37.8 0.6 fusion.3
  38.4 0.6 broadcast_multiply_fusion.shift
  39.1 0.8 add_multiply_fusion
  39.9 31.3 %faces.1 = f32[16,7,16,256]{3,2,1,0:T(8,128)S(1)} custom-call(f32[256,256]{1,0:T(8,128)S(1)} %get-tuple-element.30.base, f32[256]{0:T(256)S(1)} %broadcast_multiply_fusion.shift, f32[16,256]{1,0:T(8,128)S(1)} %constant_dynamic-slice_fusion.own_x, f32[2,256]{1,0:T(2,128)S(1)} %pad_maximum_fusion.ends, f32[16,256]{1,0:T(8,128)S(1)} %select_maximum_fusion.products, ...), custom_call_target="tpu_custom_call" | custom-call | flops 33554432000 | bytes 8388608 | tf_op jit(solution)/shard_map/faces/pallas_call | solution.py:193
  71.5 6.7 %collective-permute-done = f32[16,2,16,256]{3,2,1,0:T(8,128)S(1)} collective-permute-done((f32[16,2,16,256]{3,2,1,0:T(8,128)S(1)}, f32[16,2,16,256]{3,2,1,0:T(8,128)S(1)}, u32[]{:S(2)}, u32[]{:S(2)}) %collective-permute-start) | collective-permute-done | bytes 524320 | tf_op jit(solution)/shard_map/ppermute | solution.py:350
  78.3 19.4 %all_to_all.20 = f32[16,2,16,256]{3,2,1,0:T(8,128)} all-to-all(f32[16,2,16,256]{3,2,1,0:T(8,128)S(1)} %slice_subtract_fusion), channel_id=1, replica_groups=mesh['sub'=8,'slab'=16] {'slab'}, dimensions={0} | all-to-all | bytes 1048576 | tf_op jit(solution)/shard_map/all_to_all | solution.py:364
  97.7 1.1 reduce_sum.9
  98.8 16.2 %all_to_all.21 = f32[16,2,16,256]{3,2,1,0:T(8,128)S(1)} all-to-all(f32[16,2,16,256]{3,2,1,0:T(8,128)S(1)} %broadcast_in_dim.8), channel_id=1, replica_groups=mesh['sub'=8,'slab'=16] {'slab'}, dimensions={0} | all-to-all | bytes 1048576 | tf_op jit(solution)/shard_map/all_to_all | solution.py:364
  115.1 4.7 %all-to-all-start = ((f32[16,2,16,16,128]{4,3,2,1,0:T(8,128)}), f32[16,2,16,16,128]{4,3,2,1,0:T(8,128)}, u32[]{:S(2)}, u32[]{:S(2)}) async-start(f32[16,2,16,16,128]{4,3,2,1,0:T(8,128)} %copy-done), calls=%async_computation | async-start | bytes 8388608 | tf_op jit(solution)/shard_map/all_to_all | solution.py:364
  119.8 0.7 grams.1
  120.5 0.7 copy-done.10
  122.5 1.8 copy.15
  124.3 1.0 multiply_bitcast_fusion.stiff
  125.3 0.7 fusion
  126.0 0.9 copy-done.11
  127.0 0.9 copy-done.14
  127.9 2.1 chain0.1
  130.2 1.2 collective-permute-done.1
  131.3 0.6 collective-permute-start.2
  132.0 1.7 collective-permute-start.5
  133.7 1.2 collective-permute-done.2
  134.9 1.2 collective-permute-start.3
  136.1 43.6 %all-to-all-done.lines = f32[16,2,16,16,128]{4,3,2,1,0:T(8,128)} async-done(((f32[16,2,16,16,128]{4,3,2,1,0:T(8,128)}), f32[16,2,16,16,128]{4,3,2,1,0:T(8,128)}, u32[]{:S(2)}, u32[]{:S(2)}) %all-to-all-start) | async-done | bytes 4194336 | tf_op jit(solution)/shard_map/all_to_all | solution.py:364
  179.7 14.4 %middle.1 = f32[16,2,16,16,128]{4,3,2,1,0:T(8,128)S(1)} custom-call(f32[256,256]{1,0:T(8,128)S(1)} %get-tuple-element.31.base, f32[16]{0:T(128)S(1)} %dynamic_slice.13.shift, f32[256,256]{1,0:T(8,128)S(1)} %copy-done.8, f32[16,2,16,16,128]{4,3,2,1,0:T(8,128)} %all-to-all-done.lines), custom_call_target="tpu_custom_call" | custom-call | flops 3221225472 | bytes 8388608 | tf_op jit(solution)/shard_map/middle/pallas_call | solution.py:108
  194.2 2.0 copy-done.4
  196.2 13.0 %all-to-all-start.1 = ((f32[16,2,16,16,128]{4,3,2,1,0:T(8,128)}), f32[16,2,16,16,128]{4,3,2,1,0:T(8,128)}, u32[]{:S(2)}, u32[]{:S(2)}) async-start(f32[16,2,16,16,128]{4,3,2,1,0:T(8,128)} %copy-done.4), calls=%async_computation.1 | async-start | bytes 8388608 | tf_op jit(solution)/shard_map/all_to_all | solution.py:364
  209.2 1.0 slice_bitcast_fusion
  211.5 1.2 copy.16
  212.7 0.5 fusion.2
  214.6 0.9 copy-done.12
  215.5 0.9 copy-done.15
  216.5 4.1 %chain1.1 = (f32[256,256]{1,0:T(8,128)S(1)}, f32[8,128]{1,0:T(8,128)S(1)}, f32[16,256]{1,0:T(8,128)}) custom-call(f32[2]{0:T(128)S(1)} %pad_maximum_fusion.1.scale, f32[256,256]{1,0:T(8,128)S(1)} %bitcast.22, f32[256,256]{1,0:T(8,128)S(1)} %get-tuple-element.14.image, f32[256,256]{1,0:T(8,128)} %collective-permute-done.4.before, ...), custom_call_target="tpu_custom_call" | custom-call | flops 838860800 | bytes 3145728 | tf_op jit(solution)/shard_map/chain1/pallas_call | solution.py:304
  220.6 1.2 collective-permute-done.6
  221.8 1.0 maximum_multiply_fusion.faces_in
  222.7 2.6 collective-permute-done.7
  225.4 24.9 %extra.1 = f32[16,2,16,16,128]{4,3,2,1,0:T(8,128)S(1)} custom-call(f32[256,256]{1,0:T(8,128)S(1)} %get-tuple-element.31.base, f32[256]{0:T(256)S(1)} %broadcast_multiply_fusion.shift, f32[16,256]{1,0:T(8,128)S(1)} %constant_dynamic-slice_fusion.own_x, f32[2,256]{1,0:T(2,128)S(1)} %pad_maximum_fusion.ends, f32[2,256,256]{2,1,0:T(8,128)S(1)} %maximum_multiply_fusion.faces_in), custom_call_target="tpu_custom_call" | custom-call | flops 33554432000 | bytes 4194304 | tf_op jit(solution)/shard_map/extra/pallas_call | solution.py:229
  250.2 2.0 copy-done.3
  252.3 0.6 fusion.1
  254.2 2.1 final.1
  256.3 7.3 %all-to-all-done.1.field = f32[16,2,16,16,128]{4,3,2,1,0:T(8,128)} async-done(((f32[16,2,16,16,128]{4,3,2,1,0:T(8,128)}), f32[16,2,16,16,128]{4,3,2,1,0:T(8,128)}, u32[]{:S(2)}, u32[]{:S(2)}) %all-to-all-start.1) | async-done | bytes 4194336 | tf_op jit(solution)/shard_map/all_to_all | solution.py:364
  263.7 16.7 %backward.1 = f32[16,256,256]{2,1,0:T(8,128)} custom-call(f32[16,2,16,16,128]{4,3,2,1,0:T(8,128)} %all-to-all-done.1.field, f32[16,2,16,16,128]{4,3,2,1,0:T(8,128)} %copy-done.3, f32[256,256]{1,0:T(8,128)S(1)} %copy-done.2, f32[256,256]{1,0:T(8,128)S(1)} %copy-done.7), custom_call_target="tpu_custom_call" | custom-call | flops 3221225472 | bytes 12582912 | tf_op jit(solution)/shard_map/backward/pallas_call | solution.py:146
  (54 shorter events, 0.9 us)
Async XLA Ops:
  1.4 0.9 copy-start.1
  2.3 0.9 copy-start.6
  18.5 2.0 copy-start
  20.5 17.3 %copy-start.18 = (f32[8]{0:T(128)S(1)}, f32[8]{0:T(128)}, u32[]{:S(2)}) copy-start(f32[8]{0:T(128)} %param.12) | copy-start | bytes 100
  20.5 17.9 %copy-start.19 = (f32[256]{0:T(256)S(1)}, f32[256]{0:T(256)}, u32[]{:S(2)}) copy-start(f32[256]{0:T(256)} %param.17) | copy-start | bytes 3076
  20.5 18.6 %copy-start.16 = (f32[256]{0:T(256)S(1)}, f32[256]{0:T(256)}, u32[]{:S(2)}) copy-start(f32[256]{0:T(256)} %param.16) | copy-start | bytes 3076
  20.5 18.6 %copy-start.17 = (f32[256]{0:T(256)S(1)}, f32[256]{0:T(256)}, u32[]{:S(2)}) copy-start(f32[256]{0:T(256)} %param.18) | copy-start | bytes 3076
  20.5 19.4 %copy-start.8 = (f32[256,256]{1,0:T(8,128)S(1)}, f32[256,256]{1,0:T(8,128)}, u32[]{:S(2)}) copy-start(f32[256,256]{1,0:T(8,128)} %basis_x.3) | copy-start | bytes 786436
  35.8 2.0 copy-start.5
  71.2 7.0 %collective-permute-start = (f32[16,2,16,256]{3,2,1,0:T(8,128)S(1)}, f32[16,2,16,256]{3,2,1,0:T(8,128)S(1)}, u32[]{:S(2)}, u32[]{:S(2)}) collective-permute-start(f32[16,2,16,256]{3,2,1,0:T(8,128)S(1)} %slice.47), channel_id=1, source_target_pairs={{16,0},{32,16},{48,32},{64,48},{80,64},{96,80},{112,96},{0,112},{1... | collective-permute-start | bytes 1572872 | tf_op jit(solution)/shard_map/ppermute | solution.py:350
  115.1 4.7 %copy-start.2 = (f32[256,256]{1,0:T(8,128)S(1)}, f32[256,256]{1,0:T(8,128)}, u32[]{:S(2)}) copy-start(f32[256,256]{1,0:T(8,128)} %basis_y.11) | copy-start | bytes 786436
  115.1 64.7 %all-to-all-start = ((f32[16,2,16,16,128]{4,3,2,1,0:T(8,128)}), f32[16,2,16,16,128]{4,3,2,1,0:T(8,128)}, u32[]{:S(2)}, u32[]{:S(2)}) async-start(f32[16,2,16,16,128]{4,3,2,1,0:T(8,128)} %copy-done), calls=%async_computation | async-start | bytes 8388608 | tf_op jit(solution)/shard_map/all_to_all | solution.py:364
  120.5 0.7 copy-start.10
  121.2 3.1 %copy-start.13 = (f32[256,256]{1,0:T(8,128)}, f32[256,256]{1,0:T(8,128)S(1)}, u32[]{:S(2)}) copy-start(f32[256,256]{1,0:T(8,128)S(1)} %get-tuple-element.12.gram_y) | copy-start | bytes 786436
  126.0 0.9 copy-start.11
  127.0 0.9 copy-start.14
  130.1 1.2 collective-permute-start.1
  131.3 3.6 %collective-permute-start.2 = (f32[8,128]{1,0:T(8,128)S(1)}, f32[8,128]{1,0:T(8,128)S(1)}, u32[]{:S(2)}, u32[]{:S(2)}) collective-permute-start(f32[8,128]{1,0:T(8,128)S(1)} %add.86), channel_id=1, source_target_pairs={{0,32},{16,48},{32,0},{48,16},{64,96},{80,112},{96,64},{112,80},{1... | collective-permute-start | bytes 12296 | tf_op jit(solution)/shard_map/ppermute | solution.py:355
  132.0 82.6 %collective-permute-start.4 = (f32[256,256]{1,0:T(8,128)S(1)}, f32[256,256]{1,0:T(8,128)}, u32[]{:S(2)}, u32[]{:S(2)}) collective-permute-start(f32[256,256]{1,0:T(8,128)S(1)} %get-tuple-element.14.image), channel_id=1, source_target_pairs={{112,0},{0,16},{16,32},{32,48},{48,64},{64,80},{80,96},{96,112},{1... | collective-permute-start | bytes 786440 | tf_op jit(solution)/shard_map/ppermute | solution.py:350
  132.0 82.6 %collective-permute-start.5 = (f32[256,256]{1,0:T(8,128)S(1)}, f32[256,256]{1,0:T(8,128)}, u32[]{:S(2)}, u32[]{:S(2)}) collective-permute-start(f32[256,256]{1,0:T(8,128)S(1)} %get-tuple-element.14.image), channel_id=1, source_target_pairs={{16,0},{32,16},{48,32},{64,48},{80,64},{96,80},{112,96},{0,112},{1... | collective-permute-start | bytes 786440 | tf_op jit(solution)/shard_map/ppermute | solution.py:350
  134.9 77.7 %collective-permute-start.3 = (f32[8,128]{1,0:T(8,128)S(1)}, f32[8,128]{1,0:T(8,128)S(1)}, u32[]{:S(2)}, u32[]{:S(2)}) collective-permute-start(f32[8,128]{1,0:T(8,128)S(1)} %add.87), channel_id=1, source_target_pairs={{0,64},{16,80},{32,96},{48,112},{64,0},{80,16},{96,32},{112,48},{1... | collective-permute-start | bytes 12296 | tf_op jit(solution)/shard_map/ppermute | solution.py:355
  194.1 2.0 copy-start.4
  196.2 18.4 %copy-start.9 = (f32[1,16,16,256]{3,2,0,1:T(8,128)S(1)}, f32[1,16,16,256]{3,2,0,1:T(8,128)}, u32[]{:S(2)}) copy-start(f32[1,16,16,256]{3,2,0,1:T(8,128)} %get-tuple-element.19) | copy-start | bytes 786436
  196.2 67.5 %all-to-all-start.1 = ((f32[16,2,16,16,128]{4,3,2,1,0:T(8,128)}), f32[16,2,16,16,128]{4,3,2,1,0:T(8,128)}, u32[]{:S(2)}, u32[]{:S(2)}) async-start(f32[16,2,16,16,128]{4,3,2,1,0:T(8,128)} %copy-done.4), calls=%async_computation.1 | async-start | bytes 8388608 | tf_op jit(solution)/shard_map/all_to_all | solution.py:364
  214.6 1.0 copy-start.12
  215.5 0.9 copy-start.15
  220.6 1.2 collective-permute-start.6
  221.8 3.6 %collective-permute-start.7 = (f32[8,128]{1,0:T(8,128)S(1)}, f32[8,128]{1,0:T(8,128)S(1)}, u32[]{:S(2)}, u32[]{:S(2)}) collective-permute-start(f32[8,128]{1,0:T(8,128)S(1)} %add.90), channel_id=1, source_target_pairs={{0,32},{16,48},{32,0},{48,16},{64,96},{80,112},{96,64},{112,80},{1... | collective-permute-start | bytes 12296 | tf_op jit(solution)/shard_map/ppermute | solution.py:355
  225.4 38.3 %copy-start.7 = (f32[256,256]{1,0:T(8,128)S(1)}, f32[256,256]{1,0:T(8,128)}, u32[]{:S(2)}) copy-start(f32[256,256]{1,0:T(8,128)} %basis_z.5) | copy-start | bytes 786436
  225.4 26.9 %collective-permute-start.8 = (f32[8,128]{1,0:T(8,128)S(1)}, f32[8,128]{1,0:T(8,128)S(1)}, u32[]{:S(2)}, u32[]{:S(2)}) collective-permute-start(f32[8,128]{1,0:T(8,128)S(1)} %add.91), channel_id=1, source_target_pairs={{0,64},{16,80},{32,96},{48,112},{64,0},{80,16},{96,32},{112,48},{1... | collective-permute-start | bytes 12296 | tf_op jit(solution)/shard_map/ppermute | solution.py:355
  250.2 2.0 copy-start.3

commit v2 on v1

--- a/solution.py
+++ b/solution.py
@@ -15,6 +15,7 @@
 ROWS = 16
 SLABS = 16
 LANES = 128
+GROUP = 4
 FIELD = (SLABS, 2, N // SLABS, ROWS, LANES)
 
 
@@ -49,34 +50,38 @@
 
 
 def forward_kernel(source, coarse, basis_y, basis_z, out, left, right):
-    x = pl.program_id(0)
-
-    @pl.when(x == 0)
+    step = pl.program_id(0)
+
+    @pl.when(step == 0)
     def _():
         put_split(left, basis_y[...].T)
         put_split(right, basis_z[...])
 
-    load = source[0] + coarse[0, 0, 0]
-    part = dot3(split(load), right)
-    part = dot3(left, split(part))
-    for slab in range(SLABS):
-        for half in range(2):
-            rows = out.at[slab, half].reshape(ROWS * 8, LANES)
-            piece = part[slab * ROWS : slab * ROWS + ROWS, LANES * half : LANES * half + LANES]
-            rows[pl.ds(x % 8, ROWS, stride=8), :] = piece
+    load = (source[...] + coarse[0, 0]).reshape(GROUP * N, N)
+    first = dot3(split(load), right)
+    for x in range(GROUP):
+        part = dot3(left, split(first[x * N : x * N + N]))
+        at = pl.ds((step * GROUP + x) % 8, ROWS, stride=8)
+        for slab in range(SLABS):
+            for half in range(2):
+                rows = out.at[slab, half].reshape(ROWS * 8, LANES)
+                piece = part[slab * ROWS : slab * ROWS + ROWS, LANES * half : LANES * half + LANES]
+                rows[at, :] = piece
 
 
 def forward(source, coarse, step, basis_y, basis_z):
     return pl.pallas_call(
         forward_kernel,
-        grid=(ROWS,),
+        grid=(ROWS // GROUP,),
         in_specs=[
-            pl.BlockSpec((1, N, N), lambda x: (x, 0, 0)),
-            pl.BlockSpec((1, 1, 1, N, N), lambda x: (step, 0, x, 0, 0)),
+            pl.BlockSpec((GROUP, N, N), lambda x: (x, 0, 0)),
+            pl.BlockSpec((1, 1, GROUP, N, N), lambda x: (step, 0, x, 0, 0)),
             whole((N, N)),
             whole((N, N)),
         ],
-        out_specs=pl.BlockSpec((SLABS, 2, ROWS, 8, LANES), lambda x: (0, 0, 0, x // 8, 0)),
+        out_specs=pl.BlockSpec(
+            (SLABS, 2, ROWS, 8, LANES), lambda x: (0, 0, 0, x * GROUP // 8, 0)
+        ),
         out_shape=jax.ShapeDtypeStruct(FIELD, F32),
         scratch_shapes=[pltpu.VMEM((2, N, N), BF16), pltpu.VMEM((2, N, N), BF16)],
         compiler_params=params(),
@@ -88,26 +93,28 @@
 
 
 def middle_kernel(base, shift, basis_x, lines, out, left, right):
-    j = pl.program_id(0)
-
-    @pl.when(j == 0)
+    step = pl.program_id(0)
+
+    @pl.when(step == 0)
     def _():
         put_split(left, basis_x[...].T)
         put_split(right, basis_x[...])
 
-    field = jnp.concatenate([lines[:, half, 0].reshape(N, LANES) for half in range(2)], axis=1)
-    modes = dot3(left, split(field)) / (base[...] + shift[j])
-    spread = dot3(right, split(modes))
-    for half in range(2):
-        piece = spread[:, LANES * half : LANES * half + LANES]
-        out[:, half, 0] = piece.reshape(SLABS, ROWS, LANES)
+    for j in range(GROUP):
+        halves = [lines[:, half, j].reshape(N, LANES) for half in range(2)]
+        field = jnp.concatenate(halves, axis=1)
+        modes = dot3(left, split(field)) / (base[...] + shift[step * GROUP + j])
+        spread = dot3(right, split(modes))
+        for half in range(2):
+            piece = spread[:, LANES * half : LANES * half + LANES]
+            out[:, half, j] = piece.reshape(SLABS, ROWS, LANES)
 
 
 def middle(base, shift, basis_x, lines):
-    block = pl.BlockSpec((SLABS, 2, 1, ROWS, LANES), lambda j: (0, 0, j, 0, 0))
+    block = pl.BlockSpec((SLABS, 2, GROUP, ROWS, LANES), lambda j: (0, 0, j, 0, 0))
     return pl.pallas_call(
         middle_kernel,
-        grid=(N // SLABS,),
+        grid=(N // SLABS // GROUP,),
         in_specs=[whole((N, N)), smem(), whole((N, N)), block],
         out_specs=block,
         out_shape=jax.ShapeDtypeStruct(FIELD, F32),
@@ -121,33 +128,36 @@
 
 
 def backward_kernel(field, extra, basis_y, basis_z, out, left, right):
-    x = pl.program_id(0)
-
-    @pl.when(x == 0)
+    step = pl.program_id(0)
+
+    @pl.when(step == 0)
     def _():
         put_split(left, basis_y[...])
         put_split(right, basis_z[...].T)
 
-    def rows(ref, slab, half):
-        return ref.at[slab, half].reshape(ROWS * 8, LANES)[pl.ds(x % 8, ROWS, stride=8), :]
-
-    halves = [
-        jnp.concatenate(
-            [rows(field, slab, half) + rows(extra, slab, half) for slab in range(SLABS)], axis=0
-        )
-        for half in range(2)
-    ]
-    part = dot3(left, split(jnp.concatenate(halves, axis=1)))
-    out[0] = dot3(split(part), right)
+    def total(x, slab, half):
+        at = pl.ds((step * GROUP + x) % 8, ROWS, stride=8)
+        terms = [ref.at[slab, half].reshape(ROWS * 8, LANES)[at, :] for ref in (field, extra)]
+        return terms[0] + terms[1]
+
+    parts = []
+    for x in range(GROUP):
+        halves = [
+            jnp.concatenate([total(x, slab, half) for slab in range(SLABS)], axis=0)
+            for half in range(2)
+        ]
+        parts.append(dot3(left, split(jnp.concatenate(halves, axis=1))))
+    part = jnp.concatenate(parts, axis=0)
+    out[...] = dot3(split(part), right).reshape(GROUP, N, N)
 
 
 def backward(field, extra, basis_y, basis_z):
-    block = pl.BlockSpec((SLABS, 2, ROWS, 8, LANES), lambda x: (0, 0, 0, x // 8, 0))
+    block = pl.BlockSpec((SLABS, 2, ROWS, 8, LANES), lambda x: (0, 0, 0, x * GROUP // 8, 0))
     return pl.pallas_call(
         backward_kernel,
-        grid=(ROWS,),
+        grid=(ROWS // GROUP,),
         in_specs=[block, block, whole((N, N)), whole((N, N))],
-        out_specs=pl.BlockSpec((1, N, N), lambda x: (x, 0, 0)),
+        out_specs=pl.BlockSpec((GROUP, N, N), lambda x: (x, 0, 0)),
         out_shape=jax.ShapeDtypeStruct((ROWS, N, N), F32),
         scratch_shapes=[pltpu.VMEM((2, N, N), BF16), pltpu.VMEM((2, N, N), BF16)],
         compiler_params=params(),
@@ -394,17 +404,20 @@
     pieces = faces(base_zx, shift, own_x, ends, products, part0, part1)
     table = pieces[:, 4:].transpose(1, 0, 2, 3).reshape(3, N, N)
     following = from_behind(pieces[:, 2:4], "sub", -1)
+    pieces, following, lines = lax.optimization_barrier((pieces, following, lines))
     shares = exchange(pieces[:, 0:2] - following)
-    jumps = jnp.sum(shares, axis=0)
-    jumps = exchange(jnp.broadcast_to(jumps[None], (SLABS,) + jumps.shape))
+    own_jumps = jnp.sum(shares, axis=0)
+    jumps = exchange(jnp.broadcast_to(own_jumps[None], (SLABS,) + own_jumps.shape))
     jumps = jumps.transpose(1, 0, 2, 3).reshape(2, N, N)
+
+    spread = middle(base_xz, own_shift, basis_x, lines)
+    spread, jumps = lax.optimization_barrier((spread, jumps))
+    spread = exchange(spread)
 
     search0, image0, sums0 = chain0(jumps[0], gram_x, gram_y, stiff)
     before = from_behind(image0, "sub", 1)
     after = from_behind(image0, "sub", -1)
     alpha0 = step_length(sum_over_subs(sums0))
-
-    spread = exchange(middle(base_xz, own_shift, basis_x, lines))
 
     more = extra(base_xz, shift, own_x, ends, alpha0 * jnp.stack([image0, before]))
     scale = jnp.stack([alpha0, own_rho / next_rho])

time: 283 us -> 211 us (0.75)
  the two profiles are of different devices: /device:TPU:6 before, /device:TPU:82 now
where the time goes in v2:
time: 211 us; the launch traced here: 209 us
  Pallas kernels  101 us (48%)
  starting transfers between devices  41.2 us (20%)
  waiting for transfers between devices  33.3 us (16%)
  local copies, waits for them, and re-layouts  23.2 us (11%)
  between operations  6.07 us (3%)
  other arithmetic  4.6 us (2%)
    all_to_all x4, starting transfers between devices, exchange(): lax.all_to_all(block, 'slab', split_axis=0, concat_axis=0, tiled=True)  32.6 us
    pallas_call x1, Pallas kernels, faces(): pl.pallas_call(faces_kernel, grid=(N // 8,), in_specs=[whole((N, N)), sme...  31.4 us
    pallas_call x1, Pallas kernels, extra(): pl.pallas_call(extra_kernel, grid=(N // 8,), in_specs=[whole((N, N)), sme...  24.9 us
    all_to_all x4, waiting for transfers between devices, exchange(): lax.all_to_all(block, 'slab', split_axis=0, concat_axis=0, tiled=True)  23.5 us
    pallas_call x2, Pallas kernels, forward(): pl.pallas_call(forward_kernel, grid=(ROWS // GROUP,), in_specs=[pl.BlockS...  17.9 us
    unnamed x41, local copies, waits for them, and re-layouts  16.5 us
    pallas_call x1, Pallas kernels, backward(): pl.pallas_call(backward_kernel, grid=(ROWS // GROUP,), in_specs=[block, b...  10.7 us
    pallas_call x1, Pallas kernels, middle(): pl.pallas_call(middle_kernel, grid=(N // SLABS // GROUP,), in_specs=[whol...  6.9 us
  transfers between devices with their start and end apart: 13, of which 7 were waited for; matrix products, arithmetic and copies ran while one was open for 4% of the time, Pallas kernels for 38%

profile of v2, /device:TPU:82, one launch (start us, length us, event | category | flops | bytes accessed | tf_op | source)
XLA Modules:
  0.0 209.2 jit_solution(15014818377227730465)
XLA Ops:
  0.6 0.9 copy-done.1
  1.6 0.9 copy-done.6
  2.5 8.9 %forward.3.part1 = f32[16,2,16,16,128]{4,3,2,1,0:T(8,128)S(1)} custom-call(f32[16,256,256]{2,1,0:T(8,128)} %bitcast.25, f32[2,1,16,256,256]{4,3,2,1,0:T(8,128)} %coarse.3, f32[256,256]{1,0:T(8,128)S(1)} %copy-done.1, f32[256,256]{1,0:T(8,128)S(1)} %copy-done.6), custom_call_target="tpu_custom_call" | custom-call | flops 3221225472 | bytes 12582912 | tf_op jit(solution)/shard_map/forward/pallas_call | solution.py:73
  11.5 2.0 copy-done
  13.5 7.5 %all-to-all-start = ((f32[16,2,16,16,128]{4,3,2,1,0:T(8,128)}), f32[16,2,16,16,128]{4,3,2,1,0:T(8,128)}, u32[]{:S(2)}, u32[]{:S(2)}) async-start(f32[16,2,16,16,128]{4,3,2,1,0:T(8,128)} %copy-done), calls=%async_computation | async-start | bytes 8388608 | tf_op jit(solution)/shard_map/all_to_all | solution.py:374
  21.1 9.0 %forward.2.part0 = f32[16,2,16,16,128]{4,3,2,1,0:T(8,128)S(1)} custom-call(f32[16,256,256]{2,1,0:T(8,128)} %bitcast.26, f32[2,1,16,256,256]{4,3,2,1,0:T(8,128)} %coarse.3, f32[256,256]{1,0:T(8,128)S(1)} %copy-done.2, f32[256,256]{1,0:T(8,128)S(1)} %copy-done.7), custom_call_target="tpu_custom_call" | custom-call | flops 3221225472 | bytes 12582912 | tf_op jit(solution)/shard_map/forward/pallas_call | solution.py:73
  30.1 2.0 copy-done.5
  32.7 0.6 broadcast_multiply_fusion.shift
  33.4 0.8 add_multiply_fusion
  34.2 31.4 %faces.1 = f32[16,7,16,256]{3,2,1,0:T(8,128)S(1)} custom-call(f32[256,256]{1,0:T(8,128)S(1)} %get-tuple-element.40.base, f32[256]{0:T(256)S(1)} %broadcast_multiply_fusion.shift, f32[16,256]{1,0:T(8,128)S(1)} %get-tuple-element.45.own_x, f32[2,256]{1,0:T(2,128)S(1)} %pad_maximum_fusion.ends, f32[16,256]{1,0:T(8,128)S(1)} %get-tuple-element.44.products, ...), custom_call_target="tpu_custom_call" | custom-call | flops 33554432000 | bytes 8388608 | tf_op jit(solution)/shard_map/faces/pallas_call | solution.py:203
  65.7 6.7 %collective-permute-done = f32[16,2,16,256]{3,2,1,0:T(8,128)S(1)} collective-permute-done((f32[16,2,16,256]{3,2,1,0:T(8,128)S(1)}, f32[16,2,16,256]{3,2,1,0:T(8,128)S(1)}, u32[]{:S(2)}, u32[]{:S(2)}) %collective-permute-start) | collective-permute-done | bytes 524320 | tf_op jit(solution)/shard_map/ppermute | solution.py:360
  72.4 11.7 %all-to-all-done.lines = f32[16,2,16,16,128]{4,3,2,1,0:T(8,128)} async-done(((f32[16,2,16,16,128]{4,3,2,1,0:T(8,128)}), f32[16,2,16,16,128]{4,3,2,1,0:T(8,128)}, u32[]{:S(2)}, u32[]{:S(2)}) %all-to-all-start) | async-done | bytes 4194336 | tf_op jit(solution)/shard_map/all_to_all | solution.py:374
  84.1 0.9 slice_subtract_fusion
  85.0 10.0 %all-to-all-start.1 = ((f32[16,2,16,256]{3,2,1,0:T(8,128)}), f32[16,2,16,256]{3,2,1,0:T(8,128)}, u32[]{:S(2)}, u32[]{:S(2)}) async-start(f32[16,2,16,256]{3,2,1,0:T(8,128)} %slice_subtract_fusion), calls=%async_computation.1 | async-start | bytes 1048576 | tf_op jit(solution)/shard_map/all_to_all | solution.py:374
  95.1 0.7 grams.1
  95.8 0.7 copy-done.10
  97.8 1.1 copy.16
  98.9 2.5 %all-to-all-done.1 = f32[16,2,16,256]{3,2,1,0:T(8,128)} async-done(((f32[16,2,16,256]{3,2,1,0:T(8,128)}), f32[16,2,16,256]{3,2,1,0:T(8,128)}, u32[]{:S(2)}, u32[]{:S(2)}) %all-to-all-start.1) | async-done | bytes 524320 | tf_op jit(solution)/shard_map/all_to_all | solution.py:374
  101.4 1.1 reduce_sum.9
  102.5 0.9 broadcast_in_dim.8
  103.4 7.9 %all-to-all-start.2 = ((f32[16,2,16,256]{3,2,1,0:T(8,128)}), f32[16,2,16,256]{3,2,1,0:T(8,128)}, u32[]{:S(2)}, u32[]{:S(2)}) async-start(f32[16,2,16,256]{3,2,1,0:T(8,128)} %broadcast_in_dim.8), calls=%async_computation.2 | async-start | bytes 1048576 | tf_op jit(solution)/shard_map/all_to_all | solution.py:374
  111.3 6.9 %middle.1 = f32[16,2,16,16,128]{4,3,2,1,0:T(8,128)S(1)} custom-call(f32[256,256]{1,0:T(8,128)S(1)} %get-tuple-element.41.base, f32[16]{0:T(128)S(1)} %dynamic_slice.13.shift, f32[256,256]{1,0:T(8,128)S(1)} %copy-done.8, f32[16,2,16,16,128]{4,3,2,1,0:T(8,128)} %all-to-all-done.lines), custom_call_target="tpu_custom_call" | custom-call | flops 3221225472 | bytes 8388608 | tf_op jit(solution)/shard_map/middle/pallas_call | solution.py:115
  118.3 2.0 copy-done.4
  120.3 1.1 copy.15
  121.3 0.7 slice_bitcast_fusion.1
  122.1 0.9 copy-done.11
  123.0 0.9 copy-done.14
  124.0 2.1 %chain0.1 = (f32[256,256]{1,0:T(8,128)S(1)}, f32[256,256]{1,0:T(8,128)S(1)}, f32[8,128]{1,0:T(8,128)S(1)}) custom-call(f32[256,256]{1,0:T(8,128)S(1)} %get-tuple-element.30.jump, f32[256,256]{1,0:T(8,128)S(1)} %copy-done.11, f32[256,256]{1,0:T(8,128)S(1)} %copy-done.14, f32[256,256]{1,0:T(8,128)S(1)} %multiply_bitcast_fusion.stiff), custom_call_target="tpu_custom_call" | custom-call | flops 805306368 | bytes 1572864 | tf_op jit(solution)/shard_map/chain0/pallas_call | solution.py:289
  126.2 1.2 collective-permute-done.1
  127.9 1.7 collective-permute-start.5
  129.7 7.2 %all-to-all-start.3 = ((f32[16,2,16,16,128]{4,3,2,1,0:T(8,128)}), f32[16,2,16,16,128]{4,3,2,1,0:T(8,128)}, u32[]{:S(2)}, u32[]{:S(2)}) async-start(f32[16,2,16,16,128]{4,3,2,1,0:T(8,128)} %copy-done.4), calls=%async_computation.3 | async-start | bytes 8388608 | tf_op jit(solution)/shard_map/all_to_all | solution.py:374
  136.9 2.7 %collective-permute-start.3 = (f32[8,128]{1,0:T(8,128)S(1)}, f32[8,128]{1,0:T(8,128)S(1)}, u32[]{:S(2)}, u32[]{:S(2)}) collective-permute-start(f32[8,128]{1,0:T(8,128)S(1)} %add.87), channel_id=1, source_target_pairs={{0,64},{16,80},{32,96},{48,112},{64,0},{80,16},{96,32},{112,48},{1... | collective-permute-start | bytes 12296 | tf_op jit(solution)/shard_map/ppermute | solution.py:365
  139.6 1.0 slice_bitcast_fusion
  141.9 1.2 copy.17
  145.1 0.9 copy-done.9
  146.0 0.9 copy-done.12
  147.0 0.9 copy-done.15
  147.9 4.1 %chain1.1 = (f32[256,256]{1,0:T(8,128)S(1)}, f32[8,128]{1,0:T(8,128)S(1)}, f32[16,256]{1,0:T(8,128)}) custom-call(f32[2]{0:T(128)S(1)} %pad_maximum_fusion.1.scale, f32[256,256]{1,0:T(8,128)S(1)} %copy-done.9, f32[256,256]{1,0:T(8,128)S(1)} %get-tuple-element.24.image, f32[256,256]{1,0:T(8,128)} %collective-permute-done.4.before, ...), custom_call_target="tpu_custom_call" | custom-call | flops 838860800 | bytes 3145728 | tf_op jit(solution)/shard_map/chain1/pallas_call | solution.py:314
  152.0 1.2 collective-permute-done.6
  153.2 1.8 collective-permute-start.7
  155.0 1.0 maximum_multiply_fusion.faces_in
  156.0 0.8 collective-permute-done.7
  156.8 1.6 collective-permute-start.8
  158.4 24.9 %extra.1 = f32[16,2,16,16,128]{4,3,2,1,0:T(8,128)S(1)} custom-call(f32[256,256]{1,0:T(8,128)S(1)} %get-tuple-element.41.base, f32[256]{0:T(256)S(1)} %broadcast_multiply_fusion.shift, f32[16,256]{1,0:T(8,128)S(1)} %get-tuple-element.45.own_x, f32[2,256]{1,0:T(2,128)S(1)} %pad_maximum_fusion.ends, f32[2,256,256]{2,1,0:T(8,128)S(1)} %maximum_multiply_fusion.faces_in), custom_call_target="tpu_custom_call" | custom-call | flops 33554432000 | bytes 4194304 | tf_op jit(solution)/shard_map/extra/pallas_call | solution.py:239
  183.3 2.0 copy-done.3
  187.1 2.1 %final.1 = f32[16,256]{1,0:T(8,128)} custom-call(f32[2]{0:T(128)S(1)} %pad_maximum_fusion.2.scale, f32[256,256]{1,0:T(8,128)S(1)} %get-tuple-element.26.search0, f32[256,256]{1,0:T(8,128)S(1)} %get-tuple-element.27.search1, f32[16,256]{1,0:T(8,128)S(1)} %get-tuple-element.45.own_x, f32[256,256]{1,0:T(8,128)S(1)} %copy-done.2), custom_call_target="tpu_custom_call" | custom-call | tf_op jit(solution)/shard_map/final/pallas_call | solution.py:336
  189.2 9.2 %all-to-all-done.3.field = f32[16,2,16,16,128]{4,3,2,1,0:T(8,128)} async-done(((f32[16,2,16,16,128]{4,3,2,1,0:T(8,128)}), f32[16,2,16,16,128]{4,3,2,1,0:T(8,128)}, u32[]{:S(2)}, u32[]{:S(2)}) %all-to-all-start.3) | async-done | bytes 4194336 | tf_op jit(solution)/shard_map/all_to_all | solution.py:374
  198.5 10.7 %backward.1 = f32[16,256,256]{2,1,0:T(8,128)} custom-call(f32[16,2,16,16,128]{4,3,2,1,0:T(8,128)} %all-to-all-done.3.field, f32[16,2,16,16,128]{4,3,2,1,0:T(8,128)} %copy-done.3, f32[256,256]{1,0:T(8,128)S(1)} %copy-done.2, f32[256,256]{1,0:T(8,128)S(1)} %copy-done.7), custom_call_target="tpu_custom_call" | custom-call | flops 3221225472 | bytes 12582912 | tf_op jit(solution)/shard_map/backward/pallas_call | solution.py:156
  (56 shorter events, 2.8 us)
Async XLA Ops:
  0.6 1.0 copy-start.1
  1.6 0.9 copy-start.6
  11.5 2.0 copy-start
  13.5 7.5 %copy-start.7 = (f32[256,256]{1,0:T(8,128)S(1)}, f32[256,256]{1,0:T(8,128)}, u32[]{:S(2)}) copy-start(f32[256,256]{1,0:T(8,128)} %basis_z.5) | copy-start | bytes 786436
  13.5 7.5 %copy-start.2 = (f32[256,256]{1,0:T(8,128)S(1)}, f32[256,256]{1,0:T(8,128)}, u32[]{:S(2)}) copy-start(f32[256,256]{1,0:T(8,128)} %basis_y.11) | copy-start | bytes 786436
  13.5 70.6 %all-to-all-start = ((f32[16,2,16,16,128]{4,3,2,1,0:T(8,128)}), f32[16,2,16,16,128]{4,3,2,1,0:T(8,128)}, u32[]{:S(2)}, u32[]{:S(2)}) async-start(f32[16,2,16,16,128]{4,3,2,1,0:T(8,128)} %copy-done), calls=%async_computation | async-start | bytes 8388608 | tf_op jit(solution)/shard_map/all_to_all | solution.py:374
  21.0 11.1 %copy-start.18 = (f32[8]{0:T(128)S(1)}, f32[8]{0:T(128)}, u32[]{:S(2)}) copy-start(f32[8]{0:T(128)} %param.12) | copy-start | bytes 100
  21.0 11.7 %copy-start.19 = (f32[256]{0:T(256)S(1)}, f32[256]{0:T(256)}, u32[]{:S(2)}) copy-start(f32[256]{0:T(256)} %param.17) | copy-start | bytes 3076
  21.1 12.3 %copy-start.8 = (f32[256,256]{1,0:T(8,128)S(1)}, f32[256,256]{1,0:T(8,128)}, u32[]{:S(2)}) copy-start(f32[256,256]{1,0:T(8,128)} %basis_x.3) | copy-start | bytes 786436
  21.1 12.4 %copy-start.16 = (f32[256]{0:T(256)S(1)}, f32[256]{0:T(256)}, u32[]{:S(2)}) copy-start(f32[256]{0:T(256)} %param.16) | copy-start | bytes 3076
  21.1 12.4 %copy-start.17 = (f32[256]{0:T(256)S(1)}, f32[256]{0:T(256)}, u32[]{:S(2)}) copy-start(f32[256]{0:T(256)} %param.18) | copy-start | bytes 3076
  30.1 2.0 copy-start.5
  65.7 6.7 %collective-permute-start = (f32[16,2,16,256]{3,2,1,0:T(8,128)S(1)}, f32[16,2,16,256]{3,2,1,0:T(8,128)S(1)}, u32[]{:S(2)}, u32[]{:S(2)}) collective-permute-start(f32[16,2,16,256]{3,2,1,0:T(8,128)S(1)} %slice.44), channel_id=1, source_target_pairs={{16,0},{32,16},{48,32},{64,48},{80,64},{96,80},{112,96},{0,112},{1... | collective-permute-start | bytes 1572872 | tf_op jit(solution)/shard_map/ppermute | solution.py:360
  85.0 16.4 %all-to-all-start.1 = ((f32[16,2,16,256]{3,2,1,0:T(8,128)}), f32[16,2,16,256]{3,2,1,0:T(8,128)}, u32[]{:S(2)}, u32[]{:S(2)}) async-start(f32[16,2,16,256]{3,2,1,0:T(8,128)} %slice_subtract_fusion), calls=%async_computation.1 | async-start | bytes 1048576 | tf_op jit(solution)/shard_map/all_to_all | solution.py:374
  95.8 0.7 copy-start.10
  96.5 6.9 %copy-start.13 = (f32[256,256]{1,0:T(8,128)}, f32[256,256]{1,0:T(8,128)S(1)}, u32[]{:S(2)}) copy-start(f32[256,256]{1,0:T(8,128)S(1)} %get-tuple-element.22.gram_y) | copy-start | bytes 786436
  103.4 16.9 %all-to-all-start.2 = ((f32[16,2,16,256]{3,2,1,0:T(8,128)}), f32[16,2,16,256]{3,2,1,0:T(8,128)}, u32[]{:S(2)}, u32[]{:S(2)}) async-start(f32[16,2,16,256]{3,2,1,0:T(8,128)} %broadcast_in_dim.8), calls=%async_computation.2 | async-start | bytes 1048576 | tf_op jit(solution)/shard_map/all_to_all | solution.py:374
  118.2 2.0 copy-start.4
  122.1 0.9 copy-start.11
  123.0 0.9 copy-start.14
  126.1 1.2 collective-permute-start.1
  127.4 9.5 %collective-permute-start.2 = (f32[8,128]{1,0:T(8,128)S(1)}, f32[8,128]{1,0:T(8,128)S(1)}, u32[]{:S(2)}, u32[]{:S(2)}) collective-permute-start(f32[8,128]{1,0:T(8,128)S(1)} %add.86), channel_id=1, source_target_pairs={{0,32},{16,48},{32,0},{48,16},{64,96},{80,112},{96,64},{112,80},{1... | collective-permute-start | bytes 12296 | tf_op jit(solution)/shard_map/ppermute | solution.py:365
  127.9 17.1 %collective-permute-start.4 = (f32[256,256]{1,0:T(8,128)S(1)}, f32[256,256]{1,0:T(8,128)}, u32[]{:S(2)}, u32[]{:S(2)}) collective-permute-start(f32[256,256]{1,0:T(8,128)S(1)} %get-tuple-element.24.image), channel_id=1, source_target_pairs={{112,0},{0,16},{16,32},{32,48},{48,64},{64,80},{80,96},{96,112},{1... | collective-permute-start | bytes 786440 | tf_op jit(solution)/shard_map/ppermute | solution.py:360
  127.9 17.1 %collective-permute-start.5 = (f32[256,256]{1,0:T(8,128)S(1)}, f32[256,256]{1,0:T(8,128)}, u32[]{:S(2)}, u32[]{:S(2)}) collective-permute-start(f32[256,256]{1,0:T(8,128)S(1)} %get-tuple-element.24.image), channel_id=1, source_target_pairs={{16,0},{32,16},{48,32},{64,48},{80,64},{96,80},{112,96},{0,112},{1... | collective-permute-start | bytes 786440 | tf_op jit(solution)/shard_map/ppermute | solution.py:360
  129.7 68.8 %all-to-all-start.3 = ((f32[16,2,16,16,128]{4,3,2,1,0:T(8,128)}), f32[16,2,16,16,128]{4,3,2,1,0:T(8,128)}, u32[]{:S(2)}, u32[]{:S(2)}) async-start(f32[16,2,16,16,128]{4,3,2,1,0:T(8,128)} %copy-done.4), calls=%async_computation.3 | async-start | bytes 8388608 | tf_op jit(solution)/shard_map/all_to_all | solution.py:374
  136.9 6.2 %collective-permute-start.3 = (f32[8,128]{1,0:T(8,128)S(1)}, f32[8,128]{1,0:T(8,128)S(1)}, u32[]{:S(2)}, u32[]{:S(2)}) collective-permute-start(f32[8,128]{1,0:T(8,128)S(1)} %add.87), channel_id=1, source_target_pairs={{0,64},{16,80},{32,96},{48,112},{64,0},{80,16},{96,32},{112,48},{1... | collective-permute-start | bytes 12296 | tf_op jit(solution)/shard_map/ppermute | solution.py:365
  145.1 1.0 copy-start.9
  146.0 0.9 copy-start.12
  147.0 0.9 copy-start.15
  152.0 1.2 collective-permute-start.6
  153.2 3.6 %collective-permute-start.7 = (f32[8,128]{1,0:T(8,128)S(1)}, f32[8,128]{1,0:T(8,128)S(1)}, u32[]{:S(2)}, u32[]{:S(2)}) collective-permute-start(f32[8,128]{1,0:T(8,128)S(1)} %add.90), channel_id=1, source_target_pairs={{0,32},{16,48},{32,0},{48,16},{64,96},{80,112},{96,64},{112,80},{1... | collective-permute-start | bytes 12296 | tf_op jit(solution)/shard_map/ppermute | solution.py:365
  156.8 28.5 %collective-permute-start.8 = (f32[8,128]{1,0:T(8,128)S(1)}, f32[8,128]{1,0:T(8,128)S(1)}, u32[]{:S(2)}, u32[]{:S(2)}) collective-permute-start(f32[8,128]{1,0:T(8,128)S(1)} %add.91), channel_id=1, source_target_pairs={{0,64},{16,80},{32,96},{48,112},{64,0},{80,16},{96,32},{112,48},{1... | collective-permute-start | bytes 12296 | tf_op jit(solution)/shard_map/ppermute | solution.py:365
  183.3 2.0 copy-start.3

commit v3 on v2

--- a/solution.py
+++ b/solution.py
@@ -10,7 +10,7 @@
 HI = lax.Precision.HIGHEST
 F32 = jnp.float32
 BF16 = jnp.bfloat16
-VMEM_LIMIT = 48 * 1024 * 1024
+VMEM_LIMIT = 60 * 1024 * 1024
 N = 256
 ROWS = 16
 SLABS = 16
@@ -186,11 +186,11 @@
 def faces_kernel(base, shift, own_x, ends, products, part0, part1, out):
     block = pl.program_id(0)
     first, last = ends[0:1], ends[1:2]
-    for jj in range(8):
+    for jj in range(ROWS):
         a = jnp.concatenate([part0[0, 0, jj], part0[0, 1, jj]], axis=1)
         b = jnp.concatenate([part1[0, 0, jj], part1[0, 1, jj]], axis=1)
         rows = jnp.concatenate([a * last, b * last, a * first, b * first, products[...]], axis=0)
-        result = times_inverse(rows, base[...] + shift[block * 8 + jj])
+        result = dot3(split(rows), inverse_parts(base[...] + shift[block * ROWS + jj]))
         for face in range(4):
             piece = result[16 * face : 16 * face + 16] * own_x[...]
             out[0, face, jj : jj + 1] = jnp.sum(piece, axis=0, keepdims=True)
@@ -199,10 +199,10 @@
 
 
 def faces(base, shift, own_x, ends, products, part0, part1):
-    block = pl.BlockSpec((1, 2, 8, ROWS, LANES), lambda j: (j // 2, 0, j % 2, 0, 0))
+    block = pl.BlockSpec((1, 2, ROWS, ROWS, LANES), lambda j: (j, 0, 0, 0, 0))
     return pl.pallas_call(
         faces_kernel,
-        grid=(N // 8,),
+        grid=(N // ROWS,),
         in_specs=[
             whole((N, N)),
             smem(),
@@ -212,48 +212,51 @@
             block,
             block,
         ],
-        out_specs=pl.BlockSpec((1, 7, 8, N), lambda j: (j // 2, 0, j % 2, 0)),
+        out_specs=pl.BlockSpec((1, 7, ROWS, N), lambda j: (j, 0, 0, 0)),
         out_shape=jax.ShapeDtypeStruct((SLABS, 7, N // SLABS, N), F32),
         compiler_params=params(),
         cost_estimate=pl.CostEstimate(
-            flops=2 * 1000 * N**3, bytes_accessed=8 * ROWS * N * N, transcendentals=N**3
+            flops=N**3, bytes_accessed=N * N, transcendentals=0
         ),
         name="faces",
     )(base, shift, own_x, ends, products, part0, part1)
 
 
-def extra_kernel(base, shift, own_x, ends, faces_in, out):
+def extra_kernel(base, shift, scale, own_x, ends, own, before, out):
     block = pl.program_id(0)
+    alpha = scale[0]
     first, last = ends[0:1], ends[1:2]
-    for jj in range(8):
-        upper = own_x[...] * faces_in[0, jj : jj + 1]
-        lower = own_x[...] * faces_in[1, jj : jj + 1]
+    for jj in range(ROWS):
+        upper = own_x[...] * (alpha * own[jj : jj + 1])
+        lower = own_x[...] * (alpha * before[jj : jj + 1])
         rows = jnp.concatenate([upper, lower], axis=0)
-        result = times_inverse(rows, base[...] + shift[block * 8 + jj])
+        result = times_inverse(rows, base[...] + shift[block * ROWS + jj])
         result = first * result[16:] - last * result[:16]
         for half in range(2):
             out[0, half, jj] = result[:, LANES * half : LANES * half + LANES]
 
 
-def extra(base, shift, own_x, ends, faces_in):
+def extra(base, shift, scale, own_x, ends, own, before):
     return pl.pallas_call(
         extra_kernel,
-        grid=(N // 8,),
+        grid=(N // ROWS,),
         in_specs=[
             whole((N, N)),
             smem(),
+            smem(),
             whole((ROWS, N)),
             whole((2, N)),
-            pl.BlockSpec((2, 8, N), lambda j: (0, j, 0)),
+            pl.BlockSpec((ROWS, N), lambda j: (j, 0)),
+            pl.BlockSpec((ROWS, N), lambda j: (j, 0)),
         ],
-        out_specs=pl.BlockSpec((1, 2, 8, ROWS, LANES), lambda j: (j // 2, 0, j % 2, 0, 0)),
+        out_specs=pl.BlockSpec((1, 2, ROWS, ROWS, LANES), lambda j: (j, 0, 0, 0, 0)),
         out_shape=jax.ShapeDtypeStruct(FIELD, F32),
         compiler_params=params(),
         cost_estimate=pl.CostEstimate(
-            flops=2 * 1000 * N**3, bytes_accessed=4 * ROWS * N * N, transcendentals=N**3
+            flops=N**3, bytes_accessed=N * N, transcendentals=0
         ),
         name="extra",
-    )(base, shift, own_x, ends, faces_in)
+    )(base, shift, scale, own_x, ends, own, before)
 
 
 def exact(a, b):
@@ -277,35 +280,39 @@
     return jnp.where(at == 0, upper, jnp.where(at == 1, lower, 0.0))
 
 
-def chain0_kernel(jump, gram_x, gram_y, stiff, search, image, sums):
+def chain0_kernel(scale, jumps, gram_x, gram_y, stiff, search, image, sums):
     search[...], image[...], upper, lower = precondition(
-        jump[...], gram_x[...], gram_y[...], stiff[...]
+        jumps[:, 0].reshape(N, N), gram_x[...], gram_y[...], scale[0] * stiff[...].T
     )
     sums[...] = scalars_block(upper, lower)
 
 
-def chain0(jump, gram_x, gram_y, stiff):
+def chain0(*args):
     face = jax.ShapeDtypeStruct((N, N), F32)
     return pl.pallas_call(
         chain0_kernel,
+        in_specs=[smem()] + [pl.BlockSpec(memory_space=pltpu.VMEM)] * 4,
         out_shape=(face, face, jax.ShapeDtypeStruct((8, 128), F32)),
         compiler_params=params(),
         cost_estimate=pl.CostEstimate(
-            flops=48 * N**3, bytes_accessed=24 * N * N, transcendentals=0
+            flops=N**3, bytes_accessed=N * N, transcendentals=0
         ),
         name="chain0",
-    )(jump, gram_x, gram_y, stiff)
+    )(*args)
 
 
 def chain1_kernel(
-    scale, jump, image, before, after, table, gram_x, gram_y, stiff, own_x, basis_y, search, sums, out
+    scale, jumps, image, before, after, pieces, gram_x, gram_y, stiff, own_x, basis_y, search, sums, out
 ):
-    alpha, ratio = scale[0], scale[1]
+    alpha, ratio, weight = scale[0], scale[1], scale[2]
     t = image[...]
+    table = [pieces[:, 4 + pair].reshape(N, N) for pair in range(3)]
     own = table[1] * before[...] - table[0] * t
     other = table[2] * t - table[1] * after[...]
-    q = jump[...] + alpha * (own - ratio * other)
-    search[...], _, upper, lower = precondition(q, gram_x[...], gram_y[...], stiff[...])
+    q = jumps[:, 1].reshape(N, N) + alpha * (own - ratio * other)
+    search[...], _, upper, lower = precondition(
+        q, gram_x[...], gram_y[...], weight * stiff[...].T
+    )
     sums[...] = scalars_block(upper, lower)
     out[...] = exact_t(exact_t(own_x[...], q), basis_y[...])
 
@@ -321,7 +328,7 @@
         ),
         compiler_params=params(),
         cost_estimate=pl.CostEstimate(
-            flops=50 * N**3, bytes_accessed=48 * N * N, transcendentals=0
+            flops=N**3, bytes_accessed=N * N, transcendentals=0
         ),
         name="chain1",
     )(*args)
@@ -338,6 +345,7 @@
         in_specs=[smem()] + [pl.BlockSpec(memory_space=pltpu.VMEM)] * 4,
         out_shape=jax.ShapeDtypeStruct((ROWS, N), F32),
         compiler_params=params(),
+        cost_estimate=pl.CostEstimate(flops=N**3, bytes_accessed=N * N, transcendentals=0),
         name="final",
     )(*args)
 
@@ -397,32 +405,29 @@
     ends = jnp.stack([basis_z[0], basis_z[N - 1]])
     products = jnp.stack([ends[1] * ends[1], ends[1] * ends[0], ends[0] * ends[0]])
     products = jnp.pad(products, ((0, 13), (0, 0)))
-    stiff = weight * face_stiff.T
     gram_x, gram_y = grams(basis_x, basis_y)
 
     part0 = forward(source, coarse, 0, basis_y, basis_z)
     pieces = faces(base_zx, shift, own_x, ends, products, part0, part1)
-    table = pieces[:, 4:].transpose(1, 0, 2, 3).reshape(3, N, N)
     following = from_behind(pieces[:, 2:4], "sub", -1)
     pieces, following, lines = lax.optimization_barrier((pieces, following, lines))
     shares = exchange(pieces[:, 0:2] - following)
     own_jumps = jnp.sum(shares, axis=0)
     jumps = exchange(jnp.broadcast_to(own_jumps[None], (SLABS,) + own_jumps.shape))
-    jumps = jumps.transpose(1, 0, 2, 3).reshape(2, N, N)
 
     spread = middle(base_xz, own_shift, basis_x, lines)
     spread, jumps = lax.optimization_barrier((spread, jumps))
     spread = exchange(spread)
 
-    search0, image0, sums0 = chain0(jumps[0], gram_x, gram_y, stiff)
+    search0, image0, sums0 = chain0(weight.reshape(1), jumps, gram_x, gram_y, face_stiff)
     before = from_behind(image0, "sub", 1)
     after = from_behind(image0, "sub", -1)
     alpha0 = step_length(sum_over_subs(sums0))
 
-    more = extra(base_xz, shift, own_x, ends, alpha0 * jnp.stack([image0, before]))
-    scale = jnp.stack([alpha0, own_rho / next_rho])
+    scale = jnp.stack([alpha0, own_rho / next_rho, weight])
+    more = extra(base_xz, shift, scale, own_x, ends, image0, before)
     search1, sums1, jump = chain1(
-        scale, jumps[1], image0, before, after, table, gram_x, gram_y, stiff, own_x, basis_y
+        scale, jumps, image0, before, after, pieces, gram_x, gram_y, face_stiff, own_x, basis_y
     )
     alpha1 = step_length(sum_over_subs(sums1))
     multipliers = final(jnp.stack([alpha0, alpha1]), search0, search1, own_x, basis_y)

time: 211 us -> 204 us (0.967)
  the two profiles are of different devices: /device:TPU:82 before, /device:TPU:6 now
where the time goes in v3:
time: 204 us; the launch traced here: 201 us
  Pallas kernels  106 us (52%)
  waiting for transfers between devices  29.3 us (14%)
  starting transfers between devices  23.8 us (12%)
  blocking collectives  20.1 us (10%)
  other arithmetic  9.28 us (5%)
  local copies, waits for them, and re-layouts  6.47 us (3%)
  between operations  5.92 us (3%)
    pallas_call x1, Pallas kernels, faces(): pl.pallas_call(faces_kernel, grid=(N // ROWS,), in_specs=[whole((N, N)),...  27.9 us
    pallas_call x1, Pallas kernels, extra(): pl.pallas_call(extra_kernel, grid=(N // ROWS,), in_specs=[whole((N, N)),...  23.5 us
    pallas_call x2, Pallas kernels, forward(): pl.pallas_call(forward_kernel, grid=(ROWS // GROUP,), in_specs=[pl.BlockS...  21.2 us
    all_to_all x1, blocking collectives, exchange(): lax.all_to_all(block, 'slab', split_axis=0, concat_axis=0, tiled=True)  20.1 us
    all_to_all x3, starting transfers between devices, exchange(): lax.all_to_all(block, 'slab', split_axis=0, concat_axis=0, tiled=True)  17.7 us
    all_to_all x3, waiting for transfers between devices, exchange(): lax.all_to_all(block, 'slab', split_axis=0, concat_axis=0, tiled=True)  11.9 us
    pallas_call x1, Pallas kernels, backward(): pl.pallas_call(backward_kernel, grid=(ROWS // GROUP,), in_specs=[block, b...  10.8 us
    ppermute x6, waiting for transfers between devices, sum_over_subs(): sums = sums + lax.ppermute(sums, 'sub', [(i, i ^ bit) for i in range(8)])  10.7 us
  transfers between devices with their start and end apart: 12, of which 8 were waited for; matrix products, arithmetic and copies ran while one was open for 6% of the time, Pallas kernels for 42%

profile of v3, /device:TPU:6, one launch (start us, length us, event | category | flops | bytes accessed | tf_op | source)
XLA Modules:
  0.0 200.8 jit_solution(17369069905008438693)
XLA Ops:
  0.6 10.6 %forward.3.part1 = f32[16,2,16,16,128]{4,3,2,1,0:T(8,128)} custom-call(f32[16,256,256]{2,1,0:T(8,128)} %bitcast.10, f32[2,1,16,256,256]{4,3,2,1,0:T(8,128)} %coarse.3, f32[256,256]{1,0:T(8,128)} %basis_y.11, f32[256,256]{1,0:T(8,128)} %basis_z.5), custom_call_target="tpu_custom_call" | custom-call | flops 3221225472 | bytes 12582912 | tf_op jit(solution)/shard_map/forward/pallas_call | solution.py:73
  11.2 0.0 copy-start.5
  11.2 8.2 %all-to-all-start = ((f32[16,2,16,16,128]{4,3,2,1,0:T(8,128)}), f32[16,2,16,16,128]{4,3,2,1,0:T(8,128)}, u32[]{:S(2)}, u32[]{:S(2)}) async-start(f32[16,2,16,16,128]{4,3,2,1,0:T(8,128)} %forward.3.part1), calls=%async_computation | async-start | bytes 8388608 | tf_op jit(solution)/shard_map/all_to_all | solution.py:382
  19.5 0.6 fusion.2
  20.1 0.7 slice_multiply_fusion.1
  20.9 0.6 pad_maximum_fusion.ends
  21.4 1.3 select_maximum_fusion
  22.8 1.2 broadcast_multiply_fusion.shift
  24.0 1.6 add_multiply_fusion
  25.6 10.6 %forward.2.part0 = f32[16,2,16,16,128]{4,3,2,1,0:T(8,128)} custom-call(f32[16,256,256]{2,1,0:T(8,128)} %bitcast.11, f32[2,1,16,256,256]{4,3,2,1,0:T(8,128)} %coarse.3, f32[256,256]{1,0:T(8,128)} %basis_y.11, f32[256,256]{1,0:T(8,128)} %basis_z.5), custom_call_target="tpu_custom_call" | custom-call | flops 3221225472 | bytes 12582912 | tf_op jit(solution)/shard_map/forward/pallas_call | solution.py:73
  36.2 27.9 %faces.1.pieces = f32[16,7,16,256]{3,2,1,0:T(8,128)} custom-call(f32[256,256]{1,0:T(8,128)} %get-tuple-element.38.base, f32[256]{0:T(256)} %broadcast_multiply_fusion.shift, f32[16,256]{1,0:T(8,128)} %get-tuple-element.43.own_x, f32[2,256]{1,0:T(2,128)} %pad_maximum_fusion.ends, f32[16,256]{1,0:T(8,128)} %get-tuple-element.42.products, ...), custom_call_target="tpu_custom_call" | custom-call | flops 16777216 | bytes 65536 | tf_op jit(solution)/shard_map/faces/pallas_call | solution.py:203
  64.1 1.1 slice.32
  65.2 0.0 collective-permute-start
  65.2 6.7 %collective-permute-done = f32[16,2,16,256]{3,2,1,0:T(8,128)S(1)} collective-permute-done((f32[16,2,16,256]{3,2,1,0:T(8,128)S(1)}, f32[16,2,16,256]{3,2,1,0:T(8,128)S(1)}, u32[]{:S(2)}, u32[]{:S(2)}) %collective-permute-start) | collective-permute-done | bytes 524320 | tf_op jit(solution)/shard_map/ppermute | solution.py:368
  71.9 10.5 %all-to-all-done.lines = f32[16,2,16,16,128]{4,3,2,1,0:T(8,128)} async-done(((f32[16,2,16,16,128]{4,3,2,1,0:T(8,128)}), f32[16,2,16,16,128]{4,3,2,1,0:T(8,128)}, u32[]{:S(2)}, u32[]{:S(2)}) %all-to-all-start) | async-done | bytes 4194336 | tf_op jit(solution)/shard_map/all_to_all | solution.py:382
  82.4 1.1 slice_subtract_fusion
  83.6 20.1 %all_to_all.20 = f32[16,2,16,256]{3,2,1,0:T(8,128)S(1)} all-to-all(f32[16,2,16,256]{3,2,1,0:T(8,128)S(1)} %slice_subtract_fusion), channel_id=1, replica_groups=mesh['sub'=8,'slab'=16] {'slab'}, dimensions={0} | all-to-all | bytes 1048576 | tf_op jit(solution)/shard_map/all_to_all | solution.py:382
  103.6 0.9 broadcast_in_dim.8
  104.5 3.6 %all-to-all-start.2 = ((f32[16,2,16,256]{3,2,1,0:T(8,128)}), f32[16,2,16,256]{3,2,1,0:T(8,128)S(1)}, u32[]{:S(2)}, u32[]{:S(2)}) async-start(f32[16,2,16,256]{3,2,1,0:T(8,128)} %broadcast_in_dim.8), calls=%async_computation.2 | async-start | bytes 1048576 | tf_op jit(solution)/shard_map/all_to_all | solution.py:382
  108.1 0.6 dynamic_slice.13.shift
  108.7 8.1 %middle.1 = f32[16,2,16,16,128]{4,3,2,1,0:T(8,128)} custom-call(f32[256,256]{1,0:T(8,128)} %get-tuple-element.39.base, f32[16]{0:T(128)} %dynamic_slice.13.shift, f32[256,256]{1,0:T(8,128)} %basis_x.3, f32[16,2,16,16,128]{4,3,2,1,0:T(8,128)} %all-to-all-done.lines), custom_call_target="tpu_custom_call" | custom-call | flops 3221225472 | bytes 8388608 | tf_op jit(solution)/shard_map/middle/pallas_call | solution.py:115
  116.8 1.4 all-to-all-done.2.jumps
  118.2 0.8 copy-done
  119.0 5.8 %all-to-all-start.3 = ((f32[16,2,16,16,128]{4,3,2,1,0:T(8,128)}), f32[16,2,16,16,128]{4,3,2,1,0:T(8,128)}, u32[]{:S(2)}, u32[]{:S(2)}) async-start(f32[16,2,16,16,128]{4,3,2,1,0:T(8,128)} %middle.1), calls=%async_computation.3 | async-start | bytes 8388608 | tf_op jit(solution)/shard_map/all_to_all | solution.py:382
  124.8 2.6 %grams.1 = (f32[256,256]{1,0:T(8,128)}, f32[256,256]{1,0:T(8,128)}) custom-call(f32[256,256]{1,0:T(8,128)} %basis_x.3, f32[256,256]{1,0:T(8,128)} %basis_y.11), custom_call_target="tpu_custom_call" | custom-call | tf_op jit(solution)/shard_map/grams/pallas_call | solution.py:360
  128.6 4.0 %chain0.1 = (f32[256,256]{1,0:T(8,128)}, f32[256,256]{1,0:T(8,128)}, f32[8,128]{1,0:T(8,128)}) custom-call(f32[1]{0:T(128)} %bitcast.3.scale, f32[16,2,16,256]{3,2,1,0:T(8,128)} %copy-done, f32[256,256]{1,0:T(8,128)} %get-tuple-element.21.gram_x, f32[256,256]{1,0:T(8,128)} %get-tuple-element.22.gram_y, f32[256,256]{1,0:T(8,128)} %stiff.3), custom_call_target="tpu_custom_call" | custom-call | flops 16777216 | bytes 65536 | tf_op jit(solution)/shard_map/chain0/pallas_call | solution.py:292
  132.6 1.7 collective-permute-start.5
  134.4 1.4 collective-permute-done.1
  135.8 0.7 add.86
  136.5 0.8 collective-permute-start.2
  137.2 2.8 %collective-permute-done.2 = f32[8,128]{1,0:T(8,128)S(1)} collective-permute-done((f32[8,128]{1,0:T(8,128)S(1)}, f32[8,128]{1,0:T(8,128)S(1)}, u32[]{:S(2)}, u32[]{:S(2)}) %collective-permute-start.2) | collective-permute-done | bytes 4128 | tf_op jit(solution)/shard_map/ppermute | solution.py:373
  140.1 1.3 collective-permute-start.3
  142.7 2.5 %collective-permute-done.3 = f32[8,128]{1,0:T(8,128)S(1)} collective-permute-done((f32[8,128]{1,0:T(8,128)S(1)}, f32[8,128]{1,0:T(8,128)S(1)}, u32[]{:S(2)}, u32[]{:S(2)}) %collective-permute-start.3) | collective-permute-done | bytes 4128 | tf_op jit(solution)/shard_map/ppermute | solution.py:373
  145.2 0.5 fusion.1
  147.0 0.7 pad_maximum_fusion.1.scale
  147.7 0.7 copy-done.1
  148.4 0.7 copy-done.2
  149.1 5.2 %chain1.1 = (f32[256,256]{1,0:T(8,128)}, f32[8,128]{1,0:T(8,128)}, f32[16,256]{1,0:T(8,128)}) custom-call(f32[3]{0:T(128)} %pad_maximum_fusion.1.scale, f32[16,2,16,256]{3,2,1,0:T(8,128)} %copy-done, f32[256,256]{1,0:T(8,128)} %get-tuple-element.24.own.image, f32[256,256]{1,0:T(8,128)} %copy-done.1, f32[256,256]{1,0:T(8,128)} %copy-done.2, ...), custom_call_target="tpu_custom_call" | custom-call | flops 16777216 | bytes 65536 | tf_op jit(solution)/shard_map/chain1/pallas_call | solution.py:321
  154.3 1.4 collective-permute-done.6
  155.7 0.7 add.90
  156.4 1.0 collective-permute-start.7
  157.3 2.6 %collective-permute-done.7 = f32[8,128]{1,0:T(8,128)S(1)} collective-permute-done((f32[8,128]{1,0:T(8,128)S(1)}, f32[8,128]{1,0:T(8,128)S(1)}, u32[]{:S(2)}, u32[]{:S(2)}) %collective-permute-start.7) | collective-permute-done | bytes 4128 | tf_op jit(solution)/shard_map/ppermute | solution.py:373
  160.0 1.3 collective-permute-start.8
  161.3 23.5 %extra.1 = f32[16,2,16,16,128]{4,3,2,1,0:T(8,128)} custom-call(f32[256,256]{1,0:T(8,128)} %get-tuple-element.39.base, f32[256]{0:T(256)} %broadcast_multiply_fusion.shift, f32[3]{0:T(128)} %pad_maximum_fusion.1.scale, f32[16,256]{1,0:T(8,128)} %get-tuple-element.43.own_x, f32[2,256]{1,0:T(2,128)} %pad_maximum_fusion.ends, ...), custom_call_target="tpu_custom_call" | custom-call | flops 16777216 | bytes 65536 | tf_op jit(solution)/shard_map/extra/pallas_call | solution.py:240
  184.8 0.6 fusion
  186.7 0.7 pad_maximum_fusion.2.scale
  187.3 2.7 %final.1 = f32[16,256]{1,0:T(8,128)} custom-call(f32[2]{0:T(128)} %pad_maximum_fusion.2.scale, f32[256,256]{1,0:T(8,128)} %get-tuple-element.26.search0, f32[256,256]{1,0:T(8,128)} %get-tuple-element.27.search1, f32[16,256]{1,0:T(8,128)} %get-tuple-element.43.own_x, f32[256,256]{1,0:T(8,128)} %basis_y.11), custom_call_target="tpu_custom_call" | custom-call | flops 16777216 | bytes 65536 | tf_op jit(solution)/shard_map/final/pallas_call | solution.py:343
  190.0 10.8 %backward.1 = f32[16,256,256]{2,1,0:T(8,128)} custom-call(f32[16,2,16,16,128]{4,3,2,1,0:T(8,128)} %all-to-all-done.3.field, f32[16,2,16,16,128]{4,3,2,1,0:T(8,128)} %extra.1, f32[256,256]{1,0:T(8,128)} %basis_y.11, f32[256,256]{1,0:T(8,128)} %basis_z.5), custom_call_target="tpu_custom_call" | custom-call | flops 3221225472 | bytes 12582912 | tf_op jit(solution)/shard_map/backward/pallas_call | solution.py:156
  (24 shorter events, 0.1 us)
Async XLA Ops:
  11.2 8.3 %copy-start.6 = (f32[8]{0:T(128)S(1)}, f32[8]{0:T(128)}, u32[]{:S(2)}) copy-start(f32[8]{0:T(128)} %param.12) | copy-start | bytes 100
  11.2 11.5 %copy-start.7 = (f32[256]{0:T(256)S(1)}, f32[256]{0:T(256)}, u32[]{:S(2)}) copy-start(f32[256]{0:T(256)} %param.17) | copy-start | bytes 3076
  11.2 12.8 %copy-start.4 = (f32[256]{0:T(256)S(1)}, f32[256]{0:T(256)}, u32[]{:S(2)}) copy-start(f32[256]{0:T(256)} %param.16) | copy-start | bytes 3076
  11.2 12.7 %copy-start.5 = (f32[256]{0:T(256)S(1)}, f32[256]{0:T(256)}, u32[]{:S(2)}) copy-start(f32[256]{0:T(256)} %param.18) | copy-start | bytes 3076
  11.2 71.2 %all-to-all-start = ((f32[16,2,16,16,128]{4,3,2,1,0:T(8,128)}), f32[16,2,16,16,128]{4,3,2,1,0:T(8,128)}, u32[]{:S(2)}, u32[]{:S(2)}) async-start(f32[16,2,16,16,128]{4,3,2,1,0:T(8,128)} %forward.3.part1), calls=%async_computation | async-start | bytes 8388608 | tf_op jit(solution)/shard_map/all_to_all | solution.py:382
  64.1 44.0 %copy-start.3 = (f32[256]{0:T(256)S(1)}, f32[256]{0:T(256)}, u32[]{:S(2)}) copy-start(f32[256]{0:T(256)} %broadcast_multiply_fusion.shift) | copy-start | bytes 3076
  65.2 6.7 %collective-permute-start = (f32[16,2,16,256]{3,2,1,0:T(8,128)S(1)}, f32[16,2,16,256]{3,2,1,0:T(8,128)S(1)}, u32[]{:S(2)}, u32[]{:S(2)}) collective-permute-start(f32[16,2,16,256]{3,2,1,0:T(8,128)S(1)} %slice.32), channel_id=1, source_target_pairs={{16,0},{32,16},{48,32},{64,48},{80,64},{96,80},{112,96},{0,112},{1... | collective-permute-start | bytes 1572872 | tf_op jit(solution)/shard_map/ppermute | solution.py:368
  104.5 13.6 %all-to-all-start.2 = ((f32[16,2,16,256]{3,2,1,0:T(8,128)}), f32[16,2,16,256]{3,2,1,0:T(8,128)S(1)}, u32[]{:S(2)}, u32[]{:S(2)}) async-start(f32[16,2,16,256]{3,2,1,0:T(8,128)} %broadcast_in_dim.8), calls=%async_computation.2 | async-start | bytes 1048576 | tf_op jit(solution)/shard_map/all_to_all | solution.py:382
  118.2 0.8 copy-start
  119.0 71.1 %all-to-all-start.3 = ((f32[16,2,16,16,128]{4,3,2,1,0:T(8,128)}), f32[16,2,16,16,128]{4,3,2,1,0:T(8,128)}, u32[]{:S(2)}, u32[]{:S(2)}) async-start(f32[16,2,16,16,128]{4,3,2,1,0:T(8,128)} %middle.1), calls=%async_computation.3 | async-start | bytes 8388608 | tf_op jit(solution)/shard_map/all_to_all | solution.py:382
  132.6 15.0 %collective-permute-start.4 = (f32[256,256]{1,0:T(8,128)}, f32[256,256]{1,0:T(8,128)S(1)}, u32[]{:S(2)}, u32[]{:S(2)}) collective-permute-start(f32[256,256]{1,0:T(8,128)} %get-tuple-element.24.own.image), channel_id=1, source_target_pairs={{112,0},{0,16},{16,32},{32,48},{48,64},{64,80},{80,96},{96,112},{1... | collective-permute-start | bytes 786440 | tf_op jit(solution)/shard_map/ppermute | solution.py:368
  132.6 15.0 %collective-permute-start.5 = (f32[256,256]{1,0:T(8,128)}, f32[256,256]{1,0:T(8,128)S(1)}, u32[]{:S(2)}, u32[]{:S(2)}) collective-permute-start(f32[256,256]{1,0:T(8,128)} %get-tuple-element.24.own.image), channel_id=1, source_target_pairs={{16,0},{32,16},{48,32},{64,48},{80,64},{96,80},{112,96},{0,112},{1... | collective-permute-start | bytes 786440 | tf_op jit(solution)/shard_map/ppermute | solution.py:368
  134.4 1.4 collective-permute-start.1
  136.5 3.6 %collective-permute-start.2 = (f32[8,128]{1,0:T(8,128)S(1)}, f32[8,128]{1,0:T(8,128)S(1)}, u32[]{:S(2)}, u32[]{:S(2)}) collective-permute-start(f32[8,128]{1,0:T(8,128)S(1)} %add.86), channel_id=1, source_target_pairs={{0,32},{16,48},{32,0},{48,16},{64,96},{80,112},{96,64},{112,80},{1... | collective-permute-start | bytes 12296 | tf_op jit(solution)/shard_map/ppermute | solution.py:373
  140.1 5.1 %collective-permute-start.3 = (f32[8,128]{1,0:T(8,128)S(1)}, f32[8,128]{1,0:T(8,128)S(1)}, u32[]{:S(2)}, u32[]{:S(2)}) collective-permute-start(f32[8,128]{1,0:T(8,128)S(1)} %add.87), channel_id=1, source_target_pairs={{0,64},{16,80},{32,96},{48,112},{64,0},{80,16},{96,32},{112,48},{1... | collective-permute-start | bytes 12296 | tf_op jit(solution)/shard_map/ppermute | solution.py:373
  147.7 0.7 copy-start.1
  148.4 0.7 copy-start.2
  154.3 1.4 collective-permute-start.6
  156.4 3.6 %collective-permute-start.7 = (f32[8,128]{1,0:T(8,128)S(1)}, f32[8,128]{1,0:T(8,128)S(1)}, u32[]{:S(2)}, u32[]{:S(2)}) collective-permute-start(f32[8,128]{1,0:T(8,128)S(1)} %add.90), channel_id=1, source_target_pairs={{0,32},{16,48},{32,0},{48,16},{64,96},{80,112},{96,64},{112,80},{1... | collective-permute-start | bytes 12296 | tf_op jit(solution)/shard_map/ppermute | solution.py:373
  160.0 24.8 %collective-permute-start.8 = (f32[8,128]{1,0:T(8,128)S(1)}, f32[8,128]{1,0:T(8,128)S(1)}, u32[]{:S(2)}, u32[]{:S(2)}) collective-permute-start(f32[8,128]{1,0:T(8,128)S(1)} %add.91), channel_id=1, source_target_pairs={{0,64},{16,80},{32,96},{48,112},{64,0},{80,16},{96,32},{112,48},{1... | collective-permute-start | bytes 12296 | tf_op jit(solution)/shard_map/ppermute | solution.py:373

commit v4 on v3

--- a/solution.py
+++ b/solution.py
@@ -15,7 +15,9 @@
 ROWS = 16
 SLABS = 16
 LANES = 128
-GROUP = 4
+GROUP = 8
+PARTS = 4
+EXTRA_COST = 6 * 10**9
 FIELD = (SLABS, 2, N // SLABS, ROWS, LANES)
 
 
@@ -127,7 +129,7 @@
     )(base, shift, basis_x, lines)
 
 
-def backward_kernel(field, extra, basis_y, basis_z, out, left, right):
+def backward_kernel(scale, field, extra, basis_y, basis_z, out, left, right):
     step = pl.program_id(0)
 
     @pl.when(step == 0)
@@ -138,7 +140,7 @@
     def total(x, slab, half):
         at = pl.ds((step * GROUP + x) % 8, ROWS, stride=8)
         terms = [ref.at[slab, half].reshape(ROWS * 8, LANES)[at, :] for ref in (field, extra)]
-        return terms[0] + terms[1]
+        return terms[0] + scale[0] * terms[1]
 
     parts = []
     for x in range(GROUP):
@@ -151,12 +153,12 @@
     out[...] = dot3(split(part), right).reshape(GROUP, N, N)
 
 
-def backward(field, extra, basis_y, basis_z):
+def backward(scale, field, extra, basis_y, basis_z):
     block = pl.BlockSpec((SLABS, 2, ROWS, 8, LANES), lambda x: (0, 0, 0, x * GROUP // 8, 0))
     return pl.pallas_call(
         backward_kernel,
         grid=(ROWS // GROUP,),
-        in_specs=[block, block, whole((N, N)), whole((N, N))],
+        in_specs=[smem(), block, block, whole((N, N)), whole((N, N))],
         out_specs=pl.BlockSpec((GROUP, N, N), lambda x: (x, 0, 0)),
         out_shape=jax.ShapeDtypeStruct((ROWS, N, N), F32),
         scratch_shapes=[pltpu.VMEM((2, N, N), BF16), pltpu.VMEM((2, N, N), BF16)],
@@ -165,7 +167,7 @@
             flops=12 * ROWS * N**3, bytes_accessed=12 * ROWS * N * N, transcendentals=0
         ),
         name="backward",
-    )(field, extra, basis_y, basis_z)
+    )(scale, field, extra, basis_y, basis_z)
 
 
 def inverse_parts(denom):
@@ -222,13 +224,13 @@
     )(base, shift, own_x, ends, products, part0, part1)
 
 
-def extra_kernel(base, shift, scale, own_x, ends, own, before, out):
-    block = pl.program_id(0)
-    alpha = scale[0]
+def extra_kernel(part, base, shift, own_x, ends, own, before, *refs):
+    out = refs[-1]
+    block = part * (SLABS // PARTS) + pl.program_id(0)
     first, last = ends[0:1], ends[1:2]
     for jj in range(ROWS):
-        upper = own_x[...] * (alpha * own[jj : jj + 1])
-        lower = own_x[...] * (alpha * before[jj : jj + 1])
+        upper = own_x[...] * own[jj : jj + 1]
+        lower = own_x[...] * before[jj : jj + 1]
         rows = jnp.concatenate([upper, lower], axis=0)
         result = times_inverse(rows, base[...] + shift[block * ROWS + jj])
         result = first * result[16:] - last * result[:16]
@@ -236,27 +238,29 @@
             out[0, half, jj] = result[:, LANES * half : LANES * half + LANES]
 
 
-def extra(base, shift, scale, own_x, ends, own, before):
-    return pl.pallas_call(
-        extra_kernel,
-        grid=(N // ROWS,),
+def extra(part, base, shift, own_x, ends, own, before, filled=()):
+    skip = part * (SLABS // PARTS)
+    return pl.pallas_call(
+        functools.partial(extra_kernel, part),
+        grid=(SLABS // PARTS,),
         in_specs=[
             whole((N, N)),
             smem(),
-            smem(),
             whole((ROWS, N)),
             whole((2, N)),
-            pl.BlockSpec((ROWS, N), lambda j: (j, 0)),
-            pl.BlockSpec((ROWS, N), lambda j: (j, 0)),
-        ],
-        out_specs=pl.BlockSpec((1, 2, ROWS, ROWS, LANES), lambda j: (j, 0, 0, 0, 0)),
+            pl.BlockSpec((ROWS, N), lambda j: (skip + j, 0)),
+            pl.BlockSpec((ROWS, N), lambda j: (skip + j, 0)),
+        ]
+        + [pl.BlockSpec(memory_space=pl.ANY)] * len(filled),
+        out_specs=pl.BlockSpec((1, 2, ROWS, ROWS, LANES), lambda j: (skip + j, 0, 0, 0, 0)),
         out_shape=jax.ShapeDtypeStruct(FIELD, F32),
-        compiler_params=params(),
-        cost_estimate=pl.CostEstimate(
-            flops=N**3, bytes_accessed=N * N, transcendentals=0
-        ),
-        name="extra",
-    )(base, shift, scale, own_x, ends, own, before)
+        input_output_aliases={6: 0} if filled else {},
+        compiler_params=params(),
+        cost_estimate=pl.CostEstimate(
+            flops=EXTRA_COST, bytes_accessed=4 * ROWS * N * N // PARTS, transcendentals=0
+        ),
+        name=f"extra{part}",
+    )(base, shift, own_x, ends, own, before, *filled)
 
 
 def exact(a, b):
@@ -368,10 +372,8 @@
     return lax.ppermute(block, axis, route)
 
 
-def sum_over_subs(sums):
-    for bit in (1, 2, 4):
-        sums = sums + lax.ppermute(sums, "sub", [(i, i ^ bit) for i in range(8)])
-    return sums
+def with_partner(sums, bit):
+    return sums + lax.ppermute(sums, "sub", [(i, i ^ bit) for i in range(8)])
 
 
 def step_length(sums):
@@ -410,28 +412,41 @@
     part0 = forward(source, coarse, 0, basis_y, basis_z)
     pieces = faces(base_zx, shift, own_x, ends, products, part0, part1)
     following = from_behind(pieces[:, 2:4], "sub", -1)
-    pieces, following, lines = lax.optimization_barrier((pieces, following, lines))
+    pieces, following, lines, gram_x, gram_y = lax.optimization_barrier(
+        (pieces, following, lines, gram_x, gram_y)
+    )
+    spread = middle(base_xz, own_shift, basis_x, lines)
     shares = exchange(pieces[:, 0:2] - following)
+    shares, spread = lax.optimization_barrier((shares, spread))
     own_jumps = jnp.sum(shares, axis=0)
     jumps = exchange(jnp.broadcast_to(own_jumps[None], (SLABS,) + own_jumps.shape))
 
-    spread = middle(base_xz, own_shift, basis_x, lines)
     spread, jumps = lax.optimization_barrier((spread, jumps))
     spread = exchange(spread)
 
     search0, image0, sums0 = chain0(weight.reshape(1), jumps, gram_x, gram_y, face_stiff)
     before = from_behind(image0, "sub", 1)
     after = from_behind(image0, "sub", -1)
-    alpha0 = step_length(sum_over_subs(sums0))
+
+    terms = functools.partial(extra, base=base_xz, shift=shift, own_x=own_x, ends=ends)
+    more = terms(0, own=image0, before=before)
+    sums0, more = lax.optimization_barrier((with_partner(sums0, 1), more))
+    more = terms(1, own=image0, before=before, filled=(more,))
+    sums0, more = lax.optimization_barrier((with_partner(sums0, 2), more))
+    alpha0 = step_length(with_partner(sums0, 4))
 
     scale = jnp.stack([alpha0, own_rho / next_rho, weight])
-    more = extra(base_xz, shift, scale, own_x, ends, image0, before)
     search1, sums1, jump = chain1(
         scale, jumps, image0, before, after, pieces, gram_x, gram_y, face_stiff, own_x, basis_y
     )
-    alpha1 = step_length(sum_over_subs(sums1))
+    sums1, more = lax.optimization_barrier((sums1, more))
+    more = terms(2, own=image0, before=before, filled=(more,))
+    sums1, more = lax.optimization_barrier((with_partner(sums1, 1), more))
+    more = terms(3, own=image0, before=before, filled=(more,))
+    sums1, more = lax.optimization_barrier((with_partner(sums1, 2), more))
+    alpha1 = step_length(with_partner(sums1, 4))
     multipliers = final(jnp.stack([alpha0, alpha1]), search0, search1, own_x, basis_y)
-    solution = backward(spread, more, basis_y, basis_z)
+    solution = backward(scale, spread, more, basis_y, basis_z)
     return (solution[None], multipliers[None], jump[None])
 
 

time: 204 us -> 202 us (level)
  starting transfers between devices: 23.8 us -> 31 us
  blocking collectives: 20.1 us -> 15.1 us
  waiting for transfers between devices: 29.3 us -> 26.2 us
    all_to_all x3, starting transfers between devices: 17.7 us -> 23.1 us  [exchange(): lax.all_to_all(block, 'slab', split_axis=0, concat_axis=0, tiled=True)]
    ppermute x6, waiting for transfers between devices: 10.7 us -> 5.27 us  [with_partner(): return sums + lax.ppermute(sums, 'sub', [(i, i ^ bit) for i in range(8)])]
    all_to_all x1, blocking collectives: 20.1 us -> 15.1 us  [exchange(): lax.all_to_all(block, 'slab', split_axis=0, concat_axis=0, tiled=True)]
    pallas_call x2 -> x5, Pallas kernels: 34.3 us -> 37.5 us  [the longest x4 28.1 us: extra(): pl.pallas_call(functools.partial(extra_kernel, part), grid=(SLABS // PART...]
    ppermute x6, starting transfers between devices: 4.43 us -> 6.66 us  [with_partner(): return sums + lax.ppermute(sums, 'sub', [(i, i ^ bit) for i in range(8)])]
  transfers between devices with their start and end apart: 12 -> 12, of which waited for: 8 -> 6; matrix products, arithmetic and copies ran while one was open for 6% -> 5% of each run, Pallas kernels for 42% -> 44%
where the time goes in v4:
time: 202 us; the launch traced here: 200 us
  Pallas kernels  107 us (53%)
  starting transfers between devices  31 us (15%)
  waiting for transfers between devices  26.2 us (13%)
  blocking collectives  15.1 us (7%)
  other arithmetic  9.31 us (5%)
  between operations  5.97 us (3%)
  local copies, waits for them, and re-layouts  4.89 us (2%)
    pallas_call x4, Pallas kernels, extra(): pl.pallas_call(functools.partial(extra_kernel, part), grid=(SLABS // PART...  28.1 us
    pallas_call x1, Pallas kernels, faces(): pl.pallas_call(faces_kernel, grid=(N // ROWS,), in_specs=[whole((N, N)),...  27.9 us
    all_to_all x3, starting transfers between devices, exchange(): lax.all_to_all(block, 'slab', split_axis=0, concat_axis=0, tiled=True)  23.1 us
    pallas_call x2, Pallas kernels, forward(): pl.pallas_call(forward_kernel, grid=(ROWS // GROUP,), in_specs=[pl.BlockS...  20.1 us
    all_to_all x1, blocking collectives, exchange(): lax.all_to_all(block, 'slab', split_axis=0, concat_axis=0, tiled=True)  15.1 us
    all_to_all x3, waiting for transfers between devices, exchange(): lax.all_to_all(block, 'slab', split_axis=0, concat_axis=0, tiled=True)  13.3 us
    pallas_call x1, Pallas kernels, backward(): pl.pallas_call(backward_kernel, grid=(ROWS // GROUP,), in_specs=[smem(),...  9.39 us
    ppermute x3, waiting for transfers between devices, from_behind(): return lax.ppermute(block, axis, route)  7.69 us
  transfers between devices with their start and end apart: 12, of which 6 were waited for; matrix products, arithmetic and copies ran while one was open for 5% of the time, Pallas kernels for 44%

profile of v4, /device:TPU:6, one launch (start us, length us, event | category | flops | bytes accessed | tf_op | source)
XLA Modules:
  0.0 200.0 jit_solution(16836739123098519823)
XLA Ops:
  0.6 10.1 %forward.3.part1 = f32[16,2,16,16,128]{4,3,2,1,0:T(8,128)} custom-call(f32[16,256,256]{2,1,0:T(8,128)} %bitcast.10, f32[2,1,16,256,256]{4,3,2,1,0:T(8,128)} %coarse.3, f32[256,256]{1,0:T(8,128)} %basis_y.11, f32[256,256]{1,0:T(8,128)} %basis_z.5), custom_call_target="tpu_custom_call" | custom-call | flops 3221225472 | bytes 12582912 | tf_op jit(solution)/shard_map/forward/pallas_call | solution.py:75
  10.8 0.0 copy-start.3
  10.8 8.2 %all-to-all-start = ((f32[16,2,16,16,128]{4,3,2,1,0:T(8,128)}), f32[16,2,16,16,128]{4,3,2,1,0:T(8,128)}, u32[]{:S(2)}, u32[]{:S(2)}) async-start(f32[16,2,16,16,128]{4,3,2,1,0:T(8,128)} %forward.3.part1), calls=%async_computation | async-start | bytes 8388608 | tf_op jit(solution)/shard_map/all_to_all | solution.py:384
  19.1 0.6 fusion.2
  19.7 0.7 slice_multiply_fusion.1
  20.4 0.6 pad_maximum_fusion.ends
  21.0 1.3 select_maximum_fusion
  22.3 1.2 broadcast_multiply_fusion.shift
  23.5 1.5 add_multiply_fusion
  25.1 10.0 %forward.2.part0 = f32[16,2,16,16,128]{4,3,2,1,0:T(8,128)} custom-call(f32[16,256,256]{2,1,0:T(8,128)} %bitcast.11, f32[2,1,16,256,256]{4,3,2,1,0:T(8,128)} %coarse.3, f32[256,256]{1,0:T(8,128)} %basis_y.11, f32[256,256]{1,0:T(8,128)} %basis_z.5), custom_call_target="tpu_custom_call" | custom-call | flops 3221225472 | bytes 12582912 | tf_op jit(solution)/shard_map/forward/pallas_call | solution.py:75
  35.1 27.9 %faces.1.pieces = f32[16,7,16,256]{3,2,1,0:T(8,128)} custom-call(f32[256,256]{1,0:T(8,128)} %get-tuple-element.67.base, f32[256]{0:T(256)} %broadcast_multiply_fusion.shift, f32[16,256]{1,0:T(8,128)} %get-tuple-element.71.own_x, f32[2,256]{1,0:T(2,128)} %pad_maximum_fusion.ends, f32[16,256]{1,0:T(8,128)} %get-tuple-element.70.products, ...), custom_call_target="tpu_custom_call" | custom-call | flops 16777216 | bytes 65536 | tf_op jit(solution)/shard_map/faces/pallas_call | solution.py:205
  63.0 1.1 slice.32
  64.1 0.0 collective-permute-start
  64.1 2.6 %grams.1 = (f32[256,256]{1,0:T(8,128)}, f32[256,256]{1,0:T(8,128)}) custom-call(f32[256,256]{1,0:T(8,128)} %basis_x.3, f32[256,256]{1,0:T(8,128)} %basis_y.11), custom_call_target="tpu_custom_call" | custom-call | tf_op jit(solution)/shard_map/grams/pallas_call | solution.py:364
  66.7 4.1 %collective-permute-done = f32[16,2,16,256]{3,2,1,0:T(8,128)S(1)} collective-permute-done((f32[16,2,16,256]{3,2,1,0:T(8,128)S(1)}, f32[16,2,16,256]{3,2,1,0:T(8,128)S(1)}, u32[]{:S(2)}, u32[]{:S(2)}) %collective-permute-start) | collective-permute-done | bytes 524320 | tf_op jit(solution)/shard_map/ppermute | solution.py:372
  70.8 11.2 %all-to-all-done.lines = f32[16,2,16,16,128]{4,3,2,1,0:T(8,128)} async-done(((f32[16,2,16,16,128]{4,3,2,1,0:T(8,128)}), f32[16,2,16,16,128]{4,3,2,1,0:T(8,128)}, u32[]{:S(2)}, u32[]{:S(2)}) %all-to-all-start) | async-done | bytes 4194336 | tf_op jit(solution)/shard_map/all_to_all | solution.py:384
  82.0 1.9 slice_subtract_fusion
  83.9 10.2 %all-to-all-start.1 = ((f32[16,2,16,256]{3,2,1,0:T(8,128)}), f32[16,2,16,256]{3,2,1,0:T(8,128)S(1)}, u32[]{:S(2)}, u32[]{:S(2)}) async-start(f32[16,2,16,256]{3,2,1,0:T(8,128)} %slice_subtract_fusion), calls=%async_computation.1 | async-start | bytes 1048576 | tf_op jit(solution)/shard_map/all_to_all | solution.py:384
  94.1 0.6 dynamic_slice.15.shift
  94.7 7.4 %middle.1 = f32[16,2,16,16,128]{4,3,2,1,0:T(8,128)} custom-call(f32[256,256]{1,0:T(8,128)} %get-tuple-element.66.base, f32[16]{0:T(128)} %dynamic_slice.15.shift, f32[256,256]{1,0:T(8,128)} %basis_x.3, f32[16,2,16,16,128]{4,3,2,1,0:T(8,128)} %all-to-all-done.lines), custom_call_target="tpu_custom_call" | custom-call | flops 3221225472 | bytes 8388608 | tf_op jit(solution)/shard_map/middle/pallas_call | solution.py:117
  102.1 2.1 %all-to-all-done.1 = f32[16,2,16,256]{3,2,1,0:T(8,128)S(1)} async-done(((f32[16,2,16,256]{3,2,1,0:T(8,128)}), f32[16,2,16,256]{3,2,1,0:T(8,128)S(1)}, u32[]{:S(2)}, u32[]{:S(2)}) %all-to-all-start.1) | async-done | bytes 524320 | tf_op jit(solution)/shard_map/all_to_all | solution.py:384
  104.2 0.1 broadcast_in_dim.8
  104.2 15.1 %all_to_all.20.jumps = f32[16,2,16,256]{3,2,1,0:T(8,128)} all-to-all(f32[16,2,16,256]{3,2,1,0:T(8,128)S(1)} %broadcast_in_dim.8), channel_id=1, replica_groups=mesh['sub'=8,'slab'=16] {'slab'}, dimensions={0} | all-to-all | bytes 1048576 | tf_op jit(solution)/shard_map/all_to_all | solution.py:384
  119.4 4.7 %all-to-all-start.3 = ((f32[16,2,16,16,128]{4,3,2,1,0:T(8,128)}), f32[16,2,16,16,128]{4,3,2,1,0:T(8,128)}, u32[]{:S(2)}, u32[]{:S(2)}) async-start(f32[16,2,16,16,128]{4,3,2,1,0:T(8,128)} %middle.1), calls=%async_computation.3 | async-start | bytes 8388608 | tf_op jit(solution)/shard_map/all_to_all | solution.py:384
  125.4 4.0 %chain0.1 = (f32[256,256]{1,0:T(8,128)}, f32[256,256]{1,0:T(8,128)}, f32[8,128]{1,0:T(8,128)}) custom-call(f32[1]{0:T(128)} %bitcast.2.scale, f32[16,2,16,256]{3,2,1,0:T(8,128)} %all_to_all.20.jumps, f32[256,256]{1,0:T(8,128)} %get-tuple-element.38.gram_x, f32[256,256]{1,0:T(8,128)} %get-tuple-element.39.gram_y, f32[256,256]{1,0:T(8,128)} %stiff.3), custom_call_target="tpu_custom_call" | custom-call | flops 16777216 | bytes 65536 | tf_op jit(solution)/shard_map/chain0/pallas_call | solution.py:296
  129.4 0.5 collective-permute-start.1
  129.9 1.2 collective-permute-start.5
  131.1 0.7 add.86
  131.8 3.6 %collective-permute-done.2.before = f32[256,256]{1,0:T(8,128)S(1)} collective-permute-done((f32[256,256]{1,0:T(8,128)}, f32[256,256]{1,0:T(8,128)S(1)}, u32[]{:S(2)}, u32[]{:S(2)}) %collective-permute-start.2) | collective-permute-done | bytes 262176 | tf_op jit(solution)/shard_map/ppermute | solution.py:372
  135.4 0.7 copy-done
  136.1 7.0 %extra0.1.refs_0_ = f32[16,2,16,16,128]{4,3,2,1,0:T(8,128)} custom-call(f32[256,256]{1,0:T(8,128)} %get-tuple-element.66.base, f32[256]{0:T(256)} %broadcast_multiply_fusion.shift, f32[16,256]{1,0:T(8,128)} %get-tuple-element.71.own_x, f32[2,256]{1,0:T(2,128)} %pad_maximum_fusion.ends, f32[256,256]{1,0:T(8,128)} %get-tuple-element.41.own.image, ...), custom_call_target="tpu_custom_call" | custom-call | flops 6000000000 | bytes 1048576 | tf_op jit(solution)/shard_map/extra0/pallas_call | solution.py:243
  143.1 0.8 collective-permute-start.3
  143.9 7.0 %extra1.1.refs_0_ = f32[16,2,16,16,128]{4,3,2,1,0:T(8,128)} custom-call(f32[256,256]{1,0:T(8,128)} %get-tuple-element.66.base, f32[256]{0:T(256)} %broadcast_multiply_fusion.shift, f32[16,256]{1,0:T(8,128)} %get-tuple-element.71.own_x, f32[2,256]{1,0:T(2,128)} %pad_maximum_fusion.ends, ...), custom_call_target="tpu_custom_call", output_to_operand_aliasing={{}: (6, {})} | custom-call | flops 6000000000 | bytes 1048576 | tf_op jit(solution)/shard_map/extra1/pallas_call | solution.py:243
  150.9 2.4 %collective-permute-start.4 = (f32[8,128]{1,0:T(8,128)S(1)}, f32[8,128]{1,0:T(8,128)S(1)}, u32[]{:S(2)}, u32[]{:S(2)}) collective-permute-start(f32[8,128]{1,0:T(8,128)S(1)} %add.87), channel_id=1, source_target_pairs={{0,64},{16,80},{32,96},{48,112},{64,0},{80,16},{96,32},{112,48},{1... | collective-permute-start | bytes 12296 | tf_op jit(solution)/shard_map/ppermute | solution.py:376
  154.6 1.5 collective-permute-done.4
  156.1 0.5 fusion.1
  157.9 0.6 pad_maximum_fusion.1.scale
  158.5 0.7 copy-done.1
  159.2 5.2 %chain1.1 = (f32[256,256]{1,0:T(8,128)}, f32[8,128]{1,0:T(8,128)}, f32[16,256]{1,0:T(8,128)}) custom-call(f32[3]{0:T(128)} %pad_maximum_fusion.1.scale, f32[16,2,16,256]{3,2,1,0:T(8,128)} %all_to_all.20.jumps, f32[256,256]{1,0:T(8,128)} %get-tuple-element.41.own.image, f32[256,256]{1,0:T(8,128)} %copy-done, f32[256,256]{1,0:T(8,128)} %copy-done.1, ...), custom_call_target="tpu_custom_call" | custom-call | flops 16777216 | bytes 65536 | tf_op jit(solution)/shard_map/chain1/pallas_call | solution.py:325
  164.4 7.0 %extra2.1.refs_0_ = f32[16,2,16,16,128]{4,3,2,1,0:T(8,128)} custom-call(f32[256,256]{1,0:T(8,128)} %get-tuple-element.66.base, f32[256]{0:T(256)} %broadcast_multiply_fusion.shift, f32[16,256]{1,0:T(8,128)} %get-tuple-element.71.own_x, f32[2,256]{1,0:T(2,128)} %pad_maximum_fusion.ends, ...), custom_call_target="tpu_custom_call", output_to_operand_aliasing={{}: (6, {})} | custom-call | flops 6000000000 | bytes 1048576 | tf_op jit(solution)/shard_map/extra2/pallas_call | solution.py:243
  171.5 1.3 collective-permute-start.7
  172.8 7.1 %extra3.1.extra = f32[16,2,16,16,128]{4,3,2,1,0:T(8,128)} custom-call(f32[256,256]{1,0:T(8,128)} %get-tuple-element.66.base, f32[256]{0:T(256)} %broadcast_multiply_fusion.shift, f32[16,256]{1,0:T(8,128)} %get-tuple-element.71.own_x, f32[2,256]{1,0:T(2,128)} %pad_maximum_fusion.ends, ...), custom_call_target="tpu_custom_call", output_to_operand_aliasing={{}: (6, {})} | custom-call | flops 6000000000 | bytes 1048576 | tf_op jit(solution)/shard_map/extra3/pallas_call | solution.py:243
  179.9 1.6 collective-permute-start.8
  181.5 3.8 %collective-permute-done.8 = f32[8,128]{1,0:T(8,128)S(1)} collective-permute-done((f32[8,128]{1,0:T(8,128)S(1)}, f32[8,128]{1,0:T(8,128)S(1)}, u32[]{:S(2)}, u32[]{:S(2)}) %collective-permute-start.8) | collective-permute-done | bytes 4128 | tf_op jit(solution)/shard_map/ppermute | solution.py:376
  185.3 0.6 fusion
  187.2 0.7 pad_maximum_fusion.2.scale
  187.9 2.7 %final.1 = f32[16,256]{1,0:T(8,128)} custom-call(f32[2]{0:T(128)} %pad_maximum_fusion.2.scale, f32[256,256]{1,0:T(8,128)} %get-tuple-element.54.search0, f32[256,256]{1,0:T(8,128)} %get-tuple-element.55.search1, f32[16,256]{1,0:T(8,128)} %get-tuple-element.71.own_x, f32[256,256]{1,0:T(8,128)} %basis_y.11), custom_call_target="tpu_custom_call" | custom-call | flops 16777216 | bytes 65536 | tf_op jit(solution)/shard_map/final/pallas_call | solution.py:347
  190.6 9.4 %backward.1 = f32[16,256,256]{2,1,0:T(8,128)} custom-call(f32[3]{0:T(128)} %pad_maximum_fusion.1.scale, f32[16,2,16,16,128]{4,3,2,1,0:T(8,128)} %all-to-all-done.3.field, f32[16,2,16,16,128]{4,3,2,1,0:T(8,128)} %extra3.1.extra, f32[256,256]{1,0:T(8,128)} %basis_y.11, f32[256,256]{1,0:T(8,128)} %basis_z.5), custom_call_target="tpu_custom_call" | custom-call | flops 3221225472 | bytes 12582912 | tf_op jit(solution)/shard_map/backward/pallas_call | solution.py:158
  (27 shorter events, 0.1 us)
Async XLA Ops:
  10.8 8.3 %copy-start.6 = (f32[8]{0:T(128)S(1)}, f32[8]{0:T(128)}, u32[]{:S(2)}) copy-start(f32[8]{0:T(128)} %param.12) | copy-start | bytes 100
  10.8 11.6 %copy-start.7 = (f32[256]{0:T(256)S(1)}, f32[256]{0:T(256)}, u32[]{:S(2)}) copy-start(f32[256]{0:T(256)} %param.17) | copy-start | bytes 3076
  10.8 12.7 %copy-start.2 = (f32[256]{0:T(256)S(1)}, f32[256]{0:T(256)}, u32[]{:S(2)}) copy-start(f32[256]{0:T(256)} %param.18) | copy-start | bytes 3076
  10.8 12.7 %copy-start.3 = (f32[256]{0:T(256)S(1)}, f32[256]{0:T(256)}, u32[]{:S(2)}) copy-start(f32[256]{0:T(256)} %param.16) | copy-start | bytes 3076
  10.8 71.2 %all-to-all-start = ((f32[16,2,16,16,128]{4,3,2,1,0:T(8,128)}), f32[16,2,16,16,128]{4,3,2,1,0:T(8,128)}, u32[]{:S(2)}, u32[]{:S(2)}) async-start(f32[16,2,16,16,128]{4,3,2,1,0:T(8,128)} %forward.3.part1), calls=%async_computation | async-start | bytes 8388608 | tf_op jit(solution)/shard_map/all_to_all | solution.py:384
  63.0 31.1 %copy-start.4 = (f32[256]{0:T(256)S(1)}, f32[256]{0:T(256)}, u32[]{:S(2)}) copy-start(f32[256]{0:T(256)} %broadcast_multiply_fusion.shift) | copy-start | bytes 3076
  64.1 6.7 %collective-permute-start = (f32[16,2,16,256]{3,2,1,0:T(8,128)S(1)}, f32[16,2,16,256]{3,2,1,0:T(8,128)S(1)}, u32[]{:S(2)}, u32[]{:S(2)}) collective-permute-start(f32[16,2,16,256]{3,2,1,0:T(8,128)S(1)} %slice.32), channel_id=1, source_target_pairs={{16,0},{32,16},{48,32},{64,48},{80,64},{96,80},{112,96},{0,112},{1... | collective-permute-start | bytes 1572872 | tf_op jit(solution)/shard_map/ppermute | solution.py:372
  83.9 20.3 %all-to-all-start.1 = ((f32[16,2,16,256]{3,2,1,0:T(8,128)}), f32[16,2,16,256]{3,2,1,0:T(8,128)S(1)}, u32[]{:S(2)}, u32[]{:S(2)}) async-start(f32[16,2,16,256]{3,2,1,0:T(8,128)} %slice_subtract_fusion), calls=%async_computation.1 | async-start | bytes 1048576 | tf_op jit(solution)/shard_map/all_to_all | solution.py:384
  119.4 71.3 %all-to-all-start.3 = ((f32[16,2,16,16,128]{4,3,2,1,0:T(8,128)}), f32[16,2,16,16,128]{4,3,2,1,0:T(8,128)}, u32[]{:S(2)}, u32[]{:S(2)}) async-start(f32[16,2,16,16,128]{4,3,2,1,0:T(8,128)} %middle.1), calls=%async_computation.3 | async-start | bytes 8388608 | tf_op jit(solution)/shard_map/all_to_all | solution.py:384
  129.4 6.0 %collective-permute-start.2 = (f32[256,256]{1,0:T(8,128)}, f32[256,256]{1,0:T(8,128)S(1)}, u32[]{:S(2)}, u32[]{:S(2)}) collective-permute-start(f32[256,256]{1,0:T(8,128)} %get-tuple-element.41.own.image), channel_id=1, source_target_pairs={{112,0},{0,16},{16,32},{32,48},{48,64},{64,80},{80,96},{96,112},{1... | collective-permute-start | bytes 786440 | tf_op jit(solution)/shard_map/ppermute | solution.py:372
  129.4 1.7 collective-permute-start.1
  129.9 28.6 %collective-permute-start.5 = (f32[256,256]{1,0:T(8,128)}, f32[256,256]{1,0:T(8,128)S(1)}, u32[]{:S(2)}, u32[]{:S(2)}) collective-permute-start(f32[256,256]{1,0:T(8,128)} %get-tuple-element.41.own.image), channel_id=1, source_target_pairs={{16,0},{32,16},{48,32},{64,48},{80,64},{96,80},{112,96},{0,112},{1... | collective-permute-start | bytes 786440 | tf_op jit(solution)/shard_map/ppermute | solution.py:372
  135.4 0.7 copy-start
  143.1 7.8 %collective-permute-start.3 = (f32[8,128]{1,0:T(8,128)S(1)}, f32[8,128]{1,0:T(8,128)S(1)}, u32[]{:S(2)}, u32[]{:S(2)}) collective-permute-start(f32[8,128]{1,0:T(8,128)S(1)} %add.86), channel_id=1, source_target_pairs={{0,32},{16,48},{32,0},{48,16},{64,96},{80,112},{96,64},{112,80},{1... | collective-permute-start | bytes 12296 | tf_op jit(solution)/shard_map/ppermute | solution.py:376
  150.9 5.2 %collective-permute-start.4 = (f32[8,128]{1,0:T(8,128)S(1)}, f32[8,128]{1,0:T(8,128)S(1)}, u32[]{:S(2)}, u32[]{:S(2)}) collective-permute-start(f32[8,128]{1,0:T(8,128)S(1)} %add.87), channel_id=1, source_target_pairs={{0,64},{16,80},{32,96},{48,112},{64,0},{80,16},{96,32},{112,48},{1... | collective-permute-start | bytes 12296 | tf_op jit(solution)/shard_map/ppermute | solution.py:376
  158.5 0.7 copy-start.1
  164.4 7.1 %copy-start.5 = (f32[8,128]{1,0:T(8,128)S(1)}, f32[8,128]{1,0:T(8,128)}, u32[]{:S(2)}) copy-start(f32[8,128]{1,0:T(8,128)} %get-tuple-element.48) | copy-start | bytes 12292
  164.4 7.0 %collective-permute-start.6 = (f32[8,128]{1,0:T(8,128)}, f32[8,128]{1,0:T(8,128)S(1)}, u32[]{:S(2)}, u32[]{:S(2)}) collective-permute-start(f32[8,128]{1,0:T(8,128)} %get-tuple-element.48), channel_id=1, source_target_pairs={{0,16},{16,0},{32,48},{48,32},{64,80},{80,64},{96,112},{112,96},{1... | collective-permute-start | bytes 12296 | tf_op jit(solution)/shard_map/ppermute | solution.py:376
  171.5 8.4 %collective-permute-start.7 = (f32[8,128]{1,0:T(8,128)S(1)}, f32[8,128]{1,0:T(8,128)S(1)}, u32[]{:S(2)}, u32[]{:S(2)}) collective-permute-start(f32[8,128]{1,0:T(8,128)S(1)} %add.90), channel_id=1, source_target_pairs={{0,32},{16,48},{32,0},{48,16},{64,96},{80,112},{96,64},{112,80},{1... | collective-permute-start | bytes 12296 | tf_op jit(solution)/shard_map/ppermute | solution.py:376
  179.9 5.4 %collective-permute-start.8 = (f32[8,128]{1,0:T(8,128)S(1)}, f32[8,128]{1,0:T(8,128)S(1)}, u32[]{:S(2)}, u32[]{:S(2)}) collective-permute-start(f32[8,128]{1,0:T(8,128)S(1)} %add.91), channel_id=1, source_target_pairs={{0,64},{16,80},{32,96},{48,112},{64,0},{80,16},{96,32},{112,48},{1... | collective-permute-start | bytes 12296 | tf_op jit(solution)/shard_map/ppermute | solution.py:376

commit v5 on v4

--- a/solution.py
+++ b/solution.py
@@ -16,8 +16,8 @@
 SLABS = 16
 LANES = 128
 GROUP = 8
-PARTS = 4
-EXTRA_COST = 6 * 10**9
+PARTS = ((0, 6), (6, 11), (11, 16))
+BLOCK_COST = 15 * 10**8
 FIELD = (SLABS, 2, N // SLABS, ROWS, LANES)
 
 
@@ -226,7 +226,7 @@
 
 def extra_kernel(part, base, shift, own_x, ends, own, before, *refs):
     out = refs[-1]
-    block = part * (SLABS // PARTS) + pl.program_id(0)
+    block = PARTS[part][0] + pl.program_id(0)
     first, last = ends[0:1], ends[1:2]
     for jj in range(ROWS):
         upper = own_x[...] * own[jj : jj + 1]
@@ -239,10 +239,10 @@
 
 
 def extra(part, base, shift, own_x, ends, own, before, filled=()):
-    skip = part * (SLABS // PARTS)
+    skip, stop = PARTS[part]
     return pl.pallas_call(
         functools.partial(extra_kernel, part),
-        grid=(SLABS // PARTS,),
+        grid=(stop - skip,),
         in_specs=[
             whole((N, N)),
             smem(),
@@ -257,7 +257,7 @@
         input_output_aliases={6: 0} if filled else {},
         compiler_params=params(),
         cost_estimate=pl.CostEstimate(
-            flops=EXTRA_COST, bytes_accessed=4 * ROWS * N * N // PARTS, transcendentals=0
+            flops=BLOCK_COST * (stop - skip), bytes_accessed=N * N, transcendentals=0
         ),
         name=f"extra{part}",
     )(base, shift, own_x, ends, own, before, *filled)
@@ -284,19 +284,20 @@
     return jnp.where(at == 0, upper, jnp.where(at == 1, lower, 0.0))
 
 
-def chain0_kernel(scale, jumps, gram_x, gram_y, stiff, search, image, sums):
-    search[...], image[...], upper, lower = precondition(
+def chain0_kernel(scale, jumps, gram_x, gram_y, stiff, own_x, basis_y, rows, image, sums):
+    search, image[...], upper, lower = precondition(
         jumps[:, 0].reshape(N, N), gram_x[...], gram_y[...], scale[0] * stiff[...].T
     )
     sums[...] = scalars_block(upper, lower)
+    rows[...] = exact_t(exact_t(own_x[...], search), basis_y[...])
 
 
 def chain0(*args):
     face = jax.ShapeDtypeStruct((N, N), F32)
     return pl.pallas_call(
         chain0_kernel,
-        in_specs=[smem()] + [pl.BlockSpec(memory_space=pltpu.VMEM)] * 4,
-        out_shape=(face, face, jax.ShapeDtypeStruct((8, 128), F32)),
+        in_specs=[smem()] + [pl.BlockSpec(memory_space=pltpu.VMEM)] * 6,
+        out_shape=(jax.ShapeDtypeStruct((ROWS, N), F32), face, jax.ShapeDtypeStruct((8, 128), F32)),
         compiler_params=params(),
         cost_estimate=pl.CostEstimate(
             flops=N**3, bytes_accessed=N * N, transcendentals=0
@@ -306,7 +307,7 @@
 
 
 def chain1_kernel(
-    scale, jumps, image, before, after, pieces, gram_x, gram_y, stiff, own_x, basis_y, search, sums, out
+    scale, jumps, image, before, after, pieces, gram_x, gram_y, stiff, own_x, basis_y, sums, out, rows
 ):
     alpha, ratio, weight = scale[0], scale[1], scale[2]
     t = image[...]
@@ -314,11 +315,12 @@
     own = table[1] * before[...] - table[0] * t
     other = table[2] * t - table[1] * after[...]
     q = jumps[:, 1].reshape(N, N) + alpha * (own - ratio * other)
-    search[...], _, upper, lower = precondition(
+    search, _, upper, lower = precondition(
         q, gram_x[...], gram_y[...], weight * stiff[...].T
     )
     sums[...] = scalars_block(upper, lower)
     out[...] = exact_t(exact_t(own_x[...], q), basis_y[...])
+    rows[...] = exact_t(exact_t(own_x[...], search), basis_y[...])
 
 
 def chain1(*args):
@@ -326,31 +328,15 @@
         chain1_kernel,
         in_specs=[smem()] + [pl.BlockSpec(memory_space=pltpu.VMEM)] * 10,
         out_shape=(
-            jax.ShapeDtypeStruct((N, N), F32),
             jax.ShapeDtypeStruct((8, 128), F32),
             jax.ShapeDtypeStruct((ROWS, N), F32),
+            jax.ShapeDtypeStruct((ROWS, N), F32),
         ),
         compiler_params=params(),
         cost_estimate=pl.CostEstimate(
             flops=N**3, bytes_accessed=N * N, transcendentals=0
         ),
         name="chain1",
-    )(*args)
-
-
-def final_kernel(scale, search0, search1, own_x, basis_y, out):
-    total = scale[0] * search0[...] + scale[1] * search1[...]
-    out[...] = exact_t(exact_t(own_x[...], total), basis_y[...])
-
-
-def final(*args):
-    return pl.pallas_call(
-        final_kernel,
-        in_specs=[smem()] + [pl.BlockSpec(memory_space=pltpu.VMEM)] * 4,
-        out_shape=jax.ShapeDtypeStruct((ROWS, N), F32),
-        compiler_params=params(),
-        cost_estimate=pl.CostEstimate(flops=N**3, bytes_accessed=N * N, transcendentals=0),
-        name="final",
     )(*args)
 
 
@@ -372,8 +358,16 @@
     return lax.ppermute(block, axis, route)
 
 
-def with_partner(sums, bit):
-    return sums + lax.ppermute(sums, "sub", [(i, i ^ bit) for i in range(8)])
+def from_partner(sums, bits):
+    return lax.ppermute(sums, "sub", [(i, i ^ bits) for i in range(8)])
+
+
+def over_pair(sums):
+    return sums + from_partner(sums, 1)
+
+
+def over_pairs(sums):
+    return (sums + from_partner(sums, 2)) + (from_partner(sums, 4) + from_partner(sums, 6))
 
 
 def step_length(sums):
@@ -424,28 +418,30 @@
     spread, jumps = lax.optimization_barrier((spread, jumps))
     spread = exchange(spread)
 
-    search0, image0, sums0 = chain0(weight.reshape(1), jumps, gram_x, gram_y, face_stiff)
+    first, image0, sums0 = chain0(
+        weight.reshape(1), jumps, gram_x, gram_y, face_stiff, own_x, basis_y
+    )
     before = from_behind(image0, "sub", 1)
     after = from_behind(image0, "sub", -1)
 
     terms = functools.partial(extra, base=base_xz, shift=shift, own_x=own_x, ends=ends)
+    sums0 = over_pair(sums0)
+    before, sums0 = lax.optimization_barrier((before, sums0))
     more = terms(0, own=image0, before=before)
-    sums0, more = lax.optimization_barrier((with_partner(sums0, 1), more))
+    sums0, more = lax.optimization_barrier((over_pairs(sums0), more))
+    alpha0 = step_length(sums0)
+
+    scale = jnp.stack([alpha0, own_rho / next_rho, weight])
+    sums1, jump, change = chain1(
+        scale, jumps, image0, before, after, pieces, gram_x, gram_y, face_stiff, own_x, basis_y
+    )
+    sums1, more = lax.optimization_barrier((sums1, more))
     more = terms(1, own=image0, before=before, filled=(more,))
-    sums0, more = lax.optimization_barrier((with_partner(sums0, 2), more))
-    alpha0 = step_length(with_partner(sums0, 4))
-
-    scale = jnp.stack([alpha0, own_rho / next_rho, weight])
-    search1, sums1, jump = chain1(
-        scale, jumps, image0, before, after, pieces, gram_x, gram_y, face_stiff, own_x, basis_y
-    )
-    sums1, more = lax.optimization_barrier((sums1, more))
+    sums1, more = lax.optimization_barrier((over_pair(sums1), more))
     more = terms(2, own=image0, before=before, filled=(more,))
-    sums1, more = lax.optimization_barrier((with_partner(sums1, 1), more))
-    more = terms(3, own=image0, before=before, filled=(more,))
-    sums1, more = lax.optimization_barrier((with_partner(sums1, 2), more))
-    alpha1 = step_length(with_partner(sums1, 4))
-    multipliers = final(jnp.stack([alpha0, alpha1]), search0, search1, own_x, basis_y)
+    sums1, more = lax.optimization_barrier((over_pairs(sums1), more))
+    alpha1 = step_length(sums1)
+    multipliers = alpha0 * first + alpha1 * change
     solution = backward(scale, spread, more, basis_y, basis_z)
     return (solution[None], multipliers[None], jump[None])
 

time: 202 us -> 195 us (0.965)
  waiting for transfers between devices: 26.2 us -> 19.4 us
  starting transfers between devices: 31 us -> 34.4 us
  Pallas kernels: 107 us -> 104 us
    ppermute x6 -> x8, waiting for transfers between devices: 5.27 us -> 0.02 us  [from_partner(): return lax.ppermute(sums, 'sub', [(i, i ^ bits) for i in range(8)])]
    pallas_call x5 -> x3, Pallas kernels: 30.9 us -> 26.4 us  [extra(): pl.pallas_call(functools.partial(extra_kernel, part), grid=(stop - skip,)...]
    ppermute x6 -> x8, starting transfers between devices: 6.66 us -> 10 us  [from_partner(): return lax.ppermute(sums, 'sub', [(i, i ^ bits) for i in range(8)])]
  transfers between devices with their start and end apart: 12 -> 14, of which waited for: 6 -> 4; matrix products, arithmetic and copies ran while one was open for 5% -> 6% of each run, Pallas kernels for 44% -> 44%
where the time goes in v5:
time: 195 us; the launch traced here: 192 us
  Pallas kernels  104 us (53%)
  starting transfers between devices  34.4 us (18%)
  waiting for transfers between devices  19.4 us (10%)
  blocking collectives  15.1 us (8%)
  other arithmetic  9.4 us (5%)
  between operations  6.03 us (3%)
  local copies, waits for them, and re-layouts  4.28 us (2%)
    pallas_call x1, Pallas kernels, faces(): pl.pallas_call(faces_kernel, grid=(N // ROWS,), in_specs=[whole((N, N)),...  27.9 us
    pallas_call x3, Pallas kernels, extra(): pl.pallas_call(functools.partial(extra_kernel, part), grid=(stop - skip,)...  26.4 us
    all_to_all x3, starting transfers between devices, exchange(): lax.all_to_all(block, 'slab', split_axis=0, concat_axis=0, tiled=True)  23.1 us
    pallas_call x2, Pallas kernels, forward(): pl.pallas_call(forward_kernel, grid=(ROWS // GROUP,), in_specs=[pl.BlockS...  20.1 us
    all_to_all x1, blocking collectives, exchange(): lax.all_to_all(block, 'slab', split_axis=0, concat_axis=0, tiled=True)  15.1 us
    all_to_all x3, waiting for transfers between devices, exchange(): lax.all_to_all(block, 'slab', split_axis=0, concat_axis=0, tiled=True)  13.1 us
    ppermute x8, starting transfers between devices, from_partner(): return lax.ppermute(sums, 'sub', [(i, i ^ bits) for i in range(8)])  10 us
    pallas_call x1, Pallas kernels, backward(): pl.pallas_call(backward_kernel, grid=(ROWS // GROUP,), in_specs=[smem(),...  9.36 us
  transfers between devices with their start and end apart: 14, of which 4 were waited for; matrix products, arithmetic and copies ran while one was open for 6% of the time, Pallas kernels for 44%

profile of v5, /device:TPU:6, one launch (start us, length us, event | category | flops | bytes accessed | tf_op | source)
XLA Modules:
  0.0 192.4 jit_solution(2632289341984495455)
XLA Ops:
  0.6 10.1 %forward.3.part1 = f32[16,2,16,16,128]{4,3,2,1,0:T(8,128)} custom-call(f32[16,256,256]{2,1,0:T(8,128)} %bitcast.12, f32[2,1,16,256,256]{4,3,2,1,0:T(8,128)} %coarse.3, f32[256,256]{1,0:T(8,128)} %basis_y.11, f32[256,256]{1,0:T(8,128)} %basis_z.5), custom_call_target="tpu_custom_call" | custom-call | flops 3221225472 | bytes 12582912 | tf_op jit(solution)/shard_map/forward/pallas_call | solution.py:75
  10.8 0.0 copy-start.5
  10.8 8.2 %all-to-all-start = ((f32[16,2,16,16,128]{4,3,2,1,0:T(8,128)}), f32[16,2,16,16,128]{4,3,2,1,0:T(8,128)}, u32[]{:S(2)}, u32[]{:S(2)}) async-start(f32[16,2,16,16,128]{4,3,2,1,0:T(8,128)} %forward.3.part1), calls=%async_computation | async-start | bytes 8388608 | tf_op jit(solution)/shard_map/all_to_all | solution.py:378
  19.0 0.7 fusion.2
  19.7 0.7 slice_multiply_fusion.1
  20.4 0.6 pad_maximum_fusion.ends
  21.0 1.3 select_maximum_fusion
  22.4 1.2 broadcast_multiply_fusion.shift
  23.6 1.6 add_multiply_fusion
  25.2 10.0 %forward.2.part0 = f32[16,2,16,16,128]{4,3,2,1,0:T(8,128)} custom-call(f32[16,256,256]{2,1,0:T(8,128)} %bitcast.13, f32[2,1,16,256,256]{4,3,2,1,0:T(8,128)} %coarse.3, f32[256,256]{1,0:T(8,128)} %basis_y.11, f32[256,256]{1,0:T(8,128)} %basis_z.5), custom_call_target="tpu_custom_call" | custom-call | flops 3221225472 | bytes 12582912 | tf_op jit(solution)/shard_map/forward/pallas_call | solution.py:75
  35.2 27.9 %faces.1.pieces = f32[16,7,16,256]{3,2,1,0:T(8,128)} custom-call(f32[256,256]{1,0:T(8,128)} %get-tuple-element.67.base, f32[256]{0:T(256)} %broadcast_multiply_fusion.shift, f32[16,256]{1,0:T(8,128)} %get-tuple-element.71.own_x, f32[2,256]{1,0:T(2,128)} %pad_maximum_fusion.ends, f32[16,256]{1,0:T(8,128)} %get-tuple-element.70.products, ...), custom_call_target="tpu_custom_call" | custom-call | flops 16777216 | bytes 65536 | tf_op jit(solution)/shard_map/faces/pallas_call | solution.py:205
  63.2 1.1 slice.32
  64.3 0.0 collective-permute-start
  64.3 2.6 %grams.1 = (f32[256,256]{1,0:T(8,128)}, f32[256,256]{1,0:T(8,128)}) custom-call(f32[256,256]{1,0:T(8,128)} %basis_x.3, f32[256,256]{1,0:T(8,128)} %basis_y.11), custom_call_target="tpu_custom_call" | custom-call | tf_op jit(solution)/shard_map/grams/pallas_call | solution.py:350
  66.9 4.1 %collective-permute-done = f32[16,2,16,256]{3,2,1,0:T(8,128)S(1)} collective-permute-done((f32[16,2,16,256]{3,2,1,0:T(8,128)S(1)}, f32[16,2,16,256]{3,2,1,0:T(8,128)S(1)}, u32[]{:S(2)}, u32[]{:S(2)}) %collective-permute-start) | collective-permute-done | bytes 524320 | tf_op jit(solution)/shard_map/ppermute | solution.py:358
  71.0 11.0 %all-to-all-done.lines = f32[16,2,16,16,128]{4,3,2,1,0:T(8,128)} async-done(((f32[16,2,16,16,128]{4,3,2,1,0:T(8,128)}), f32[16,2,16,16,128]{4,3,2,1,0:T(8,128)}, u32[]{:S(2)}, u32[]{:S(2)}) %all-to-all-start) | async-done | bytes 4194336 | tf_op jit(solution)/shard_map/all_to_all | solution.py:378
  82.0 1.9 %slice_subtract_fusion = f32[16,2,16,256]{3,2,1,0:T(8,128)} fusion(f32[16,2,16,256]{3,2,1,0:T(8,128)S(1)} %collective-permute-done, f32[16,7,16,256]{3,2,1,0:T(8,128)} %faces.1.pieces), kind=kLoop, calls=%fused_computation | loop fusion | flops 131072 | bytes 1572864 | tf_op jit(solution)/shard_map/sub | solution.py:413
  83.9 10.2 %all-to-all-start.1 = ((f32[16,2,16,256]{3,2,1,0:T(8,128)}), f32[16,2,16,256]{3,2,1,0:T(8,128)S(1)}, u32[]{:S(2)}, u32[]{:S(2)}) async-start(f32[16,2,16,256]{3,2,1,0:T(8,128)} %slice_subtract_fusion), calls=%async_computation.1 | async-start | bytes 1048576 | tf_op jit(solution)/shard_map/all_to_all | solution.py:378
  94.1 0.6 dynamic_slice.15.shift
  94.7 7.4 %middle.1 = f32[16,2,16,16,128]{4,3,2,1,0:T(8,128)} custom-call(f32[256,256]{1,0:T(8,128)} %get-tuple-element.66.base, f32[16]{0:T(128)} %dynamic_slice.15.shift, f32[256,256]{1,0:T(8,128)} %basis_x.3, f32[16,2,16,16,128]{4,3,2,1,0:T(8,128)} %all-to-all-done.lines), custom_call_target="tpu_custom_call" | custom-call | flops 3221225472 | bytes 8388608 | tf_op jit(solution)/shard_map/middle/pallas_call | solution.py:117
  102.0 2.1 %all-to-all-done.1 = f32[16,2,16,256]{3,2,1,0:T(8,128)S(1)} async-done(((f32[16,2,16,256]{3,2,1,0:T(8,128)}), f32[16,2,16,256]{3,2,1,0:T(8,128)S(1)}, u32[]{:S(2)}, u32[]{:S(2)}) %all-to-all-start.1) | async-done | bytes 524320 | tf_op jit(solution)/shard_map/all_to_all | solution.py:378
  104.2 0.1 broadcast_in_dim.8
  104.2 15.1 %all_to_all.20.jumps = f32[16,2,16,256]{3,2,1,0:T(8,128)} all-to-all(f32[16,2,16,256]{3,2,1,0:T(8,128)S(1)} %broadcast_in_dim.8), channel_id=1, replica_groups=mesh['sub'=8,'slab'=16] {'slab'}, dimensions={0} | all-to-all | bytes 1048576 | tf_op jit(solution)/shard_map/all_to_all | solution.py:378
  119.4 4.7 %all-to-all-start.3 = ((f32[16,2,16,16,128]{4,3,2,1,0:T(8,128)}), f32[16,2,16,16,128]{4,3,2,1,0:T(8,128)}, u32[]{:S(2)}, u32[]{:S(2)}) async-start(f32[16,2,16,16,128]{4,3,2,1,0:T(8,128)} %middle.1), calls=%async_computation.3 | async-start | bytes 8388608 | tf_op jit(solution)/shard_map/all_to_all | solution.py:378
  125.4 4.3 %chain0.1 = (f32[16,256]{1,0:T(8,128)}, f32[256,256]{1,0:T(8,128)}, f32[8,128]{1,0:T(8,128)}) custom-call(f32[1]{0:T(128)} %bitcast.2.scale, f32[16,2,16,256]{3,2,1,0:T(8,128)} %all_to_all.20.jumps, f32[256,256]{1,0:T(8,128)} %get-tuple-element.38.gram_x, f32[256,256]{1,0:T(8,128)} %get-tuple-element.39.gram_y, f32[256,256]{1,0:T(8,128)} %stiff.3, ...), custom_call_target="tpu_custom_call" | custom-call | flops 16777216 | bytes 65536 | tf_op jit(solution)/shard_map/chain0/pallas_call | solution.py:297
  129.7 0.0 collective-permute-start.1
  129.7 0.5 collective-permute-start.2
  131.6 1.2 collective-permute-start.6
  132.8 0.0 collective-permute-done.2
  132.8 0.7 add.95
  133.5 2.2 %collective-permute-done.1.before = f32[256,256]{1,0:T(8,128)S(1)} collective-permute-done((f32[256,256]{1,0:T(8,128)}, f32[256,256]{1,0:T(8,128)S(1)}, u32[]{:S(2)}, u32[]{:S(2)}) %collective-permute-start.1) | collective-permute-done | bytes 262176 | tf_op jit(solution)/shard_map/ppermute | solution.py:358
  135.7 0.8 collective-permute-start.3
  136.5 2.3 %collective-permute-start.4 = (f32[8,128]{1,0:T(8,128)S(1)}, f32[8,128]{1,0:T(8,128)S(1)}, u32[]{:S(2)}, u32[]{:S(2)}) collective-permute-start(f32[8,128]{1,0:T(8,128)S(1)} %add.95), channel_id=1, source_target_pairs={{0,64},{16,80},{32,96},{48,112},{64,0},{80,16},{96,32},{112,48},{1... | collective-permute-start | bytes 12296 | tf_op jit(solution)/shard_map/ppermute | solution.py:362
  138.8 1.6 collective-permute-start.5
  140.4 9.7 %extra0.1.refs_0_ = f32[16,2,16,16,128]{4,3,2,1,0:T(8,128)} custom-call(f32[256,256]{1,0:T(8,128)} %get-tuple-element.66.base, f32[256]{0:T(256)} %broadcast_multiply_fusion.shift, f32[16,256]{1,0:T(8,128)} %get-tuple-element.71.own_x, f32[2,256]{1,0:T(2,128)} %pad_maximum_fusion.ends, f32[256,256]{1,0:T(8,128)} %get-tuple-element.40.own.image, ...), custom_call_target="tpu_custom_call" | custom-call | flops 8999999488 | bytes 65536 | tf_op jit(solution)/shard_map/extra0/pallas_call | solution.py:243
  150.2 0.0 collective-permute-done.5
  150.2 0.5 fusion.1
  152.0 0.6 pad_maximum_fusion.1.scale
  152.6 0.7 copy-done.1
  153.3 5.6 %chain1.1 = (f32[8,128]{1,0:T(8,128)}, f32[16,256]{1,0:T(8,128)}, f32[16,256]{1,0:T(8,128)}) custom-call(f32[3]{0:T(128)} %pad_maximum_fusion.1.scale, f32[16,2,16,256]{3,2,1,0:T(8,128)} %all_to_all.20.jumps, f32[256,256]{1,0:T(8,128)} %get-tuple-element.40.own.image, f32[256,256]{1,0:T(8,128)} %copy-done, f32[256,256]{1,0:T(8,128)} %copy-done.1, ...), custom_call_target="tpu_custom_call" | custom-call | flops 16777216 | bytes 65536 | tf_op jit(solution)/shard_map/chain1/pallas_call | solution.py:327
  158.9 8.4 %extra1.1.refs_0_ = f32[16,2,16,16,128]{4,3,2,1,0:T(8,128)} custom-call(f32[256,256]{1,0:T(8,128)} %get-tuple-element.66.base, f32[256]{0:T(256)} %broadcast_multiply_fusion.shift, f32[16,256]{1,0:T(8,128)} %get-tuple-element.71.own_x, f32[2,256]{1,0:T(2,128)} %pad_maximum_fusion.ends, ...), custom_call_target="tpu_custom_call", output_to_operand_aliasing={{}: (6, {})} | custom-call | flops 7500000256 | bytes 65536 | tf_op jit(solution)/shard_map/extra1/pallas_call | solution.py:243
  167.3 0.0 copy-start.2
  167.4 1.7 collective-permute-start.10
  169.1 3.1 %collective-permute-start.9 = (f32[8,128]{1,0:T(8,128)S(1)}, f32[8,128]{1,0:T(8,128)S(1)}, u32[]{:S(2)}, u32[]{:S(2)}) collective-permute-start(f32[8,128]{1,0:T(8,128)S(1)} %add.100), channel_id=1, source_target_pairs={{0,64},{16,80},{32,96},{48,112},{64,0},{80,16},{96,32},{112,48},{1... | collective-permute-start | bytes 12296 | tf_op jit(solution)/shard_map/ppermute | solution.py:362
  172.1 8.4 %extra2.1.extra = f32[16,2,16,16,128]{4,3,2,1,0:T(8,128)} custom-call(f32[256,256]{1,0:T(8,128)} %get-tuple-element.66.base, f32[256]{0:T(256)} %broadcast_multiply_fusion.shift, f32[16,256]{1,0:T(8,128)} %get-tuple-element.71.own_x, f32[2,256]{1,0:T(2,128)} %pad_maximum_fusion.ends, ...), custom_call_target="tpu_custom_call", output_to_operand_aliasing={{}: (6, {})} | custom-call | flops 7500000256 | bytes 65536 | tf_op jit(solution)/shard_map/extra2/pallas_call | solution.py:243
  180.5 0.6 fusion
  182.4 0.6 add_bitcast_fusion
  183.1 9.4 %backward.1 = f32[16,256,256]{2,1,0:T(8,128)} custom-call(f32[3]{0:T(128)} %pad_maximum_fusion.1.scale, f32[16,2,16,16,128]{4,3,2,1,0:T(8,128)} %all-to-all-done.3.field, f32[16,2,16,16,128]{4,3,2,1,0:T(8,128)} %extra2.1.extra, f32[256,256]{1,0:T(8,128)} %basis_y.11, f32[256,256]{1,0:T(8,128)} %basis_z.5), custom_call_target="tpu_custom_call" | custom-call | flops 3221225472 | bytes 12582912 | tf_op jit(solution)/shard_map/backward/pallas_call | solution.py:158
  (31 shorter events, 0.1 us)
Async XLA Ops:
  10.7 8.3 %copy-start.8 = (f32[8]{0:T(128)S(1)}, f32[8]{0:T(128)}, u32[]{:S(2)}) copy-start(f32[8]{0:T(128)} %param.12) | copy-start | bytes 100
  10.7 11.6 %copy-start.9 = (f32[256]{0:T(256)S(1)}, f32[256]{0:T(256)}, u32[]{:S(2)}) copy-start(f32[256]{0:T(256)} %param.17) | copy-start | bytes 3076
  10.8 12.9 %copy-start.4 = (f32[256]{0:T(256)S(1)}, f32[256]{0:T(256)}, u32[]{:S(2)}) copy-start(f32[256]{0:T(256)} %param.18) | copy-start | bytes 3076
  10.8 12.9 %copy-start.5 = (f32[256]{0:T(256)S(1)}, f32[256]{0:T(256)}, u32[]{:S(2)}) copy-start(f32[256]{0:T(256)} %param.16) | copy-start | bytes 3076
  10.8 71.2 %all-to-all-start = ((f32[16,2,16,16,128]{4,3,2,1,0:T(8,128)}), f32[16,2,16,16,128]{4,3,2,1,0:T(8,128)}, u32[]{:S(2)}, u32[]{:S(2)}) async-start(f32[16,2,16,16,128]{4,3,2,1,0:T(8,128)} %forward.3.part1), calls=%async_computation | async-start | bytes 8388608 | tf_op jit(solution)/shard_map/all_to_all | solution.py:378
  63.2 30.9 %copy-start.6 = (f32[256]{0:T(256)S(1)}, f32[256]{0:T(256)}, u32[]{:S(2)}) copy-start(f32[256]{0:T(256)} %broadcast_multiply_fusion.shift) | copy-start | bytes 3076
  64.3 6.7 %collective-permute-start = (f32[16,2,16,256]{3,2,1,0:T(8,128)S(1)}, f32[16,2,16,256]{3,2,1,0:T(8,128)S(1)}, u32[]{:S(2)}, u32[]{:S(2)}) collective-permute-start(f32[16,2,16,256]{3,2,1,0:T(8,128)S(1)} %slice.32), channel_id=1, source_target_pairs={{16,0},{32,16},{48,32},{64,48},{80,64},{96,80},{112,96},{0,112},{1... | collective-permute-start | bytes 1572872 | tf_op jit(solution)/shard_map/ppermute | solution.py:358
  83.9 20.3 %all-to-all-start.1 = ((f32[16,2,16,256]{3,2,1,0:T(8,128)}), f32[16,2,16,256]{3,2,1,0:T(8,128)S(1)}, u32[]{:S(2)}, u32[]{:S(2)}) async-start(f32[16,2,16,256]{3,2,1,0:T(8,128)} %slice_subtract_fusion), calls=%async_computation.1 | async-start | bytes 1048576 | tf_op jit(solution)/shard_map/all_to_all | solution.py:378
  119.4 63.7 %all-to-all-start.3 = ((f32[16,2,16,16,128]{4,3,2,1,0:T(8,128)}), f32[16,2,16,16,128]{4,3,2,1,0:T(8,128)}, u32[]{:S(2)}, u32[]{:S(2)}) async-start(f32[16,2,16,16,128]{4,3,2,1,0:T(8,128)} %middle.1), calls=%async_computation.3 | async-start | bytes 8388608 | tf_op jit(solution)/shard_map/all_to_all | solution.py:378
  129.7 6.0 %collective-permute-start.1 = (f32[256,256]{1,0:T(8,128)}, f32[256,256]{1,0:T(8,128)S(1)}, u32[]{:S(2)}, u32[]{:S(2)}) collective-permute-start(f32[256,256]{1,0:T(8,128)} %get-tuple-element.40.own.image), channel_id=1, source_target_pairs={{112,0},{0,16},{16,32},{32,48},{48,64},{64,80},{80,96},{96,112},{1... | collective-permute-start | bytes 786440 | tf_op jit(solution)/shard_map/ppermute | solution.py:358
  129.7 3.1 %collective-permute-start.2 = (f32[8,128]{1,0:T(8,128)}, f32[8,128]{1,0:T(8,128)S(1)}, u32[]{:S(2)}, u32[]{:S(2)}) collective-permute-start(f32[8,128]{1,0:T(8,128)} %get-tuple-element.41), channel_id=1, source_target_pairs={{0,16},{16,0},{32,48},{48,32},{64,80},{80,64},{96,112},{112,96},{1... | collective-permute-start | bytes 12296 | tf_op jit(solution)/shard_map/ppermute | solution.py:362
  131.6 21.0 %collective-permute-start.6 = (f32[256,256]{1,0:T(8,128)}, f32[256,256]{1,0:T(8,128)S(1)}, u32[]{:S(2)}, u32[]{:S(2)}) collective-permute-start(f32[256,256]{1,0:T(8,128)} %get-tuple-element.40.own.image), channel_id=1, source_target_pairs={{16,0},{32,16},{48,32},{64,48},{80,64},{96,80},{112,96},{0,112},{1... | collective-permute-start | bytes 786440 | tf_op jit(solution)/shard_map/ppermute | solution.py:358
  135.7 4.7 %copy-start = (f32[256,256]{1,0:T(8,128)}, f32[256,256]{1,0:T(8,128)S(1)}, u32[]{:S(2)}) copy-start(f32[256,256]{1,0:T(8,128)S(1)} %collective-permute-done.1.before) | copy-start | bytes 786436
  135.7 14.4 %collective-permute-start.3 = (f32[8,128]{1,0:T(8,128)S(1)}, f32[8,128]{1,0:T(8,128)S(1)}, u32[]{:S(2)}, u32[]{:S(2)}) collective-permute-start(f32[8,128]{1,0:T(8,128)S(1)} %add.95), channel_id=1, source_target_pairs={{0,32},{16,48},{32,0},{48,16},{64,96},{80,112},{96,64},{112,80},{1... | collective-permute-start | bytes 12296 | tf_op jit(solution)/shard_map/ppermute | solution.py:362
  136.5 13.7 %collective-permute-start.4 = (f32[8,128]{1,0:T(8,128)S(1)}, f32[8,128]{1,0:T(8,128)S(1)}, u32[]{:S(2)}, u32[]{:S(2)}) collective-permute-start(f32[8,128]{1,0:T(8,128)S(1)} %add.95), channel_id=1, source_target_pairs={{0,64},{16,80},{32,96},{48,112},{64,0},{80,16},{96,32},{112,48},{1... | collective-permute-start | bytes 12296 | tf_op jit(solution)/shard_map/ppermute | solution.py:362
  138.8 11.3 %collective-permute-start.5 = (f32[8,128]{1,0:T(8,128)S(1)}, f32[8,128]{1,0:T(8,128)S(1)}, u32[]{:S(2)}, u32[]{:S(2)}) collective-permute-start(f32[8,128]{1,0:T(8,128)S(1)} %add.95), channel_id=1, source_target_pairs={{0,96},{16,112},{32,64},{48,80},{64,32},{80,48},{96,0},{112,16},{1... | collective-permute-start | bytes 12296 | tf_op jit(solution)/shard_map/ppermute | solution.py:362
  152.6 0.7 copy-start.1
  158.9 8.4 %copy-start.7 = (f32[8,128]{1,0:T(8,128)S(1)}, f32[8,128]{1,0:T(8,128)}, u32[]{:S(2)}) copy-start(f32[8,128]{1,0:T(8,128)} %get-tuple-element.48) | copy-start | bytes 12292
  158.9 8.4 %collective-permute-start.7 = (f32[8,128]{1,0:T(8,128)}, f32[8,128]{1,0:T(8,128)S(1)}, u32[]{:S(2)}, u32[]{:S(2)}) collective-permute-start(f32[8,128]{1,0:T(8,128)} %get-tuple-element.48), channel_id=1, source_target_pairs={{0,16},{16,0},{32,48},{48,32},{64,80},{80,64},{96,112},{112,96},{1... | collective-permute-start | bytes 12296 | tf_op jit(solution)/shard_map/ppermute | solution.py:362
  167.3 15.1 %copy-start.2 = (f32[16,256]{1,0:T(8,128)S(1)}, f32[16,256]{1,0:T(8,128)}, u32[]{:S(2)}) copy-start(f32[16,256]{1,0:T(8,128)} %get-tuple-element.53) | copy-start | bytes 49156
  167.4 15.1 %copy-start.3 = (f32[16,256]{1,0:T(8,128)S(1)}, f32[16,256]{1,0:T(8,128)}, u32[]{:S(2)}) copy-start(f32[16,256]{1,0:T(8,128)} %get-tuple-element.55) | copy-start | bytes 49156
  167.4 13.1 %collective-permute-start.10 = (f32[8,128]{1,0:T(8,128)S(1)}, f32[8,128]{1,0:T(8,128)S(1)}, u32[]{:S(2)}, u32[]{:S(2)}) collective-permute-start(f32[8,128]{1,0:T(8,128)S(1)} %add.100), channel_id=1, source_target_pairs={{0,96},{16,112},{32,64},{48,80},{64,32},{80,48},{96,0},{112,16},{1... | collective-permute-start | bytes 12296 | tf_op jit(solution)/shard_map/ppermute | solution.py:362
  169.1 11.5 %collective-permute-start.8 = (f32[8,128]{1,0:T(8,128)S(1)}, f32[8,128]{1,0:T(8,128)S(1)}, u32[]{:S(2)}, u32[]{:S(2)}) collective-permute-start(f32[8,128]{1,0:T(8,128)S(1)} %add.100), channel_id=1, source_target_pairs={{0,32},{16,48},{32,0},{48,16},{64,96},{80,112},{96,64},{112,80},{1... | collective-permute-start | bytes 12296 | tf_op jit(solution)/shard_map/ppermute | solution.py:362
  169.1 11.5 %collective-permute-start.9 = (f32[8,128]{1,0:T(8,128)S(1)}, f32[8,128]{1,0:T(8,128)S(1)}, u32[]{:S(2)}, u32[]{:S(2)}) collective-permute-start(f32[8,128]{1,0:T(8,128)S(1)} %add.100), channel_id=1, source_target_pairs={{0,64},{16,80},{32,96},{48,112},{64,0},{80,16},{96,32},{112,48},{1... | collective-permute-start | bytes 12296 | tf_op jit(solution)/shard_map/ppermute | solution.py:362

commit v6 on v5

--- a/solution.py
+++ b/solution.py
@@ -129,18 +129,22 @@
     )(base, shift, basis_x, lines)
 
 
-def backward_kernel(scale, field, extra, basis_y, basis_z, out, left, right):
+def backward_kernel(
+    sums0, sums1, first, change, field, extra, basis_y, basis_z, out, multipliers, left, right
+):
     step = pl.program_id(0)
+    alpha = step_length(sums0[...])
 
     @pl.when(step == 0)
     def _():
+        multipliers[...] = alpha * first[...] + step_length(sums1[...]) * change[...]
         put_split(left, basis_y[...])
         put_split(right, basis_z[...].T)
 
     def total(x, slab, half):
         at = pl.ds((step * GROUP + x) % 8, ROWS, stride=8)
         terms = [ref.at[slab, half].reshape(ROWS * 8, LANES)[at, :] for ref in (field, extra)]
-        return terms[0] + scale[0] * terms[1]
+        return terms[0] + alpha * terms[1]
 
     parts = []
     for x in range(GROUP):
@@ -153,21 +157,33 @@
     out[...] = dot3(split(part), right).reshape(GROUP, N, N)
 
 
-def backward(scale, field, extra, basis_y, basis_z):
+def backward(sums0, sums1, first, change, field, extra, basis_y, basis_z):
     block = pl.BlockSpec((SLABS, 2, ROWS, 8, LANES), lambda x: (0, 0, 0, x * GROUP // 8, 0))
     return pl.pallas_call(
         backward_kernel,
         grid=(ROWS // GROUP,),
-        in_specs=[smem(), block, block, whole((N, N)), whole((N, N))],
-        out_specs=pl.BlockSpec((GROUP, N, N), lambda x: (x, 0, 0)),
-        out_shape=jax.ShapeDtypeStruct((ROWS, N, N), F32),
+        in_specs=[
+            whole((8, 128)),
+            whole((8, 128)),
+            whole((ROWS, N)),
+            whole((ROWS, N)),
+            block,
+            block,
+            whole((N, N)),
+            whole((N, N)),
+        ],
+        out_specs=[pl.BlockSpec((GROUP, N, N), lambda x: (x, 0, 0)), whole((ROWS, N))],
+        out_shape=[
+            jax.ShapeDtypeStruct((ROWS, N, N), F32),
+            jax.ShapeDtypeStruct((ROWS, N), F32),
+        ],
         scratch_shapes=[pltpu.VMEM((2, N, N), BF16), pltpu.VMEM((2, N, N), BF16)],
         compiler_params=params(),
         cost_estimate=pl.CostEstimate(
             flops=12 * ROWS * N**3, bytes_accessed=12 * ROWS * N * N, transcendentals=0
         ),
         name="backward",
-    )(scale, field, extra, basis_y, basis_z)
+    )(sums0, sums1, first, change, field, extra, basis_y, basis_z)
 
 
 def inverse_parts(denom):
@@ -185,43 +201,67 @@
     return both[:count] + (both[count:] + dot(high, w_low))
 
 
-def faces_kernel(base, shift, own_x, ends, products, part0, part1, out):
+def faces_kernel(
+    own_rho, shift, eigen_x, eigen_z, own_x, basis_z, part0, part1, out, near, base, products
+):
     block = pl.program_id(0)
-    first, last = ends[0:1], ends[1:2]
+    first, last = basis_z[0:1], basis_z[N - 1 : N]
+
+    @pl.when(block == 0)
+    def _():
+        rows = jnp.broadcast_to(eigen_z[...], (N, N)).T
+        base[...] = own_rho[0] * (rows + eigen_x[...])
+        at = lax.broadcasted_iota(jnp.int32, (16, N), 0)
+        products[...] = jnp.where(
+            at == 0,
+            last * last,
+            jnp.where(at == 1, last * first, jnp.where(at == 2, first * first, 0.0)),
+        )
+
     for jj in range(ROWS):
         a = jnp.concatenate([part0[0, 0, jj], part0[0, 1, jj]], axis=1)
         b = jnp.concatenate([part1[0, 0, jj], part1[0, 1, jj]], axis=1)
         rows = jnp.concatenate([a * last, b * last, a * first, b * first, products[...]], axis=0)
         result = dot3(split(rows), inverse_parts(base[...] + shift[block * ROWS + jj]))
-        for face in range(4):
-            piece = result[16 * face : 16 * face + 16] * own_x[...]
-            out[0, face, jj : jj + 1] = jnp.sum(piece, axis=0, keepdims=True)
+        sums = [
+            jnp.sum(result[16 * face : 16 * face + 16] * own_x[...], axis=0, keepdims=True)
+            for face in range(4)
+        ]
+        for load in range(2):
+            out[0, load, jj : jj + 1] = sums[load]
+            near[0, load, jj : jj + 1] = sums[2 + load]
         for pair in range(3):
-            out[0, 4 + pair, jj : jj + 1] = result[64 + pair : 65 + pair]
-
-
-def faces(base, shift, own_x, ends, products, part0, part1):
+            out[0, 2 + pair, jj : jj + 1] = result[64 + pair : 65 + pair]
+
+
+def faces(own_rho, shift, eigen_x, eigen_z, own_x, basis_z, part0, part1):
     block = pl.BlockSpec((1, 2, ROWS, ROWS, LANES), lambda j: (j, 0, 0, 0, 0))
     return pl.pallas_call(
         faces_kernel,
-        grid=(N // ROWS,),
+        grid=(SLABS,),
         in_specs=[
+            smem(),
+            smem(),
+            whole((1, N)),
+            whole((1, N)),
+            whole((ROWS, N)),
             whole((N, N)),
-            smem(),
-            whole((ROWS, N)),
-            whole((2, N)),
-            whole((16, N)),
             block,
             block,
         ],
-        out_specs=pl.BlockSpec((1, 7, ROWS, N), lambda j: (j, 0, 0, 0)),
-        out_shape=jax.ShapeDtypeStruct((SLABS, 7, N // SLABS, N), F32),
-        compiler_params=params(),
-        cost_estimate=pl.CostEstimate(
-            flops=N**3, bytes_accessed=N * N, transcendentals=0
-        ),
+        out_specs=[
+            pl.BlockSpec((1, 5, ROWS, N), lambda j: (j, 0, 0, 0)),
+            pl.BlockSpec((1, 2, ROWS, N), lambda j: (j, 0, 0, 0)),
+        ],
+        out_shape=[
+            jax.ShapeDtypeStruct((SLABS, 5, ROWS, N), F32),
+            jax.ShapeDtypeStruct((SLABS, 2, ROWS, N), F32),
+        ],
+        scratch_shapes=[pltpu.VMEM((N, N), F32), pltpu.VMEM((16, N), F32)],
+        compiler_params=params(),
+        cost_estimate=pl.CostEstimate(flops=N**3, bytes_accessed=N * N, transcendentals=0),
         name="faces",
-    )(base, shift, own_x, ends, products, part0, part1)
+    )(own_rho, shift, eigen_x, eigen_z, own_x, basis_z, part0, part1)
 
 
 def extra_kernel(part, base, shift, own_x, ends, own, before, *refs):
@@ -279,6 +319,10 @@
     return search, image, jnp.sum(seen * search), jnp.sum(image * search)
 
 
+def step_length(sums):
+    return sums[0:1, 0:1] / (sums[1:2, 0:1] + 1e-06)
+
+
 def scalars_block(upper, lower):
     at = lax.broadcasted_iota(jnp.int32, (8, 128), 0)
     return jnp.where(at == 0, upper, jnp.where(at == 1, lower, 0.0))
@@ -307,11 +351,11 @@
 
 
 def chain1_kernel(
-    scale, jumps, image, before, after, pieces, gram_x, gram_y, stiff, own_x, basis_y, sums, out, rows
+    scale, sums_in, jumps, image, before, after, pieces, gram_x, gram_y, stiff, own_x, basis_y, sums, out, rows
 ):
-    alpha, ratio, weight = scale[0], scale[1], scale[2]
+    alpha, ratio, weight = step_length(sums_in[...]), scale[0], scale[1]
     t = image[...]
-    table = [pieces[:, 4 + pair].reshape(N, N) for pair in range(3)]
+    table = [pieces[:, 2 + pair].reshape(N, N) for pair in range(3)]
     own = table[1] * before[...] - table[0] * t
     other = table[2] * t - table[1] * after[...]
     q = jumps[:, 1].reshape(N, N) + alpha * (own - ratio * other)
@@ -326,7 +370,7 @@
 def chain1(*args):
     return pl.pallas_call(
         chain1_kernel,
-        in_specs=[smem()] + [pl.BlockSpec(memory_space=pltpu.VMEM)] * 10,
+        in_specs=[smem()] + [pl.BlockSpec(memory_space=pltpu.VMEM)] * 11,
         out_shape=(
             jax.ShapeDtypeStruct((8, 128), F32),
             jax.ShapeDtypeStruct((ROWS, N), F32),
@@ -368,10 +412,6 @@
 
 def over_pairs(sums):
     return (sums + from_partner(sums, 2)) + (from_partner(sums, 4) + from_partner(sums, 6))
-
-
-def step_length(sums):
-    return sums[0, 0] / (sums[1, 0] + 1e-06)
 
 
 def exchange(block):
@@ -391,30 +431,30 @@
     start = slab_index * ROWS
     own_x = lax.dynamic_slice_in_dim(basis_x, start, ROWS, 0)
 
+    own_shift = own_rho * lax.dynamic_slice_in_dim(eigen_y, start, ROWS, 0)
+    shift = exchange(jnp.broadcast_to(own_shift, (SLABS, ROWS))).reshape(N)
+
     part1 = forward(source, coarse, 1, basis_y, basis_z)
+    part1, shift = lax.optimization_barrier((part1, shift))
     lines = exchange(part1)
 
     base_xz = own_rho * (eigen_x[:, None] + eigen_z[None, :])
-    base_zx = own_rho * (eigen_z[:, None] + eigen_x[None, :])
-    shift = own_rho * eigen_y
-    own_shift = lax.dynamic_slice_in_dim(shift, start, ROWS, 0)
     ends = jnp.stack([basis_z[0], basis_z[N - 1]])
-    products = jnp.stack([ends[1] * ends[1], ends[1] * ends[0], ends[0] * ends[0]])
-    products = jnp.pad(products, ((0, 13), (0, 0)))
     gram_x, gram_y = grams(basis_x, basis_y)
 
     part0 = forward(source, coarse, 0, basis_y, basis_z)
-    pieces = faces(base_zx, shift, own_x, ends, products, part0, part1)
-    following = from_behind(pieces[:, 2:4], "sub", -1)
-    pieces, following, lines, gram_x, gram_y = lax.optimization_barrier(
-        (pieces, following, lines, gram_x, gram_y)
+    pieces, near = faces(
+        own_rho.reshape(1), shift, eigen_x[None], eigen_z[None], own_x, basis_z, part0, part1
+    )
+    shares = pieces[:, 0:2] - from_behind(near, "sub", -1)
+    shares, lines, gram_x, gram_y, base_xz, ends = lax.optimization_barrier(
+        (shares, lines, gram_x, gram_y, base_xz, ends)
     )
     spread = middle(base_xz, own_shift, basis_x, lines)
-    shares = exchange(pieces[:, 0:2] - following)
+    shares = exchange(shares)
     shares, spread = lax.optimization_barrier((shares, spread))
     own_jumps = jnp.sum(shares, axis=0)
     jumps = exchange(jnp.broadcast_to(own_jumps[None], (SLABS,) + own_jumps.shape))
-
     spread, jumps = lax.optimization_barrier((spread, jumps))
     spread = exchange(spread)
 
@@ -429,20 +469,30 @@
     before, sums0 = lax.optimization_barrier((before, sums0))
     more = terms(0, own=image0, before=before)
     sums0, more = lax.optimization_barrier((over_pairs(sums0), more))
-    alpha0 = step_length(sums0)
-
-    scale = jnp.stack([alpha0, own_rho / next_rho, weight])
+
+    scale = jnp.stack([own_rho / next_rho, weight])
     sums1, jump, change = chain1(
-        scale, jumps, image0, before, after, pieces, gram_x, gram_y, face_stiff, own_x, basis_y
+        scale,
+        sums0,
+        jumps,
+        image0,
+        before,
+        after,
+        pieces,
+        gram_x,
+        gram_y,
+        face_stiff,
+        own_x,
+        basis_y,
     )
     sums1, more = lax.optimization_barrier((sums1, more))
     more = terms(1, own=image0, before=before, filled=(more,))
     sums1, more = lax.optimization_barrier((over_pair(sums1), more))
     more = terms(2, own=image0, before=before, filled=(more,))
     sums1, more = lax.optimization_barrier((over_pairs(sums1), more))
-    alpha1 = step_length(sums1)
-    multipliers = alpha0 * first + alpha1 * change
-    solution = backward(scale, spread, more, basis_y, basis_z)
+    solution, multipliers = backward(
+        sums0, sums1, first, change, spread, more, basis_y, basis_z
+    )
     return (solution[None], multipliers[None], jump[None])
 
 

time: 195 us -> 191 us (0.979)
  waiting for transfers between devices: 19.4 us -> 11.4 us
  starting transfers between devices: 34.4 us -> 40.3 us
  between operations: 6.03 us -> 3.42 us
    all_to_all x3 -> x4, waiting for transfers between devices: 13.1 us -> 5.55 us  [exchange(): lax.all_to_all(block, 'slab', split_axis=0, concat_axis=0, tiled=True)]
    all_to_all x3 -> x4, starting transfers between devices: 23.1 us -> 30.2 us  [exchange(): lax.all_to_all(block, 'slab', split_axis=0, concat_axis=0, tiled=True)]
  transfers between devices with their start and end apart: 14 -> 15, of which waited for: 4 -> 4; matrix products, arithmetic and copies ran while one was open for 6% -> 5% of each run, Pallas kernels for 44% -> 50%
where the time goes in v6:
time: 191 us; the launch traced here: 189 us
  Pallas kernels  104 us (54%)
  starting transfers between devices  40.3 us (21%)
  blocking collectives  14.5 us (8%)
  waiting for transfers between devices  11.4 us (6%)
  other arithmetic  8.52 us (4%)
  local copies, waits for them, and re-layouts  5.97 us (3%)
  between operations  3.42 us (2%)
    all_to_all x4, starting transfers between devices, exchange(): lax.all_to_all(block, 'slab', split_axis=0, concat_axis=0, tiled=True)  30.2 us
    pallas_call x1, Pallas kernels, faces(): pl.pallas_call(faces_kernel, grid=(SLABS,), in_specs=[smem(), smem(), who...  28.7 us
    pallas_call x3, Pallas kernels, extra(): pl.pallas_call(functools.partial(extra_kernel, part), grid=(stop - skip,)...  26.5 us
    pallas_call x2, Pallas kernels, forward(): pl.pallas_call(forward_kernel, grid=(ROWS // GROUP,), in_specs=[pl.BlockS...  20.1 us
    all_to_all x1, blocking collectives, exchange(): lax.all_to_all(block, 'slab', split_axis=0, concat_axis=0, tiled=True)  14.5 us
    pallas_call x1, Pallas kernels, backward(): pl.pallas_call(backward_kernel, grid=(ROWS // GROUP,), in_specs=[whole((8...  9.27 us
    ppermute x8, starting transfers between devices, from_partner(): return lax.ppermute(sums, 'sub', [(i, i ^ bits) for i in range(8)])  8.97 us
    pallas_call x1, Pallas kernels, middle(): pl.pallas_call(middle_kernel, grid=(N // SLABS // GROUP,), in_specs=[whol...  7.41 us
  transfers between devices with their start and end apart: 15, of which 4 were waited for; matrix products, arithmetic and copies ran while one was open for 5% of the time, Pallas kernels for 50%

profile of v6, /device:TPU:6, one launch (start us, length us, event | category | flops | bytes accessed | tf_op | source)
XLA Modules:
  0.0 188.5 jit_solution(5458406341645274823)
XLA Ops:
  0.6 1.4 fusion.1
  2.0 1.4 dynamic-slice_multiply_fusion.shift
  3.4 0.6 broadcast_in_dim.26
  4.0 8.0 %all-to-all-start = ((f32[16,1,16]{2,1,0:T(1,128)}), f32[16,1,16]{2,1,0:T(1,128)S(1)}, u32[]{:S(2)}, u32[]{:S(2)}) async-start(f32[16,1,16]{2,1,0:T(1,128)} %broadcast_in_dim.26), calls=%async_computation | async-start | bytes 16384 | tf_op jit(solution)/shard_map/all_to_all | solution.py:418
  12.1 10.1 %forward.2.part1 = f32[16,2,16,16,128]{4,3,2,1,0:T(8,128)} custom-call(f32[16,256,256]{2,1,0:T(8,128)} %bitcast.10, f32[2,1,16,256,256]{4,3,2,1,0:T(8,128)} %coarse.3, f32[256,256]{1,0:T(8,128)} %basis_y.11, f32[256,256]{1,0:T(8,128)} %basis_z.7), custom_call_target="tpu_custom_call" | custom-call | flops 3221225472 | bytes 12582912 | tf_op jit(solution)/shard_map/forward/pallas_call | solution.py:75
  22.2 0.0 all-to-all-done
  22.2 0.5 broadcast.10
  22.7 0.7 reduce.3
  23.4 0.7 reshape.21.shift
  24.0 7.3 %all-to-all-start.1 = ((f32[16,2,16,16,128]{4,3,2,1,0:T(8,128)}), f32[16,2,16,16,128]{4,3,2,1,0:T(8,128)}, u32[]{:S(2)}, u32[]{:S(2)}) async-start(f32[16,2,16,16,128]{4,3,2,1,0:T(8,128)} %forward.2.part1), calls=%async_computation.1 | async-start | bytes 8388608 | tf_op jit(solution)/shard_map/all_to_all | solution.py:418
  31.3 2.6 %grams.1 = (f32[256,256]{1,0:T(8,128)}, f32[256,256]{1,0:T(8,128)}) custom-call(f32[256,256]{1,0:T(8,128)} %basis_x.3, f32[256,256]{1,0:T(8,128)} %basis_y.11), custom_call_target="tpu_custom_call" | custom-call | tf_op jit(solution)/shard_map/grams/pallas_call | solution.py:394
  33.9 1.3 constant_dynamic-slice_fusion.own_x
  35.2 10.0 %forward.3.part0 = f32[16,2,16,16,128]{4,3,2,1,0:T(8,128)} custom-call(f32[16,256,256]{2,1,0:T(8,128)} %bitcast.11, f32[2,1,16,256,256]{4,3,2,1,0:T(8,128)} %coarse.3, f32[256,256]{1,0:T(8,128)} %basis_y.11, f32[256,256]{1,0:T(8,128)} %basis_z.7), custom_call_target="tpu_custom_call" | custom-call | flops 3221225472 | bytes 12582912 | tf_op jit(solution)/shard_map/forward/pallas_call | solution.py:75
  45.2 28.7 %faces.1 = (f32[16,5,16,256]{3,2,1,0:T(8,128)}, f32[16,2,16,256]{3,2,1,0:T(8,128)}) custom-call(f32[1]{0:T(128)} %get-tuple-element.74.own_rho, f32[256]{0:T(256)} %reshape.21.shift, f32[1,256]{1,0:T(1,128)} %bitcast.12, f32[1,256]{1,0:T(1,128)} %bitcast.13, f32[16,256]{1,0:T(8,128)} %constant_dynamic-slice_fusion.own_x, f32[256,256]{1,0:T(8,128)} %basis_z.7, ...), custom_call_target="tpu_custom_call" | custom-call | flops 16777216 | bytes 65536 | tf_op jit(solution)/shard_map/faces/pallas_call | solution.py:239
  73.9 0.7 fusion
  74.7 0.6 pad_maximum_fusion.ends
  75.2 1.4 add_multiply_fusion.base
  76.6 4.3 %collective-permute-done = f32[16,2,16,256]{3,2,1,0:T(8,128)S(1)} collective-permute-done((f32[16,2,16,256]{3,2,1,0:T(8,128)}, f32[16,2,16,256]{3,2,1,0:T(8,128)S(1)}, u32[]{:S(2)}, u32[]{:S(2)}) %collective-permute-start) | collective-permute-done | bytes 524320 | tf_op jit(solution)/shard_map/ppermute | solution.py:402
  80.9 1.9 %slice_subtract_fusion = f32[16,2,16,256]{3,2,1,0:T(8,128)} fusion(f32[16,2,16,256]{3,2,1,0:T(8,128)S(1)} %collective-permute-done, f32[16,5,16,256]{3,2,1,0:T(8,128)} %get-tuple-element.39.pieces), kind=kLoop, calls=%fused_computation | loop fusion | flops 131072 | bytes 1572864 | tf_op jit(solution)/shard_map/sub | solution.py:449
  82.9 2.9 %all-to-all-done.1.lines = f32[16,2,16,16,128]{4,3,2,1,0:T(8,128)} async-done(((f32[16,2,16,16,128]{4,3,2,1,0:T(8,128)}), f32[16,2,16,16,128]{4,3,2,1,0:T(8,128)}, u32[]{:S(2)}, u32[]{:S(2)}) %all-to-all-start.1) | async-done | bytes 4194336 | tf_op jit(solution)/shard_map/all_to_all | solution.py:418
  85.7 10.1 %all-to-all-start.2 = ((f32[16,2,16,256]{3,2,1,0:T(8,128)}), f32[16,2,16,256]{3,2,1,0:T(8,128)S(1)}, u32[]{:S(2)}, u32[]{:S(2)}) async-start(f32[16,2,16,256]{3,2,1,0:T(8,128)} %slice_subtract_fusion), calls=%async_computation.2 | async-start | bytes 1048576 | tf_op jit(solution)/shard_map/all_to_all | solution.py:418
  95.9 7.4 %middle.1 = f32[16,2,16,16,128]{4,3,2,1,0:T(8,128)} custom-call(f32[256,256]{1,0:T(8,128)} %add_multiply_fusion.base, f32[16]{0:T(128)} %copy-done.5, f32[256,256]{1,0:T(8,128)} %basis_x.3, f32[16,2,16,16,128]{4,3,2,1,0:T(8,128)} %all-to-all-done.1.lines), custom_call_target="tpu_custom_call" | custom-call | flops 3221225472 | bytes 8388608 | tf_op jit(solution)/shard_map/middle/pallas_call | solution.py:117
  103.3 2.7 %all-to-all-done.2 = f32[16,2,16,256]{3,2,1,0:T(8,128)S(1)} async-done(((f32[16,2,16,256]{3,2,1,0:T(8,128)}), f32[16,2,16,256]{3,2,1,0:T(8,128)S(1)}, u32[]{:S(2)}, u32[]{:S(2)}) %all-to-all-start.2) | async-done | bytes 524320 | tf_op jit(solution)/shard_map/all_to_all | solution.py:418
  106.0 0.1 broadcast_in_dim.29
  106.1 14.5 %all_to_all.26.jumps = f32[16,2,16,256]{3,2,1,0:T(8,128)} all-to-all(f32[16,2,16,256]{3,2,1,0:T(8,128)S(1)} %broadcast_in_dim.29), channel_id=1, replica_groups=mesh['sub'=8,'slab'=16] {'slab'}, dimensions={0} | all-to-all | bytes 1048576 | tf_op jit(solution)/shard_map/all_to_all | solution.py:418
  120.6 4.7 %all-to-all-start.4 = ((f32[16,2,16,16,128]{4,3,2,1,0:T(8,128)}), f32[16,2,16,16,128]{4,3,2,1,0:T(8,128)}, u32[]{:S(2)}, u32[]{:S(2)}) async-start(f32[16,2,16,16,128]{4,3,2,1,0:T(8,128)} %middle.1), calls=%async_computation.4 | async-start | bytes 8388608 | tf_op jit(solution)/shard_map/all_to_all | solution.py:418
  126.7 4.3 %chain0.1 = (f32[16,256]{1,0:T(8,128)}, f32[256,256]{1,0:T(8,128)}, f32[8,128]{1,0:T(8,128)}) custom-call(f32[1]{0:T(128)} %bitcast.2.scale, f32[16,2,16,256]{3,2,1,0:T(8,128)} %all_to_all.26.jumps, f32[256,256]{1,0:T(8,128)} %get-tuple-element.49.gram_x, f32[256,256]{1,0:T(8,128)} %get-tuple-element.50.gram_y, f32[256,256]{1,0:T(8,128)} %stiff.3, ...), custom_call_target="tpu_custom_call" | custom-call | flops 16777216 | bytes 65536 | tf_op jit(solution)/shard_map/chain0/pallas_call | solution.py:341
  132.3 0.7 collective-permute-start.2
  133.0 0.6 pad_maximum_fusion.1.scale
  133.7 1.1 collective-permute-start.6
  134.8 0.0 collective-permute-done.2
  134.8 0.7 add.66
  135.5 1.5 collective-permute-done.1.before
  137.0 1.7 collective-permute-start.5
  138.7 1.2 collective-permute-start.4
  139.9 1.2 collective-permute-start.3
  141.1 9.7 %extra0.1.refs_0_ = f32[16,2,16,16,128]{4,3,2,1,0:T(8,128)} custom-call(f32[256,256]{1,0:T(8,128)} %add_multiply_fusion.base, f32[256]{0:T(256)} %reshape.21.shift, f32[16,256]{1,0:T(8,128)} %constant_dynamic-slice_fusion.own_x, f32[2,256]{1,0:T(2,128)} %pad_maximum_fusion.ends, f32[256,256]{1,0:T(8,128)} %get-tuple-element.51.own.image, f32[256,256]{1,0:T(8,128)} %copy-done), custom_call_target="tpu_custom_call" | custom-call | flops 8999999488 | bytes 65536 | tf_op jit(solution)/shard_map/extra0/pallas_call | solution.py:283
  150.8 0.0 collective-permute-done.5
  150.8 0.6 add_add_fusion.1.sums_in.sums0
  151.4 0.7 copy-done.1
  152.1 5.5 %chain1.1 = (f32[8,128]{1,0:T(8,128)}, f32[16,256]{1,0:T(8,128)}, f32[16,256]{1,0:T(8,128)}) custom-call(f32[2]{0:T(128)} %pad_maximum_fusion.1.scale, f32[8,128]{1,0:T(8,128)} %add_add_fusion.1.sums_in.sums0, f32[16,2,16,256]{3,2,1,0:T(8,128)} %all_to_all.26.jumps, f32[256,256]{1,0:T(8,128)} %get-tuple-element.51.own.image, f32[256,256]{1,0:T(8,128)} %copy-done, ...), custom_call_target="tpu_custom_call" | custom-call | flops 16777216 | bytes 65536 | tf_op jit(solution)/shard_map/chain1/pallas_call | solution.py:371
  157.6 8.4 %extra1.1.refs_0_ = f32[16,2,16,16,128]{4,3,2,1,0:T(8,128)} custom-call(f32[256,256]{1,0:T(8,128)} %add_multiply_fusion.base, f32[256]{0:T(256)} %reshape.21.shift, f32[16,256]{1,0:T(8,128)} %constant_dynamic-slice_fusion.own_x, f32[2,256]{1,0:T(2,128)} %pad_maximum_fusion.ends, ...), custom_call_target="tpu_custom_call", output_to_operand_aliasing={{}: (6, {})} | custom-call | flops 7500000256 | bytes 65536 | tf_op jit(solution)/shard_map/extra1/pallas_call | solution.py:283
  166.0 1.8 collective-permute-start.10
  167.8 1.2 collective-permute-start.9
  169.0 1.2 collective-permute-start.8
  170.2 8.4 %extra2.1.extra = f32[16,2,16,16,128]{4,3,2,1,0:T(8,128)} custom-call(f32[256,256]{1,0:T(8,128)} %add_multiply_fusion.base, f32[256]{0:T(256)} %reshape.21.shift, f32[16,256]{1,0:T(8,128)} %constant_dynamic-slice_fusion.own_x, f32[2,256]{1,0:T(2,128)} %pad_maximum_fusion.ends, ...), custom_call_target="tpu_custom_call", output_to_operand_aliasing={{}: (6, {})} | custom-call | flops 7500000256 | bytes 65536 | tf_op jit(solution)/shard_map/extra2/pallas_call | solution.py:283
  178.6 0.6 add_add_fusion.sums1
  179.2 9.3 %backward.1 = (f32[16,256,256]{2,1,0:T(8,128)}, f32[16,256]{1,0:T(8,128)}) custom-call(f32[8,128]{1,0:T(8,128)} %add_add_fusion.1.sums_in.sums0, f32[8,128]{1,0:T(8,128)} %add_add_fusion.sums1, f32[16,256]{1,0:T(8,128)} %get-tuple-element.64.first, f32[16,256]{1,0:T(8,128)} %get-tuple-element.65.change, f32[16,2,16,16,128]{4,3,2,1,0:T(8,128)} %all-to-all-done.4.field, ...), custom_call_target="tpu_custom_call" | custom-call | flops 3221225472 | bytes 12582912 | tf_op jit(solution)/shard_map/backward/pallas_call | solution.py:162
  (24 shorter events, 0.1 us)
Async XLA Ops:
  3.4 18.8 %copy-start.5 = (f32[16]{0:T(128)}, f32[16]{0:T(128)S(1)}, u32[]{:S(2)}) copy-start(f32[16]{0:T(128)S(1)} %dynamic-slice_multiply_fusion.shift) | copy-start | bytes 196
  4.0 18.2 %all-to-all-start = ((f32[16,1,16]{2,1,0:T(1,128)}), f32[16,1,16]{2,1,0:T(1,128)S(1)}, u32[]{:S(2)}, u32[]{:S(2)}) async-start(f32[16,1,16]{2,1,0:T(1,128)} %broadcast_in_dim.26), calls=%async_computation | async-start | bytes 16384 | tf_op jit(solution)/shard_map/all_to_all | solution.py:418
  24.0 61.7 %all-to-all-start.1 = ((f32[16,2,16,16,128]{4,3,2,1,0:T(8,128)}), f32[16,2,16,16,128]{4,3,2,1,0:T(8,128)}, u32[]{:S(2)}, u32[]{:S(2)}) async-start(f32[16,2,16,16,128]{4,3,2,1,0:T(8,128)} %forward.2.part1), calls=%async_computation.1 | async-start | bytes 8388608 | tf_op jit(solution)/shard_map/all_to_all | solution.py:418
  45.2 30.0 %copy-start.3 = (f32[256]{0:T(256)S(1)}, f32[256]{0:T(256)}, u32[]{:S(2)}) copy-start(f32[256]{0:T(256)} %param.16) | copy-start | bytes 3076
  45.2 30.0 %copy-start.4 = (f32[256]{0:T(256)S(1)}, f32[256]{0:T(256)}, u32[]{:S(2)}) copy-start(f32[256]{0:T(256)} %param.18) | copy-start | bytes 3076
  73.9 7.0 %collective-permute-start = (f32[16,2,16,256]{3,2,1,0:T(8,128)}, f32[16,2,16,256]{3,2,1,0:T(8,128)S(1)}, u32[]{:S(2)}, u32[]{:S(2)}) collective-permute-start(f32[16,2,16,256]{3,2,1,0:T(8,128)} %get-tuple-element.40), channel_id=1, source_target_pairs={{16,0},{32,16},{48,32},{64,48},{80,64},{96,80},{112,96},{0,112},{1... | collective-permute-start | bytes 1572872 | tf_op jit(solution)/shard_map/ppermute | solution.py:402
  85.7 20.3 %all-to-all-start.2 = ((f32[16,2,16,256]{3,2,1,0:T(8,128)}), f32[16,2,16,256]{3,2,1,0:T(8,128)S(1)}, u32[]{:S(2)}, u32[]{:S(2)}) async-start(f32[16,2,16,256]{3,2,1,0:T(8,128)} %slice_subtract_fusion), calls=%async_computation.2 | async-start | bytes 1048576 | tf_op jit(solution)/shard_map/all_to_all | solution.py:418
  120.6 58.6 %all-to-all-start.4 = ((f32[16,2,16,16,128]{4,3,2,1,0:T(8,128)}), f32[16,2,16,16,128]{4,3,2,1,0:T(8,128)}, u32[]{:S(2)}, u32[]{:S(2)}) async-start(f32[16,2,16,16,128]{4,3,2,1,0:T(8,128)} %middle.1), calls=%async_computation.4 | async-start | bytes 8388608 | tf_op jit(solution)/shard_map/all_to_all | solution.py:418
  131.0 6.0 %collective-permute-start.1 = (f32[256,256]{1,0:T(8,128)}, f32[256,256]{1,0:T(8,128)S(1)}, u32[]{:S(2)}, u32[]{:S(2)}) collective-permute-start(f32[256,256]{1,0:T(8,128)} %get-tuple-element.51.own.image), channel_id=1, source_target_pairs={{112,0},{0,16},{16,32},{32,48},{48,64},{64,80},{80,96},{96,112},{1... | collective-permute-start | bytes 786440 | tf_op jit(solution)/shard_map/ppermute | solution.py:402
  132.3 2.5 %collective-permute-start.2 = (f32[8,128]{1,0:T(8,128)}, f32[8,128]{1,0:T(8,128)S(1)}, u32[]{:S(2)}, u32[]{:S(2)}) collective-permute-start(f32[8,128]{1,0:T(8,128)} %get-tuple-element.52), channel_id=1, source_target_pairs={{0,16},{16,0},{32,48},{48,32},{64,80},{80,64},{96,112},{112,96},{1... | collective-permute-start | bytes 12296 | tf_op jit(solution)/shard_map/ppermute | solution.py:406
  133.7 17.7 %collective-permute-start.6 = (f32[256,256]{1,0:T(8,128)}, f32[256,256]{1,0:T(8,128)S(1)}, u32[]{:S(2)}, u32[]{:S(2)}) collective-permute-start(f32[256,256]{1,0:T(8,128)} %get-tuple-element.51.own.image), channel_id=1, source_target_pairs={{16,0},{32,16},{48,32},{64,48},{80,64},{96,80},{112,96},{0,112},{1... | collective-permute-start | bytes 786440 | tf_op jit(solution)/shard_map/ppermute | solution.py:402
  137.0 4.1 %copy-start = (f32[256,256]{1,0:T(8,128)}, f32[256,256]{1,0:T(8,128)S(1)}, u32[]{:S(2)}) copy-start(f32[256,256]{1,0:T(8,128)S(1)} %collective-permute-done.1.before) | copy-start | bytes 786436
  137.0 13.8 %collective-permute-start.5 = (f32[8,128]{1,0:T(8,128)S(1)}, f32[8,128]{1,0:T(8,128)S(1)}, u32[]{:S(2)}, u32[]{:S(2)}) collective-permute-start(f32[8,128]{1,0:T(8,128)S(1)} %add.66), channel_id=1, source_target_pairs={{0,96},{16,112},{32,64},{48,80},{64,32},{80,48},{96,0},{112,16},{1... | collective-permute-start | bytes 12296 | tf_op jit(solution)/shard_map/ppermute | solution.py:406
  138.7 12.1 %collective-permute-start.4 = (f32[8,128]{1,0:T(8,128)S(1)}, f32[8,128]{1,0:T(8,128)S(1)}, u32[]{:S(2)}, u32[]{:S(2)}) collective-permute-start(f32[8,128]{1,0:T(8,128)S(1)} %add.66), channel_id=1, source_target_pairs={{0,64},{16,80},{32,96},{48,112},{64,0},{80,16},{96,32},{112,48},{1... | collective-permute-start | bytes 12296 | tf_op jit(solution)/shard_map/ppermute | solution.py:406
  139.9 10.9 %collective-permute-start.3 = (f32[8,128]{1,0:T(8,128)S(1)}, f32[8,128]{1,0:T(8,128)S(1)}, u32[]{:S(2)}, u32[]{:S(2)}) collective-permute-start(f32[8,128]{1,0:T(8,128)S(1)} %add.66), channel_id=1, source_target_pairs={{0,32},{16,48},{32,0},{48,16},{64,96},{80,112},{96,64},{112,80},{1... | collective-permute-start | bytes 12296 | tf_op jit(solution)/shard_map/ppermute | solution.py:406
  151.4 0.7 copy-start.1
  157.6 8.4 %copy-start.2 = (f32[8,128]{1,0:T(8,128)S(1)}, f32[8,128]{1,0:T(8,128)}, u32[]{:S(2)}) copy-start(f32[8,128]{1,0:T(8,128)} %get-tuple-element.59) | copy-start | bytes 12292
  157.6 8.4 %collective-permute-start.7 = (f32[8,128]{1,0:T(8,128)}, f32[8,128]{1,0:T(8,128)S(1)}, u32[]{:S(2)}, u32[]{:S(2)}) collective-permute-start(f32[8,128]{1,0:T(8,128)} %get-tuple-element.59), channel_id=1, source_target_pairs={{0,16},{16,0},{32,48},{48,32},{64,80},{80,64},{96,112},{112,96},{1... | collective-permute-start | bytes 12296 | tf_op jit(solution)/shard_map/ppermute | solution.py:406
  166.0 12.6 %collective-permute-start.10 = (f32[8,128]{1,0:T(8,128)S(1)}, f32[8,128]{1,0:T(8,128)S(1)}, u32[]{:S(2)}, u32[]{:S(2)}) collective-permute-start(f32[8,128]{1,0:T(8,128)S(1)} %add.70), channel_id=1, source_target_pairs={{0,96},{16,112},{32,64},{48,80},{64,32},{80,48},{96,0},{112,16},{1... | collective-permute-start | bytes 12296 | tf_op jit(solution)/shard_map/ppermute | solution.py:406
  167.8 10.8 %collective-permute-start.9 = (f32[8,128]{1,0:T(8,128)S(1)}, f32[8,128]{1,0:T(8,128)S(1)}, u32[]{:S(2)}, u32[]{:S(2)}) collective-permute-start(f32[8,128]{1,0:T(8,128)S(1)} %add.70), channel_id=1, source_target_pairs={{0,64},{16,80},{32,96},{48,112},{64,0},{80,16},{96,32},{112,48},{1... | collective-permute-start | bytes 12296 | tf_op jit(solution)/shard_map/ppermute | solution.py:406
  169.0 9.6 %collective-permute-start.8 = (f32[8,128]{1,0:T(8,128)S(1)}, f32[8,128]{1,0:T(8,128)S(1)}, u32[]{:S(2)}, u32[]{:S(2)}) collective-permute-start(f32[8,128]{1,0:T(8,128)S(1)} %add.70), channel_id=1, source_target_pairs={{0,32},{16,48},{32,0},{48,16},{64,96},{80,112},{96,64},{112,80},{1... | collective-permute-start | bytes 12296 | tf_op jit(solution)/shard_map/ppermute | solution.py:406

commit v7 on v6

--- a/solution.py
+++ b/solution.py
@@ -431,13 +431,11 @@
     start = slab_index * ROWS
     own_x = lax.dynamic_slice_in_dim(basis_x, start, ROWS, 0)
 
-    own_shift = own_rho * lax.dynamic_slice_in_dim(eigen_y, start, ROWS, 0)
-    shift = exchange(jnp.broadcast_to(own_shift, (SLABS, ROWS))).reshape(N)
-
     part1 = forward(source, coarse, 1, basis_y, basis_z)
-    part1, shift = lax.optimization_barrier((part1, shift))
     lines = exchange(part1)
 
+    shift = own_rho * eigen_y
+    own_shift = lax.dynamic_slice_in_dim(shift, start, ROWS, 0)
     base_xz = own_rho * (eigen_x[:, None] + eigen_z[None, :])
     ends = jnp.stack([basis_z[0], basis_z[N - 1]])
     gram_x, gram_y = grams(basis_x, basis_y)

time: 191 us -> 188 us (0.984)
  starting transfers between devices: 40.3 us -> 33.2 us
  waiting for transfers between devices: 11.4 us -> 17.5 us
    all_to_all x4 -> x3, waiting for transfers between devices: 5.55 us -> 14.2 us  [exchange(): lax.all_to_all(block, 'slab', split_axis=0, concat_axis=0, tiled=True)]
    all_to_all x4 -> x3, starting transfers between devices: 30.2 us -> 23.1 us  [exchange(): lax.all_to_all(block, 'slab', split_axis=0, concat_axis=0, tiled=True)]
    ppermute x3, waiting for transfers between devices: 5.78 us -> 3.24 us  [from_behind(): return lax.ppermute(block, axis, route)]
  transfers between devices with their start and end apart: 15 -> 14, of which waited for: 4 -> 4; matrix products, arithmetic and copies ran while one was open for 5% -> 6% of each run, Pallas kernels for 50% -> 46%
where the time goes in v7:
time: 188 us; the launch traced here: 185 us
  Pallas kernels  104 us (55%)
  starting transfers between devices  33.2 us (18%)
  waiting for transfers between devices  17.5 us (9%)
  blocking collectives  15.1 us (8%)
  other arithmetic  7.66 us (4%)
  local copies, waits for them, and re-layouts  4.07 us (2%)
  between operations  3.34 us (2%)
    pallas_call x1, Pallas kernels, faces(): pl.pallas_call(faces_kernel, grid=(SLABS,), in_specs=[smem(), smem(), who...  28.7 us
    pallas_call x3, Pallas kernels, extra(): pl.pallas_call(functools.partial(extra_kernel, part), grid=(stop - skip,)...  26.5 us
    all_to_all x3, starting transfers between devices, exchange(): lax.all_to_all(block, 'slab', split_axis=0, concat_axis=0, tiled=True)  23.1 us
    pallas_call x2, Pallas kernels, forward(): pl.pallas_call(forward_kernel, grid=(ROWS // GROUP,), in_specs=[pl.BlockS...  20.1 us
    all_to_all x1, blocking collectives, exchange(): lax.all_to_all(block, 'slab', split_axis=0, concat_axis=0, tiled=True)  15.1 us
    all_to_all x3, waiting for transfers between devices, exchange(): lax.all_to_all(block, 'slab', split_axis=0, concat_axis=0, tiled=True)  14.2 us
    pallas_call x1, Pallas kernels, backward(): pl.pallas_call(backward_kernel, grid=(ROWS // GROUP,), in_specs=[whole((8...  9.26 us
    ppermute x8, starting transfers between devices, from_partner(): return lax.ppermute(sums, 'sub', [(i, i ^ bits) for i in range(8)])  8.82 us
  transfers between devices with their start and end apart: 14, of which 4 were waited for; matrix products, arithmetic and copies ran while one was open for 6% of the time, Pallas kernels for 46%

profile of v7, /device:TPU:6, one launch (start us, length us, event | category | flops | bytes accessed | tf_op | source)
XLA Modules:
  0.0 185.2 jit_solution(16101439874107594601)
XLA Ops:
  0.6 10.1 %forward.3.part1 = f32[16,2,16,16,128]{4,3,2,1,0:T(8,128)} custom-call(f32[16,256,256]{2,1,0:T(8,128)} %bitcast.10, f32[2,1,16,256,256]{4,3,2,1,0:T(8,128)} %coarse.3, f32[256,256]{1,0:T(8,128)} %basis_y.11, f32[256,256]{1,0:T(8,128)} %basis_z.7), custom_call_target="tpu_custom_call" | custom-call | flops 3221225472 | bytes 12582912 | tf_op jit(solution)/shard_map/forward/pallas_call | solution.py:75
  10.8 8.2 %all-to-all-start = ((f32[16,2,16,16,128]{4,3,2,1,0:T(8,128)}), f32[16,2,16,16,128]{4,3,2,1,0:T(8,128)}, u32[]{:S(2)}, u32[]{:S(2)}) async-start(f32[16,2,16,16,128]{4,3,2,1,0:T(8,128)} %forward.3.part1), calls=%async_computation | async-start | bytes 8388608 | tf_op jit(solution)/shard_map/all_to_all | solution.py:418
  19.0 0.7 fusion.1
  19.7 1.3 constant_dynamic-slice_fusion.own_x
  21.0 1.2 broadcast_multiply_fusion.shift
  22.2 10.0 %forward.2.part0 = f32[16,2,16,16,128]{4,3,2,1,0:T(8,128)} custom-call(f32[16,256,256]{2,1,0:T(8,128)} %bitcast.11, f32[2,1,16,256,256]{4,3,2,1,0:T(8,128)} %coarse.3, f32[256,256]{1,0:T(8,128)} %basis_y.11, f32[256,256]{1,0:T(8,128)} %basis_z.7), custom_call_target="tpu_custom_call" | custom-call | flops 3221225472 | bytes 12582912 | tf_op jit(solution)/shard_map/forward/pallas_call | solution.py:75
  32.2 28.7 %faces.1 = (f32[16,5,16,256]{3,2,1,0:T(8,128)}, f32[16,2,16,256]{3,2,1,0:T(8,128)}) custom-call(f32[1]{0:T(128)} %get-tuple-element.70.own_rho, f32[256]{0:T(256)} %broadcast_multiply_fusion.shift, f32[1,256]{1,0:T(1,128)} %bitcast.12, f32[1,256]{1,0:T(1,128)} %bitcast.13, f32[16,256]{1,0:T(8,128)} %constant_dynamic-slice_fusion.own_x, f32[256,256]{1,0:T(8,128)} %basis_z.7, ...), custom_call_target="tpu_custom_call" | custom-call | flops 16777216 | bytes 65536 | tf_op jit(solution)/shard_map/faces/pallas_call | solution.py:239
  60.9 0.0 collective-permute-start
  60.9 2.6 %grams.1 = (f32[256,256]{1,0:T(8,128)}, f32[256,256]{1,0:T(8,128)}) custom-call(f32[256,256]{1,0:T(8,128)} %basis_x.3, f32[256,256]{1,0:T(8,128)} %basis_y.11), custom_call_target="tpu_custom_call" | custom-call | tf_op jit(solution)/shard_map/grams/pallas_call | solution.py:394
  63.5 0.7 fusion
  64.2 0.5 pad_maximum_fusion.ends
  64.7 1.4 add_multiply_fusion.base
  66.2 1.7 collective-permute-done
  67.9 1.9 %slice_subtract_fusion = f32[16,2,16,256]{3,2,1,0:T(8,128)} fusion(f32[16,2,16,256]{3,2,1,0:T(8,128)S(1)} %collective-permute-done, f32[16,5,16,256]{3,2,1,0:T(8,128)} %get-tuple-element.35.pieces), kind=kLoop, calls=%fused_computation | loop fusion | flops 131072 | bytes 1572864 | tf_op jit(solution)/shard_map/sub | solution.py:447
  69.9 12.1 %all-to-all-done.lines = f32[16,2,16,16,128]{4,3,2,1,0:T(8,128)} async-done(((f32[16,2,16,16,128]{4,3,2,1,0:T(8,128)}), f32[16,2,16,16,128]{4,3,2,1,0:T(8,128)}, u32[]{:S(2)}, u32[]{:S(2)}) %all-to-all-start) | async-done | bytes 4194336 | tf_op jit(solution)/shard_map/all_to_all | solution.py:418
  81.9 10.2 %all-to-all-start.1 = ((f32[16,2,16,256]{3,2,1,0:T(8,128)}), f32[16,2,16,256]{3,2,1,0:T(8,128)S(1)}, u32[]{:S(2)}, u32[]{:S(2)}) async-start(f32[16,2,16,256]{3,2,1,0:T(8,128)} %slice_subtract_fusion), calls=%async_computation.1 | async-start | bytes 1048576 | tf_op jit(solution)/shard_map/all_to_all | solution.py:418
  92.1 0.6 dynamic_slice.15.shift
  92.7 7.4 %middle.1 = f32[16,2,16,16,128]{4,3,2,1,0:T(8,128)} custom-call(f32[256,256]{1,0:T(8,128)} %add_multiply_fusion.base, f32[16]{0:T(128)} %dynamic_slice.15.shift, f32[256,256]{1,0:T(8,128)} %basis_x.3, f32[16,2,16,16,128]{4,3,2,1,0:T(8,128)} %all-to-all-done.lines), custom_call_target="tpu_custom_call" | custom-call | flops 3221225472 | bytes 8388608 | tf_op jit(solution)/shard_map/middle/pallas_call | solution.py:117
  100.1 2.1 %all-to-all-done.1 = f32[16,2,16,256]{3,2,1,0:T(8,128)S(1)} async-done(((f32[16,2,16,256]{3,2,1,0:T(8,128)}), f32[16,2,16,256]{3,2,1,0:T(8,128)S(1)}, u32[]{:S(2)}, u32[]{:S(2)}) %all-to-all-start.1) | async-done | bytes 524320 | tf_op jit(solution)/shard_map/all_to_all | solution.py:418
  102.2 0.1 broadcast_in_dim.25
  102.3 15.1 %all_to_all.20.jumps = f32[16,2,16,256]{3,2,1,0:T(8,128)} all-to-all(f32[16,2,16,256]{3,2,1,0:T(8,128)S(1)} %broadcast_in_dim.25), channel_id=1, replica_groups=mesh['sub'=8,'slab'=16] {'slab'}, dimensions={0} | all-to-all | bytes 1048576 | tf_op jit(solution)/shard_map/all_to_all | solution.py:418
  117.4 4.7 %all-to-all-start.3 = ((f32[16,2,16,16,128]{4,3,2,1,0:T(8,128)}), f32[16,2,16,16,128]{4,3,2,1,0:T(8,128)}, u32[]{:S(2)}, u32[]{:S(2)}) async-start(f32[16,2,16,16,128]{4,3,2,1,0:T(8,128)} %middle.1), calls=%async_computation.3 | async-start | bytes 8388608 | tf_op jit(solution)/shard_map/all_to_all | solution.py:418
  123.4 4.3 %chain0.1 = (f32[16,256]{1,0:T(8,128)}, f32[256,256]{1,0:T(8,128)}, f32[8,128]{1,0:T(8,128)}) custom-call(f32[1]{0:T(128)} %bitcast.2.scale, f32[16,2,16,256]{3,2,1,0:T(8,128)} %all_to_all.20.jumps, f32[256,256]{1,0:T(8,128)} %get-tuple-element.45.gram_x, f32[256,256]{1,0:T(8,128)} %get-tuple-element.46.gram_y, f32[256,256]{1,0:T(8,128)} %stiff.3, ...), custom_call_target="tpu_custom_call" | custom-call | flops 16777216 | bytes 65536 | tf_op jit(solution)/shard_map/chain0/pallas_call | solution.py:341
  129.0 0.6 collective-permute-start.2
  129.6 0.6 pad_maximum_fusion.1.scale
  130.3 1.2 collective-permute-start.6
  131.5 0.0 collective-permute-done.2
  131.5 0.7 add.66
  132.2 1.5 collective-permute-done.1.before
  133.7 1.3 collective-permute-start.4
  135.1 2.1 %collective-permute-start.5 = (f32[8,128]{1,0:T(8,128)S(1)}, f32[8,128]{1,0:T(8,128)S(1)}, u32[]{:S(2)}, u32[]{:S(2)}) collective-permute-start(f32[8,128]{1,0:T(8,128)S(1)} %add.66), channel_id=1, source_target_pairs={{0,96},{16,112},{32,64},{48,80},{64,32},{80,48},{96,0},{112,16},{1... | collective-permute-start | bytes 12296 | tf_op jit(solution)/shard_map/ppermute | solution.py:406
  137.2 0.1 collective-permute-start.3
  137.2 9.7 %extra0.1.refs_0_ = f32[16,2,16,16,128]{4,3,2,1,0:T(8,128)} custom-call(f32[256,256]{1,0:T(8,128)} %add_multiply_fusion.base, f32[256]{0:T(256)} %broadcast_multiply_fusion.shift, f32[16,256]{1,0:T(8,128)} %constant_dynamic-slice_fusion.own_x, f32[2,256]{1,0:T(2,128)} %pad_maximum_fusion.ends, f32[256,256]{1,0:T(8,128)} %get-tuple-element.47.own.image, ...), custom_call_target="tpu_custom_call" | custom-call | flops 8999999488 | bytes 65536 | tf_op jit(solution)/shard_map/extra0/pallas_call | solution.py:283
  147.0 0.0 collective-permute-done.4
  147.0 0.0 collective-permute-done.5
  147.0 0.6 add_add_fusion.1.sums_in.sums0
  147.6 0.7 copy-done.1
  148.3 5.5 %chain1.1 = (f32[8,128]{1,0:T(8,128)}, f32[16,256]{1,0:T(8,128)}, f32[16,256]{1,0:T(8,128)}) custom-call(f32[2]{0:T(128)} %pad_maximum_fusion.1.scale, f32[8,128]{1,0:T(8,128)} %add_add_fusion.1.sums_in.sums0, f32[16,2,16,256]{3,2,1,0:T(8,128)} %all_to_all.20.jumps, f32[256,256]{1,0:T(8,128)} %get-tuple-element.47.own.image, f32[256,256]{1,0:T(8,128)} %copy-done, ...), custom_call_target="tpu_custom_call" | custom-call | flops 16777216 | bytes 65536 | tf_op jit(solution)/shard_map/chain1/pallas_call | solution.py:371
  153.8 0.0 collective-permute-start.7
  153.8 8.4 %extra1.1.refs_0_ = f32[16,2,16,16,128]{4,3,2,1,0:T(8,128)} custom-call(f32[256,256]{1,0:T(8,128)} %add_multiply_fusion.base, f32[256]{0:T(256)} %broadcast_multiply_fusion.shift, f32[16,256]{1,0:T(8,128)} %constant_dynamic-slice_fusion.own_x, f32[2,256]{1,0:T(2,128)} %pad_maximum_fusion.ends, ...), custom_call_target="tpu_custom_call", output_to_operand_aliasing={{}: (6, {})} | custom-call | flops 7500000256 | bytes 65536 | tf_op jit(solution)/shard_map/extra1/pallas_call | solution.py:283
  162.2 2.6 %collective-permute-start.9 = (f32[8,128]{1,0:T(8,128)S(1)}, f32[8,128]{1,0:T(8,128)S(1)}, u32[]{:S(2)}, u32[]{:S(2)}) collective-permute-start(f32[8,128]{1,0:T(8,128)S(1)} %add.70), channel_id=1, source_target_pairs={{0,64},{16,80},{32,96},{48,112},{64,0},{80,16},{96,32},{112,48},{1... | collective-permute-start | bytes 12296 | tf_op jit(solution)/shard_map/ppermute | solution.py:406
  164.8 2.1 %collective-permute-start.10 = (f32[8,128]{1,0:T(8,128)S(1)}, f32[8,128]{1,0:T(8,128)S(1)}, u32[]{:S(2)}, u32[]{:S(2)}) collective-permute-start(f32[8,128]{1,0:T(8,128)S(1)} %add.70), channel_id=1, source_target_pairs={{0,96},{16,112},{32,64},{48,80},{64,32},{80,48},{96,0},{112,16},{1... | collective-permute-start | bytes 12296 | tf_op jit(solution)/shard_map/ppermute | solution.py:406
  166.9 0.0 collective-permute-start.8
  166.9 8.4 %extra2.1.extra = f32[16,2,16,16,128]{4,3,2,1,0:T(8,128)} custom-call(f32[256,256]{1,0:T(8,128)} %add_multiply_fusion.base, f32[256]{0:T(256)} %broadcast_multiply_fusion.shift, f32[16,256]{1,0:T(8,128)} %constant_dynamic-slice_fusion.own_x, f32[2,256]{1,0:T(2,128)} %pad_maximum_fusion.ends, ...), custom_call_target="tpu_custom_call", output_to_operand_aliasing={{}: (6, {})} | custom-call | flops 7500000256 | bytes 65536 | tf_op jit(solution)/shard_map/extra2/pallas_call | solution.py:283
  175.3 0.0 collective-permute-done.8
  175.3 0.6 add_add_fusion.sums1
  175.9 0.0 all-to-all-done.3.field
  175.9 9.3 %backward.1 = (f32[16,256,256]{2,1,0:T(8,128)}, f32[16,256]{1,0:T(8,128)}) custom-call(f32[8,128]{1,0:T(8,128)} %add_add_fusion.1.sums_in.sums0, f32[8,128]{1,0:T(8,128)} %add_add_fusion.sums1, f32[16,256]{1,0:T(8,128)} %get-tuple-element.60.first, f32[16,256]{1,0:T(8,128)} %get-tuple-element.61.change, f32[16,2,16,16,128]{4,3,2,1,0:T(8,128)} %all-to-all-done.3.field, ...), custom_call_target="tpu_custom_call" | custom-call | flops 3221225472 | bytes 12582912 | tf_op jit(solution)/shard_map/backward/pallas_call | solution.py:162
  (23 shorter events, 0.1 us)
Async XLA Ops:
  10.8 8.3 %copy-start.6 = (f32[8]{0:T(128)S(1)}, f32[8]{0:T(128)}, u32[]{:S(2)}) copy-start(f32[8]{0:T(128)} %param.12) | copy-start | bytes 100
  10.8 10.3 %copy-start.7 = (f32[256]{0:T(256)S(1)}, f32[256]{0:T(256)}, u32[]{:S(2)}) copy-start(f32[256]{0:T(256)} %param.17) | copy-start | bytes 3076
  10.8 71.2 %all-to-all-start = ((f32[16,2,16,16,128]{4,3,2,1,0:T(8,128)}), f32[16,2,16,16,128]{4,3,2,1,0:T(8,128)}, u32[]{:S(2)}, u32[]{:S(2)}) async-start(f32[16,2,16,16,128]{4,3,2,1,0:T(8,128)} %forward.3.part1), calls=%async_computation | async-start | bytes 8388608 | tf_op jit(solution)/shard_map/all_to_all | solution.py:418
  32.2 32.5 %copy-start.3 = (f32[256]{0:T(256)S(1)}, f32[256]{0:T(256)}, u32[]{:S(2)}) copy-start(f32[256]{0:T(256)} %param.16) | copy-start | bytes 3076
  32.2 32.5 %copy-start.4 = (f32[256]{0:T(256)S(1)}, f32[256]{0:T(256)}, u32[]{:S(2)}) copy-start(f32[256]{0:T(256)} %param.18) | copy-start | bytes 3076
  32.2 59.9 %copy-start.5 = (f32[256]{0:T(256)S(1)}, f32[256]{0:T(256)}, u32[]{:S(2)}) copy-start(f32[256]{0:T(256)} %broadcast_multiply_fusion.shift) | copy-start | bytes 3076
  60.9 7.0 %collective-permute-start = (f32[16,2,16,256]{3,2,1,0:T(8,128)}, f32[16,2,16,256]{3,2,1,0:T(8,128)S(1)}, u32[]{:S(2)}, u32[]{:S(2)}) collective-permute-start(f32[16,2,16,256]{3,2,1,0:T(8,128)} %get-tuple-element.36), channel_id=1, source_target_pairs={{16,0},{32,16},{48,32},{64,48},{80,64},{96,80},{112,96},{0,112},{1... | collective-permute-start | bytes 1572872 | tf_op jit(solution)/shard_map/ppermute | solution.py:402
  81.9 20.3 %all-to-all-start.1 = ((f32[16,2,16,256]{3,2,1,0:T(8,128)}), f32[16,2,16,256]{3,2,1,0:T(8,128)S(1)}, u32[]{:S(2)}, u32[]{:S(2)}) async-start(f32[16,2,16,256]{3,2,1,0:T(8,128)} %slice_subtract_fusion), calls=%async_computation.1 | async-start | bytes 1048576 | tf_op jit(solution)/shard_map/all_to_all | solution.py:418
  117.4 58.5 %all-to-all-start.3 = ((f32[16,2,16,16,128]{4,3,2,1,0:T(8,128)}), f32[16,2,16,16,128]{4,3,2,1,0:T(8,128)}, u32[]{:S(2)}, u32[]{:S(2)}) async-start(f32[16,2,16,16,128]{4,3,2,1,0:T(8,128)} %middle.1), calls=%async_computation.3 | async-start | bytes 8388608 | tf_op jit(solution)/shard_map/all_to_all | solution.py:418
  127.7 6.0 %collective-permute-start.1 = (f32[256,256]{1,0:T(8,128)}, f32[256,256]{1,0:T(8,128)S(1)}, u32[]{:S(2)}, u32[]{:S(2)}) collective-permute-start(f32[256,256]{1,0:T(8,128)} %get-tuple-element.47.own.image), channel_id=1, source_target_pairs={{112,0},{0,16},{16,32},{32,48},{48,64},{64,80},{80,96},{96,112},{1... | collective-permute-start | bytes 786440 | tf_op jit(solution)/shard_map/ppermute | solution.py:402
  129.0 2.5 %collective-permute-start.2 = (f32[8,128]{1,0:T(8,128)}, f32[8,128]{1,0:T(8,128)S(1)}, u32[]{:S(2)}, u32[]{:S(2)}) collective-permute-start(f32[8,128]{1,0:T(8,128)} %get-tuple-element.48), channel_id=1, source_target_pairs={{0,16},{16,0},{32,48},{48,32},{64,80},{80,64},{96,112},{112,96},{1... | collective-permute-start | bytes 12296 | tf_op jit(solution)/shard_map/ppermute | solution.py:406
  130.3 17.3 %collective-permute-start.6 = (f32[256,256]{1,0:T(8,128)}, f32[256,256]{1,0:T(8,128)S(1)}, u32[]{:S(2)}, u32[]{:S(2)}) collective-permute-start(f32[256,256]{1,0:T(8,128)} %get-tuple-element.47.own.image), channel_id=1, source_target_pairs={{16,0},{32,16},{48,32},{64,48},{80,64},{96,80},{112,96},{0,112},{1... | collective-permute-start | bytes 786440 | tf_op jit(solution)/shard_map/ppermute | solution.py:402
  133.7 3.5 %copy-start = (f32[256,256]{1,0:T(8,128)}, f32[256,256]{1,0:T(8,128)S(1)}, u32[]{:S(2)}) copy-start(f32[256,256]{1,0:T(8,128)S(1)} %collective-permute-done.1.before) | copy-start | bytes 786436
  133.7 13.2 %collective-permute-start.4 = (f32[8,128]{1,0:T(8,128)S(1)}, f32[8,128]{1,0:T(8,128)S(1)}, u32[]{:S(2)}, u32[]{:S(2)}) collective-permute-start(f32[8,128]{1,0:T(8,128)S(1)} %add.66), channel_id=1, source_target_pairs={{0,64},{16,80},{32,96},{48,112},{64,0},{80,16},{96,32},{112,48},{1... | collective-permute-start | bytes 12296 | tf_op jit(solution)/shard_map/ppermute | solution.py:406
  135.1 11.9 %collective-permute-start.5 = (f32[8,128]{1,0:T(8,128)S(1)}, f32[8,128]{1,0:T(8,128)S(1)}, u32[]{:S(2)}, u32[]{:S(2)}) collective-permute-start(f32[8,128]{1,0:T(8,128)S(1)} %add.66), channel_id=1, source_target_pairs={{0,96},{16,112},{32,64},{48,80},{64,32},{80,48},{96,0},{112,16},{1... | collective-permute-start | bytes 12296 | tf_op jit(solution)/shard_map/ppermute | solution.py:406
  137.2 9.8 %collective-permute-start.3 = (f32[8,128]{1,0:T(8,128)S(1)}, f32[8,128]{1,0:T(8,128)S(1)}, u32[]{:S(2)}, u32[]{:S(2)}) collective-permute-start(f32[8,128]{1,0:T(8,128)S(1)} %add.66), channel_id=1, source_target_pairs={{0,32},{16,48},{32,0},{48,16},{64,96},{80,112},{96,64},{112,80},{1... | collective-permute-start | bytes 12296 | tf_op jit(solution)/shard_map/ppermute | solution.py:406
  147.6 0.7 copy-start.1
  153.8 8.4 %copy-start.2 = (f32[8,128]{1,0:T(8,128)S(1)}, f32[8,128]{1,0:T(8,128)}, u32[]{:S(2)}) copy-start(f32[8,128]{1,0:T(8,128)} %get-tuple-element.55) | copy-start | bytes 12292
  153.8 8.4 %collective-permute-start.7 = (f32[8,128]{1,0:T(8,128)}, f32[8,128]{1,0:T(8,128)S(1)}, u32[]{:S(2)}, u32[]{:S(2)}) collective-permute-start(f32[8,128]{1,0:T(8,128)} %get-tuple-element.55), channel_id=1, source_target_pairs={{0,16},{16,0},{32,48},{48,32},{64,80},{80,64},{96,112},{112,96},{1... | collective-permute-start | bytes 12296 | tf_op jit(solution)/shard_map/ppermute | solution.py:406
  162.2 13.1 %collective-permute-start.9 = (f32[8,128]{1,0:T(8,128)S(1)}, f32[8,128]{1,0:T(8,128)S(1)}, u32[]{:S(2)}, u32[]{:S(2)}) collective-permute-start(f32[8,128]{1,0:T(8,128)S(1)} %add.70), channel_id=1, source_target_pairs={{0,64},{16,80},{32,96},{48,112},{64,0},{80,16},{96,32},{112,48},{1... | collective-permute-start | bytes 12296 | tf_op jit(solution)/shard_map/ppermute | solution.py:406
  164.8 10.5 %collective-permute-start.10 = (f32[8,128]{1,0:T(8,128)S(1)}, f32[8,128]{1,0:T(8,128)S(1)}, u32[]{:S(2)}, u32[]{:S(2)}) collective-permute-start(f32[8,128]{1,0:T(8,128)S(1)} %add.70), channel_id=1, source_target_pairs={{0,96},{16,112},{32,64},{48,80},{64,32},{80,48},{96,0},{112,16},{1... | collective-permute-start | bytes 12296 | tf_op jit(solution)/shard_map/ppermute | solution.py:406
  166.9 8.4 %collective-permute-start.8 = (f32[8,128]{1,0:T(8,128)S(1)}, f32[8,128]{1,0:T(8,128)S(1)}, u32[]{:S(2)}, u32[]{:S(2)}) collective-permute-start(f32[8,128]{1,0:T(8,128)S(1)} %add.70), channel_id=1, source_target_pairs={{0,32},{16,48},{32,0},{48,16},{64,96},{80,112},{96,64},{112,80},{1... | collective-permute-start | bytes 12296 | tf_op jit(solution)/shard_map/ppermute | solution.py:406

commit v8 on v7

--- a/solution.py
+++ b/solution.py
@@ -163,8 +163,8 @@
         backward_kernel,
         grid=(ROWS // GROUP,),
         in_specs=[
-            whole((8, 128)),
-            whole((8, 128)),
+            whole((8, N)),
+            whole((8, N)),
             whole((ROWS, N)),
             whole((ROWS, N)),
             block,
@@ -324,24 +324,25 @@
 
 
 def scalars_block(upper, lower):
-    at = lax.broadcasted_iota(jnp.int32, (8, 128), 0)
+    at = lax.broadcasted_iota(jnp.int32, (8, N), 0)
     return jnp.where(at == 0, upper, jnp.where(at == 1, lower, 0.0))
 
 
-def chain0_kernel(scale, jumps, gram_x, gram_y, stiff, own_x, basis_y, rows, image, sums):
-    search, image[...], upper, lower = precondition(
-        jumps[:, 0].reshape(N, N), gram_x[...], gram_y[...], scale[0] * stiff[...].T
-    )
-    sums[...] = scalars_block(upper, lower)
+def chain0_kernel(weight, jumps, gram_x, gram_y, stiff, own_x, basis_y, rows, image):
+    search, image[0:N], upper, lower = precondition(
+        jumps[:, 0].reshape(N, N), gram_x[...], gram_y[...], weight[...] * stiff[...].T
+    )
+    image[N : N + 8] = scalars_block(upper, lower)
     rows[...] = exact_t(exact_t(own_x[...], search), basis_y[...])
 
 
 def chain0(*args):
-    face = jax.ShapeDtypeStruct((N, N), F32)
     return pl.pallas_call(
         chain0_kernel,
-        in_specs=[smem()] + [pl.BlockSpec(memory_space=pltpu.VMEM)] * 6,
-        out_shape=(jax.ShapeDtypeStruct((ROWS, N), F32), face, jax.ShapeDtypeStruct((8, 128), F32)),
+        out_shape=(
+            jax.ShapeDtypeStruct((ROWS, N), F32),
+            jax.ShapeDtypeStruct((N + 8, N), F32),
+        ),
         compiler_params=params(),
         cost_estimate=pl.CostEstimate(
             flops=N**3, bytes_accessed=N * N, transcendentals=0
@@ -351,16 +352,16 @@
 
 
 def chain1_kernel(
-    scale, sums_in, jumps, image, before, after, pieces, gram_x, gram_y, stiff, own_x, basis_y, sums, out, rows
+    ratio, weight, sums_in, jumps, image, before, after, pieces, gram_x, gram_y, stiff, own_x, basis_y, sums, out, rows
 ):
-    alpha, ratio, weight = step_length(sums_in[...]), scale[0], scale[1]
-    t = image[...]
+    alpha = step_length(sums_in[...])
+    t = image[0:N]
     table = [pieces[:, 2 + pair].reshape(N, N) for pair in range(3)]
-    own = table[1] * before[...] - table[0] * t
-    other = table[2] * t - table[1] * after[...]
-    q = jumps[:, 1].reshape(N, N) + alpha * (own - ratio * other)
+    own = table[1] * before[0:N] - table[0] * t
+    other = table[2] * t - table[1] * after[0:N]
+    q = jumps[:, 1].reshape(N, N) + alpha * (own - ratio[...] * other)
     search, _, upper, lower = precondition(
-        q, gram_x[...], gram_y[...], weight * stiff[...].T
+        q, gram_x[...], gram_y[...], weight[...] * stiff[...].T
     )
     sums[...] = scalars_block(upper, lower)
     out[...] = exact_t(exact_t(own_x[...], q), basis_y[...])
@@ -370,9 +371,8 @@
 def chain1(*args):
     return pl.pallas_call(
         chain1_kernel,
-        in_specs=[smem()] + [pl.BlockSpec(memory_space=pltpu.VMEM)] * 11,
         out_shape=(
-            jax.ShapeDtypeStruct((8, 128), F32),
+            jax.ShapeDtypeStruct((8, N), F32),
             jax.ShapeDtypeStruct((ROWS, N), F32),
             jax.ShapeDtypeStruct((ROWS, N), F32),
         ),
@@ -456,21 +456,21 @@
     spread, jumps = lax.optimization_barrier((spread, jumps))
     spread = exchange(spread)
 
-    first, image0, sums0 = chain0(
-        weight.reshape(1), jumps, gram_x, gram_y, face_stiff, own_x, basis_y
+    first, image0 = chain0(
+        weight.reshape(1, 1), jumps, gram_x, gram_y, face_stiff, own_x, basis_y
     )
     before = from_behind(image0, "sub", 1)
     after = from_behind(image0, "sub", -1)
 
     terms = functools.partial(extra, base=base_xz, shift=shift, own_x=own_x, ends=ends)
-    sums0 = over_pair(sums0)
+    sums0 = image0[N:] + before[N:]
     before, sums0 = lax.optimization_barrier((before, sums0))
     more = terms(0, own=image0, before=before)
     sums0, more = lax.optimization_barrier((over_pairs(sums0), more))
 
-    scale = jnp.stack([own_rho / next_rho, weight])
     sums1, jump, change = chain1(
-        scale,
+        (own_rho / next_rho).reshape(1, 1),
+        weight.reshape(1, 1),
         sums0,
         jumps,
         image0,

time: 188 us -> 189 us (level)
    ppermute x8 -> x7, starting transfers between devices: 8.82 us -> 8.21 us  [from_partner(): return lax.ppermute(sums, 'sub', [(i, i ^ bits) for i in range(8)])]
  transfers between devices with their start and end apart: 14 -> 13, of which waited for: 4 -> 4; matrix products, arithmetic and copies ran while one was open for 6% -> 6% of each run, Pallas kernels for 46% -> 46%
where the time goes in v8:
time: 189 us; the launch traced here: 186 us
  Pallas kernels  105 us (56%)
  starting transfers between devices  33.1 us (18%)
  waiting for transfers between devices  18.7 us (10%)
  blocking collectives  15.2 us (8%)
  other arithmetic  7.13 us (4%)
  local copies, waits for them, and re-layouts  4.14 us (2%)
  between operations  3.45 us (2%)
    pallas_call x1, Pallas kernels, faces(): pl.pallas_call(faces_kernel, grid=(SLABS,), in_specs=[smem(), smem(), who...  28.7 us
    pallas_call x3, Pallas kernels, extra(): pl.pallas_call(functools.partial(extra_kernel, part), grid=(stop - skip,)...  26.6 us
    all_to_all x3, starting transfers between devices, exchange(): lax.all_to_all(block, 'slab', split_axis=0, concat_axis=0, tiled=True)  23.1 us
    pallas_call x2, Pallas kernels, forward(): pl.pallas_call(forward_kernel, grid=(ROWS // GROUP,), in_specs=[pl.BlockS...  20.1 us
    all_to_all x1, blocking collectives, exchange(): lax.all_to_all(block, 'slab', split_axis=0, concat_axis=0, tiled=True)  15.2 us
    all_to_all x3, waiting for transfers between devices, exchange(): lax.all_to_all(block, 'slab', split_axis=0, concat_axis=0, tiled=True)  14 us
    pallas_call x1, Pallas kernels, backward(): pl.pallas_call(backward_kernel, grid=(ROWS // GROUP,), in_specs=[whole((8...  9.32 us
    ppermute x7, starting transfers between devices, from_partner(): return lax.ppermute(sums, 'sub', [(i, i ^ bits) for i in range(8)])  8.21 us
  transfers between devices with their start and end apart: 13, of which 4 were waited for; matrix products, arithmetic and copies ran while one was open for 6% of the time, Pallas kernels for 46%

profile of v8, /device:TPU:6, one launch (start us, length us, event | category | flops | bytes accessed | tf_op | source)
XLA Modules:
  0.0 186.4 jit_solution(14217698956434920314)
XLA Ops:
  0.6 10.1 %forward.3.part1 = f32[16,2,16,16,128]{4,3,2,1,0:T(8,128)} custom-call(f32[16,256,256]{2,1,0:T(8,128)} %bitcast.10, f32[2,1,16,256,256]{4,3,2,1,0:T(8,128)} %coarse.3, f32[256,256]{1,0:T(8,128)} %basis_y.11, f32[256,256]{1,0:T(8,128)} %basis_z.7), custom_call_target="tpu_custom_call" | custom-call | flops 3221225472 | bytes 12582912 | tf_op jit(solution)/shard_map/forward/pallas_call | solution.py:75
  10.8 8.2 %all-to-all-start = ((f32[16,2,16,16,128]{4,3,2,1,0:T(8,128)}), f32[16,2,16,16,128]{4,3,2,1,0:T(8,128)}, u32[]{:S(2)}, u32[]{:S(2)}) async-start(f32[16,2,16,16,128]{4,3,2,1,0:T(8,128)} %forward.3.part1), calls=%async_computation | async-start | bytes 8388608 | tf_op jit(solution)/shard_map/all_to_all | solution.py:418
  19.0 0.7 fusion.1
  19.7 1.3 constant_dynamic-slice_fusion.own_x
  21.0 1.2 broadcast_multiply_fusion.shift
  22.2 10.0 %forward.2.part0 = f32[16,2,16,16,128]{4,3,2,1,0:T(8,128)} custom-call(f32[16,256,256]{2,1,0:T(8,128)} %bitcast.11, f32[2,1,16,256,256]{4,3,2,1,0:T(8,128)} %coarse.3, f32[256,256]{1,0:T(8,128)} %basis_y.11, f32[256,256]{1,0:T(8,128)} %basis_z.7), custom_call_target="tpu_custom_call" | custom-call | flops 3221225472 | bytes 12582912 | tf_op jit(solution)/shard_map/forward/pallas_call | solution.py:75
  32.2 28.7 %faces.1 = (f32[16,5,16,256]{3,2,1,0:T(8,128)}, f32[16,2,16,256]{3,2,1,0:T(8,128)}) custom-call(f32[1]{0:T(128)} %get-tuple-element.68.own_rho, f32[256]{0:T(256)} %broadcast_multiply_fusion.shift, f32[1,256]{1,0:T(1,128)} %bitcast.12, f32[1,256]{1,0:T(1,128)} %bitcast.13, f32[16,256]{1,0:T(8,128)} %constant_dynamic-slice_fusion.own_x, f32[256,256]{1,0:T(8,128)} %basis_z.7, ...), custom_call_target="tpu_custom_call" | custom-call | flops 16777216 | bytes 65536 | tf_op jit(solution)/shard_map/faces/pallas_call | solution.py:239
  61.0 0.0 collective-permute-start
  61.0 2.5 %grams.1 = (f32[256,256]{1,0:T(8,128)}, f32[256,256]{1,0:T(8,128)}) custom-call(f32[256,256]{1,0:T(8,128)} %basis_x.3, f32[256,256]{1,0:T(8,128)} %basis_y.11), custom_call_target="tpu_custom_call" | custom-call | tf_op jit(solution)/shard_map/grams/pallas_call | solution.py:394
  63.5 0.7 fusion
  64.2 0.6 pad_maximum_fusion.ends
  64.8 1.5 add_multiply_fusion.base
  66.3 1.7 collective-permute-done
  68.0 1.9 %slice_subtract_fusion = f32[16,2,16,256]{3,2,1,0:T(8,128)} fusion(f32[16,2,16,256]{3,2,1,0:T(8,128)S(1)} %collective-permute-done, f32[16,5,16,256]{3,2,1,0:T(8,128)} %get-tuple-element.34.pieces), kind=kLoop, calls=%fused_computation | loop fusion | flops 131072 | bytes 1572864 | tf_op jit(solution)/shard_map/sub | solution.py:447
  69.9 12.0 %all-to-all-done.lines = f32[16,2,16,16,128]{4,3,2,1,0:T(8,128)} async-done(((f32[16,2,16,16,128]{4,3,2,1,0:T(8,128)}), f32[16,2,16,16,128]{4,3,2,1,0:T(8,128)}, u32[]{:S(2)}, u32[]{:S(2)}) %all-to-all-start) | async-done | bytes 4194336 | tf_op jit(solution)/shard_map/all_to_all | solution.py:418
  81.9 10.2 %all-to-all-start.1 = ((f32[16,2,16,256]{3,2,1,0:T(8,128)}), f32[16,2,16,256]{3,2,1,0:T(8,128)S(1)}, u32[]{:S(2)}, u32[]{:S(2)}) async-start(f32[16,2,16,256]{3,2,1,0:T(8,128)} %slice_subtract_fusion), calls=%async_computation.1 | async-start | bytes 1048576 | tf_op jit(solution)/shard_map/all_to_all | solution.py:418
  92.1 0.7 dynamic_slice.15.shift
  92.8 7.4 %middle.1 = f32[16,2,16,16,128]{4,3,2,1,0:T(8,128)} custom-call(f32[256,256]{1,0:T(8,128)} %add_multiply_fusion.base, f32[16]{0:T(128)} %dynamic_slice.15.shift, f32[256,256]{1,0:T(8,128)} %basis_x.3, f32[16,2,16,16,128]{4,3,2,1,0:T(8,128)} %all-to-all-done.lines), custom_call_target="tpu_custom_call" | custom-call | flops 3221225472 | bytes 8388608 | tf_op jit(solution)/shard_map/middle/pallas_call | solution.py:117
  100.2 2.0 %all-to-all-done.1 = f32[16,2,16,256]{3,2,1,0:T(8,128)S(1)} async-done(((f32[16,2,16,256]{3,2,1,0:T(8,128)}), f32[16,2,16,256]{3,2,1,0:T(8,128)S(1)}, u32[]{:S(2)}, u32[]{:S(2)}) %all-to-all-start.1) | async-done | bytes 524320 | tf_op jit(solution)/shard_map/all_to_all | solution.py:418
  102.2 0.1 broadcast_in_dim.25
  102.3 15.2 %all_to_all.20.jumps = f32[16,2,16,256]{3,2,1,0:T(8,128)} all-to-all(f32[16,2,16,256]{3,2,1,0:T(8,128)S(1)} %broadcast_in_dim.25), channel_id=1, replica_groups=mesh['sub'=8,'slab'=16] {'slab'}, dimensions={0} | all-to-all | bytes 1048576 | tf_op jit(solution)/shard_map/all_to_all | solution.py:418
  117.5 4.7 %all-to-all-start.3 = ((f32[16,2,16,16,128]{4,3,2,1,0:T(8,128)}), f32[16,2,16,16,128]{4,3,2,1,0:T(8,128)}, u32[]{:S(2)}, u32[]{:S(2)}) async-start(f32[16,2,16,16,128]{4,3,2,1,0:T(8,128)} %middle.1), calls=%async_computation.3 | async-start | bytes 8388608 | tf_op jit(solution)/shard_map/all_to_all | solution.py:418
  123.5 4.3 %chain0.1 = (f32[16,256]{1,0:T(8,128)}, f32[264,256]{1,0:T(8,128)}) custom-call(f32[1,1]{1,0:T(1,128)} %bitcast.2.weight, f32[16,2,16,256]{3,2,1,0:T(8,128)} %all_to_all.20.jumps, f32[256,256]{1,0:T(8,128)} %get-tuple-element.44.gram_x, f32[256,256]{1,0:T(8,128)} %get-tuple-element.45.gram_y, f32[256,256]{1,0:T(8,128)} %stiff.3, ...), custom_call_target="tpu_custom_call" | custom-call | flops 16777216 | bytes 65536 | tf_op jit(solution)/shard_map/chain0/pallas_call | solution.py:340
  127.9 0.0 collective-permute-start.1
  129.2 1.8 collective-permute-start.5
  131.0 3.0 %collective-permute-done.1.before = f32[264,256]{1,0:T(8,128)S(1)} collective-permute-done((f32[264,256]{1,0:T(8,128)}, f32[264,256]{1,0:T(8,128)S(1)}, u32[]{:S(2)}, u32[]{:S(2)}) %collective-permute-start.1) | collective-permute-done | bytes 270368 | tf_op jit(solution)/shard_map/ppermute | solution.py:402
  134.0 0.7 slice_add_fusion
  134.7 1.3 collective-permute-start.3
  136.0 2.1 %collective-permute-start.4 = (f32[8,256]{1,0:T(8,128)S(1)}, f32[8,256]{1,0:T(8,128)S(1)}, u32[]{:S(2)}, u32[]{:S(2)}) collective-permute-start(f32[8,256]{1,0:T(8,128)S(1)} %slice_add_fusion), channel_id=1, source_target_pairs={{0,96},{16,112},{32,64},{48,80},{64,32},{80,48},{96,0},{112,16},{1... | collective-permute-start | bytes 24584 | tf_op jit(solution)/shard_map/ppermute | solution.py:406
  138.1 0.1 collective-permute-start.2
  138.2 9.7 %extra0.1.refs_0_ = f32[16,2,16,16,128]{4,3,2,1,0:T(8,128)} custom-call(f32[256,256]{1,0:T(8,128)} %add_multiply_fusion.base, f32[256]{0:T(256)} %broadcast_multiply_fusion.shift, f32[16,256]{1,0:T(8,128)} %constant_dynamic-slice_fusion.own_x, f32[2,256]{1,0:T(2,128)} %pad_maximum_fusion.ends, f32[264,256]{1,0:T(8,128)} %get-tuple-element.46.own.image, ...), custom_call_target="tpu_custom_call" | custom-call | flops 8999999488 | bytes 65536 | tf_op jit(solution)/shard_map/extra0/pallas_call | solution.py:283
  147.9 0.0 collective-permute-done.3
  147.9 0.0 collective-permute-done.2
  147.9 0.6 add_add_fusion.1.sums_in.sums0
  148.5 0.7 copy-done.1
  149.2 5.6 %chain1.1 = (f32[8,256]{1,0:T(8,128)}, f32[16,256]{1,0:T(8,128)}, f32[16,256]{1,0:T(8,128)}) custom-call(f32[1,1]{1,0:T(1,128)} %bitcast.6.ratio, f32[1,1]{1,0:T(1,128)} %bitcast.2.weight, f32[8,256]{1,0:T(8,128)} %add_add_fusion.1.sums_in.sums0, f32[16,2,16,256]{3,2,1,0:T(8,128)} %all_to_all.20.jumps, f32[264,256]{1,0:T(8,128)} %get-tuple-element.46.own.image, ...), custom_call_target="tpu_custom_call" | custom-call | flops 16777216 | bytes 65536 | tf_op jit(solution)/shard_map/chain1/pallas_call | solution.py:372
  154.8 0.0 collective-permute-start.6
  154.8 8.4 %extra1.1.refs_0_ = f32[16,2,16,16,128]{4,3,2,1,0:T(8,128)} custom-call(f32[256,256]{1,0:T(8,128)} %add_multiply_fusion.base, f32[256]{0:T(256)} %broadcast_multiply_fusion.shift, f32[16,256]{1,0:T(8,128)} %constant_dynamic-slice_fusion.own_x, f32[2,256]{1,0:T(2,128)} %pad_maximum_fusion.ends, ...), custom_call_target="tpu_custom_call", output_to_operand_aliasing={{}: (6, {})} | custom-call | flops 7500000256 | bytes 65536 | tf_op jit(solution)/shard_map/extra1/pallas_call | solution.py:283
  163.2 0.0 collective-permute-done.6
  163.3 2.6 %collective-permute-start.8 = (f32[8,256]{1,0:T(8,128)S(1)}, f32[8,256]{1,0:T(8,128)S(1)}, u32[]{:S(2)}, u32[]{:S(2)}) collective-permute-start(f32[8,256]{1,0:T(8,128)S(1)} %add.70), channel_id=1, source_target_pairs={{0,64},{16,80},{32,96},{48,112},{64,0},{80,16},{96,32},{112,48},{1... | collective-permute-start | bytes 24584 | tf_op jit(solution)/shard_map/ppermute | solution.py:406
  165.9 2.1 %collective-permute-start.9 = (f32[8,256]{1,0:T(8,128)S(1)}, f32[8,256]{1,0:T(8,128)S(1)}, u32[]{:S(2)}, u32[]{:S(2)}) collective-permute-start(f32[8,256]{1,0:T(8,128)S(1)} %add.70), channel_id=1, source_target_pairs={{0,96},{16,112},{32,64},{48,80},{64,32},{80,48},{96,0},{112,16},{1... | collective-permute-start | bytes 24584 | tf_op jit(solution)/shard_map/ppermute | solution.py:406
  168.0 0.0 collective-permute-start.7
  168.0 8.4 %extra2.1.extra = f32[16,2,16,16,128]{4,3,2,1,0:T(8,128)} custom-call(f32[256,256]{1,0:T(8,128)} %add_multiply_fusion.base, f32[256]{0:T(256)} %broadcast_multiply_fusion.shift, f32[16,256]{1,0:T(8,128)} %constant_dynamic-slice_fusion.own_x, f32[2,256]{1,0:T(2,128)} %pad_maximum_fusion.ends, ...), custom_call_target="tpu_custom_call", output_to_operand_aliasing={{}: (6, {})} | custom-call | flops 7500000256 | bytes 65536 | tf_op jit(solution)/shard_map/extra2/pallas_call | solution.py:283
  176.4 0.0 collective-permute-done.8
  176.4 0.0 collective-permute-done.9
  176.4 0.6 add_add_fusion.sums1
  177.0 0.0 all-to-all-done.3.field
  177.0 9.3 %backward.1 = (f32[16,256,256]{2,1,0:T(8,128)}, f32[16,256]{1,0:T(8,128)}) custom-call(f32[8,256]{1,0:T(8,128)} %add_add_fusion.1.sums_in.sums0, f32[8,256]{1,0:T(8,128)} %add_add_fusion.sums1, f32[16,256]{1,0:T(8,128)} %get-tuple-element.58.first, f32[16,256]{1,0:T(8,128)} %get-tuple-element.59.change, f32[16,2,16,16,128]{4,3,2,1,0:T(8,128)} %all-to-all-done.3.field, ...), custom_call_target="tpu_custom_call" | custom-call | flops 3221225472 | bytes 12582912 | tf_op jit(solution)/shard_map/backward/pallas_call | solution.py:162
  (20 shorter events, 0.1 us)
Async XLA Ops:
  10.8 8.3 %copy-start.6 = (f32[8]{0:T(128)S(1)}, f32[8]{0:T(128)}, u32[]{:S(2)}) copy-start(f32[8]{0:T(128)} %param.12) | copy-start | bytes 100
  10.8 10.3 %copy-start.7 = (f32[256]{0:T(256)S(1)}, f32[256]{0:T(256)}, u32[]{:S(2)}) copy-start(f32[256]{0:T(256)} %param.17) | copy-start | bytes 3076
  10.8 71.2 %all-to-all-start = ((f32[16,2,16,16,128]{4,3,2,1,0:T(8,128)}), f32[16,2,16,16,128]{4,3,2,1,0:T(8,128)}, u32[]{:S(2)}, u32[]{:S(2)}) async-start(f32[16,2,16,16,128]{4,3,2,1,0:T(8,128)} %forward.3.part1), calls=%async_computation | async-start | bytes 8388608 | tf_op jit(solution)/shard_map/all_to_all | solution.py:418
  32.2 32.6 %copy-start.3 = (f32[256]{0:T(256)S(1)}, f32[256]{0:T(256)}, u32[]{:S(2)}) copy-start(f32[256]{0:T(256)} %param.16) | copy-start | bytes 3076
  32.2 32.6 %copy-start.4 = (f32[256]{0:T(256)S(1)}, f32[256]{0:T(256)}, u32[]{:S(2)}) copy-start(f32[256]{0:T(256)} %param.18) | copy-start | bytes 3076
  32.2 59.9 %copy-start.5 = (f32[256]{0:T(256)S(1)}, f32[256]{0:T(256)}, u32[]{:S(2)}) copy-start(f32[256]{0:T(256)} %broadcast_multiply_fusion.shift) | copy-start | bytes 3076
  61.0 7.0 %collective-permute-start = (f32[16,2,16,256]{3,2,1,0:T(8,128)}, f32[16,2,16,256]{3,2,1,0:T(8,128)S(1)}, u32[]{:S(2)}, u32[]{:S(2)}) collective-permute-start(f32[16,2,16,256]{3,2,1,0:T(8,128)} %get-tuple-element.35), channel_id=1, source_target_pairs={{16,0},{32,16},{48,32},{64,48},{80,64},{96,80},{112,96},{0,112},{1... | collective-permute-start | bytes 1572872 | tf_op jit(solution)/shard_map/ppermute | solution.py:402
  81.9 20.3 %all-to-all-start.1 = ((f32[16,2,16,256]{3,2,1,0:T(8,128)}), f32[16,2,16,256]{3,2,1,0:T(8,128)S(1)}, u32[]{:S(2)}, u32[]{:S(2)}) async-start(f32[16,2,16,256]{3,2,1,0:T(8,128)} %slice_subtract_fusion), calls=%async_computation.1 | async-start | bytes 1048576 | tf_op jit(solution)/shard_map/all_to_all | solution.py:418
  117.5 59.6 %all-to-all-start.3 = ((f32[16,2,16,16,128]{4,3,2,1,0:T(8,128)}), f32[16,2,16,16,128]{4,3,2,1,0:T(8,128)}, u32[]{:S(2)}, u32[]{:S(2)}) async-start(f32[16,2,16,16,128]{4,3,2,1,0:T(8,128)} %middle.1), calls=%async_computation.3 | async-start | bytes 8388608 | tf_op jit(solution)/shard_map/all_to_all | solution.py:418
  127.9 6.1 %collective-permute-start.1 = (f32[264,256]{1,0:T(8,128)}, f32[264,256]{1,0:T(8,128)S(1)}, u32[]{:S(2)}, u32[]{:S(2)}) collective-permute-start(f32[264,256]{1,0:T(8,128)} %get-tuple-element.46.own.image), channel_id=1, source_target_pairs={{112,0},{0,16},{16,32},{32,48},{48,64},{64,80},{80,96},{96,112},{1... | collective-permute-start | bytes 811016 | tf_op jit(solution)/shard_map/ppermute | solution.py:402
  129.2 19.3 %collective-permute-start.5 = (f32[264,256]{1,0:T(8,128)}, f32[264,256]{1,0:T(8,128)S(1)}, u32[]{:S(2)}, u32[]{:S(2)}) collective-permute-start(f32[264,256]{1,0:T(8,128)} %get-tuple-element.46.own.image), channel_id=1, source_target_pairs={{16,0},{32,16},{48,32},{64,48},{80,64},{96,80},{112,96},{0,112},{1... | collective-permute-start | bytes 811016 | tf_op jit(solution)/shard_map/ppermute | solution.py:402
  134.0 4.2 %copy-start = (f32[264,256]{1,0:T(8,128)}, f32[264,256]{1,0:T(8,128)S(1)}, u32[]{:S(2)}) copy-start(f32[264,256]{1,0:T(8,128)S(1)} %collective-permute-done.1.before) | copy-start | bytes 811012
  134.7 13.2 %collective-permute-start.3 = (f32[8,256]{1,0:T(8,128)S(1)}, f32[8,256]{1,0:T(8,128)S(1)}, u32[]{:S(2)}, u32[]{:S(2)}) collective-permute-start(f32[8,256]{1,0:T(8,128)S(1)} %slice_add_fusion), channel_id=1, source_target_pairs={{0,64},{16,80},{32,96},{48,112},{64,0},{80,16},{96,32},{112,48},{1... | collective-permute-start | bytes 24584 | tf_op jit(solution)/shard_map/ppermute | solution.py:406
  136.0 11.9 %collective-permute-start.4 = (f32[8,256]{1,0:T(8,128)S(1)}, f32[8,256]{1,0:T(8,128)S(1)}, u32[]{:S(2)}, u32[]{:S(2)}) collective-permute-start(f32[8,256]{1,0:T(8,128)S(1)} %slice_add_fusion), channel_id=1, source_target_pairs={{0,96},{16,112},{32,64},{48,80},{64,32},{80,48},{96,0},{112,16},{1... | collective-permute-start | bytes 24584 | tf_op jit(solution)/shard_map/ppermute | solution.py:406
  138.1 9.8 %collective-permute-start.2 = (f32[8,256]{1,0:T(8,128)S(1)}, f32[8,256]{1,0:T(8,128)S(1)}, u32[]{:S(2)}, u32[]{:S(2)}) collective-permute-start(f32[8,256]{1,0:T(8,128)S(1)} %slice_add_fusion), channel_id=1, source_target_pairs={{0,32},{16,48},{32,0},{48,16},{64,96},{80,112},{96,64},{112,80},{1... | collective-permute-start | bytes 24584 | tf_op jit(solution)/shard_map/ppermute | solution.py:406
  148.5 0.7 copy-start.1
  154.8 8.4 %copy-start.2 = (f32[8,256]{1,0:T(8,128)S(1)}, f32[8,256]{1,0:T(8,128)}, u32[]{:S(2)}) copy-start(f32[8,256]{1,0:T(8,128)} %get-tuple-element.53) | copy-start | bytes 24580
  154.8 8.4 %collective-permute-start.6 = (f32[8,256]{1,0:T(8,128)}, f32[8,256]{1,0:T(8,128)S(1)}, u32[]{:S(2)}, u32[]{:S(2)}) collective-permute-start(f32[8,256]{1,0:T(8,128)} %get-tuple-element.53), channel_id=1, source_target_pairs={{0,16},{16,0},{32,48},{48,32},{64,80},{80,64},{96,112},{112,96},{1... | collective-permute-start | bytes 24584 | tf_op jit(solution)/shard_map/ppermute | solution.py:406
  163.3 13.2 %collective-permute-start.8 = (f32[8,256]{1,0:T(8,128)S(1)}, f32[8,256]{1,0:T(8,128)S(1)}, u32[]{:S(2)}, u32[]{:S(2)}) collective-permute-start(f32[8,256]{1,0:T(8,128)S(1)} %add.70), channel_id=1, source_target_pairs={{0,64},{16,80},{32,96},{48,112},{64,0},{80,16},{96,32},{112,48},{1... | collective-permute-start | bytes 24584 | tf_op jit(solution)/shard_map/ppermute | solution.py:406
  165.9 10.6 %collective-permute-start.9 = (f32[8,256]{1,0:T(8,128)S(1)}, f32[8,256]{1,0:T(8,128)S(1)}, u32[]{:S(2)}, u32[]{:S(2)}) collective-permute-start(f32[8,256]{1,0:T(8,128)S(1)} %add.70), channel_id=1, source_target_pairs={{0,96},{16,112},{32,64},{48,80},{64,32},{80,48},{96,0},{112,16},{1... | collective-permute-start | bytes 24584 | tf_op jit(solution)/shard_map/ppermute | solution.py:406
  168.0 8.5 %collective-permute-start.7 = (f32[8,256]{1,0:T(8,128)S(1)}, f32[8,256]{1,0:T(8,128)S(1)}, u32[]{:S(2)}, u32[]{:S(2)}) collective-permute-start(f32[8,256]{1,0:T(8,128)S(1)} %add.70), channel_id=1, source_target_pairs={{0,32},{16,48},{32,0},{48,16},{64,96},{80,112},{96,64},{112,80},{1... | collective-permute-start | bytes 24584 | tf_op jit(solution)/shard_map/ppermute | solution.py:406

commit v9 on v7

--- a/solution.py
+++ b/solution.py
@@ -431,18 +431,25 @@
     start = slab_index * ROWS
     own_x = lax.dynamic_slice_in_dim(basis_x, start, ROWS, 0)
 
+    near_x = from_behind(eigen_x, "slab", 1)
+    near_z = from_behind(eigen_z, "slab", 4)
+    near_y = from_behind(eigen_y, "slab", -1)
+    far_x = from_behind(eigen_x, "slab", -4)
     part1 = forward(source, coarse, 1, basis_y, basis_z)
+    near_x, near_y, near_z, far_x, part1 = lax.optimization_barrier(
+        (near_x, near_y, near_z, far_x, part1)
+    )
     lines = exchange(part1)
 
-    shift = own_rho * eigen_y
+    shift = own_rho * near_y
     own_shift = lax.dynamic_slice_in_dim(shift, start, ROWS, 0)
-    base_xz = own_rho * (eigen_x[:, None] + eigen_z[None, :])
+    base_xz = own_rho * (far_x[:, None] + eigen_z[None, :])
     ends = jnp.stack([basis_z[0], basis_z[N - 1]])
     gram_x, gram_y = grams(basis_x, basis_y)
 
     part0 = forward(source, coarse, 0, basis_y, basis_z)
     pieces, near = faces(
-        own_rho.reshape(1), shift, eigen_x[None], eigen_z[None], own_x, basis_z, part0, part1
+        own_rho.reshape(1), shift, near_x[None], near_z[None], own_x, basis_z, part0, part1
     )
     shares = pieces[:, 0:2] - from_behind(near, "sub", -1)
     shares, lines, gram_x, gram_y, base_xz, ends = lax.optimization_barrier(

time: 188 us -> 183 us (0.973)
  waiting for transfers between devices: 17.5 us -> 10.4 us
  starting transfers between devices: 33.2 us -> 36.1 us
    all_to_all x3, waiting for transfers between devices: 14.2 us -> 4.41 us  [exchange(): lax.all_to_all(block, 'slab', split_axis=0, concat_axis=0, tiled=True)]
    ppermute x3 -> x7, starting transfers between devices: 1.25 us -> 9.47 us  [from_behind(): return lax.ppermute(block, axis, route)]
    all_to_all x3, starting transfers between devices: 23.1 us -> 17.4 us  [exchange(): lax.all_to_all(block, 'slab', split_axis=0, concat_axis=0, tiled=True)]
    ppermute x3 -> x7, waiting for transfers between devices: 3.24 us -> 5.92 us  [from_behind(): return lax.ppermute(block, axis, route)]
  transfers between devices with their start and end apart: 14 -> 18, of which waited for: 4 -> 4; matrix products, arithmetic and copies ran while one was open for 6% -> 6% of each run, Pallas kernels for 46% -> 53%
where the time goes in v9:
time: 183 us; the launch traced here: 180 us
  Pallas kernels  104 us (57%)
  starting transfers between devices  36.1 us (20%)
  blocking collectives  14.6 us (8%)
  waiting for transfers between devices  10.4 us (6%)
  other arithmetic  7.57 us (4%)
  local copies, waits for them, and re-layouts  4.06 us (2%)
  between operations  3.34 us (2%)
    pallas_call x1, Pallas kernels, faces(): pl.pallas_call(faces_kernel, grid=(SLABS,), in_specs=[smem(), smem(), who...  28.7 us
    pallas_call x3, Pallas kernels, extra(): pl.pallas_call(functools.partial(extra_kernel, part), grid=(stop - skip,)...  26.4 us
    pallas_call x2, Pallas kernels, forward(): pl.pallas_call(forward_kernel, grid=(ROWS // GROUP,), in_specs=[pl.BlockS...  20.1 us
    all_to_all x3, starting transfers between devices, exchange(): lax.all_to_all(block, 'slab', split_axis=0, concat_axis=0, tiled=True)  17.4 us
    all_to_all x1, blocking collectives, exchange(): lax.all_to_all(block, 'slab', split_axis=0, concat_axis=0, tiled=True)  14.6 us
    ppermute x7, starting transfers between devices, from_behind(): return lax.ppermute(block, axis, route)  9.47 us
    pallas_call x1, Pallas kernels, backward(): pl.pallas_call(backward_kernel, grid=(ROWS // GROUP,), in_specs=[whole((8...  9.28 us
    ppermute x8, starting transfers between devices, from_partner(): return lax.ppermute(sums, 'sub', [(i, i ^ bits) for i in range(8)])  9.23 us
  transfers between devices with their start and end apart: 18, of which 4 were waited for; matrix products, arithmetic and copies ran while one was open for 6% of the time, Pallas kernels for 53%

profile of v9, /device:TPU:6, one launch (start us, length us, event | category | flops | bytes accessed | tf_op | source)
XLA Modules:
  0.0 180.3 jit_solution(11309465723455310697)
XLA Ops:
  0.6 3.1 %collective-permute-start.3 = (f32[256]{0:T(256)}, f32[256]{0:T(256)S(1)}, u32[]{:S(2)}, u32[]{:S(2)}) collective-permute-start(f32[256]{0:T(256)} %param.16), channel_id=1, source_target_pairs={{4,0},{5,1},{6,2},{7,3},{8,4},{9,5},{10,6},{11,7},{12,8},{13,9},{1... | collective-permute-start | bytes 3080 | tf_op jit(solution)/shard_map/ppermute | solution.py:402
  3.7 1.9 %collective-permute-start = (f32[256]{0:T(256)}, f32[256]{0:T(256)S(1)}, u32[]{:S(2)}, u32[]{:S(2)}) collective-permute-start(f32[256]{0:T(256)} %param.16), channel_id=1, source_target_pairs={{15,0},{0,1},{1,2},{2,3},{3,4},{4,5},{5,6},{6,7},{7,8},{8,9},{9,10... | collective-permute-start | bytes 3080 | tf_op jit(solution)/shard_map/ppermute | solution.py:402
  5.6 3.4 %collective-permute-start.1 = (f32[256]{0:T(256)}, f32[256]{0:T(256)S(1)}, u32[]{:S(2)}, u32[]{:S(2)}) collective-permute-start(f32[256]{0:T(256)} %param.17), channel_id=1, source_target_pairs={{1,0},{2,1},{3,2},{4,3},{5,4},{6,5},{7,6},{8,7},{9,8},{10,9},{11,1... | collective-permute-start | bytes 3080 | tf_op jit(solution)/shard_map/ppermute | solution.py:402
  9.1 0.2 collective-permute-start.2
  9.2 10.1 %forward.2.part1 = f32[16,2,16,16,128]{4,3,2,1,0:T(8,128)} custom-call(f32[16,256,256]{2,1,0:T(8,128)} %bitcast.10, f32[2,1,16,256,256]{4,3,2,1,0:T(8,128)} %coarse.3, f32[256,256]{1,0:T(8,128)} %basis_y.11, f32[256,256]{1,0:T(8,128)} %basis_z.7), custom_call_target="tpu_custom_call" | custom-call | flops 3221225472 | bytes 12582912 | tf_op jit(solution)/shard_map/forward/pallas_call | solution.py:75
  19.3 0.0 collective-permute-done.1
  19.3 0.0 collective-permute-done
  19.3 0.0 copy-start.6
  19.4 4.7 %all-to-all-start = ((f32[16,2,16,16,128]{4,3,2,1,0:T(8,128)}), f32[16,2,16,16,128]{4,3,2,1,0:T(8,128)}, u32[]{:S(2)}, u32[]{:S(2)}) async-start(f32[16,2,16,16,128]{4,3,2,1,0:T(8,128)} %forward.2.part1), calls=%async_computation | async-start | bytes 8388608 | tf_op jit(solution)/shard_map/all_to_all | solution.py:418
  24.1 2.6 %grams.1 = (f32[256,256]{1,0:T(8,128)}, f32[256,256]{1,0:T(8,128)}) custom-call(f32[256,256]{1,0:T(8,128)} %basis_x.3, f32[256,256]{1,0:T(8,128)} %basis_y.11), custom_call_target="tpu_custom_call" | custom-call | tf_op jit(solution)/shard_map/grams/pallas_call | solution.py:394
  26.7 0.7 fusion.1
  27.3 1.3 constant_dynamic-slice_fusion.own_x
  28.6 10.0 %forward.3.part0 = f32[16,2,16,16,128]{4,3,2,1,0:T(8,128)} custom-call(f32[16,256,256]{2,1,0:T(8,128)} %bitcast.11, f32[2,1,16,256,256]{4,3,2,1,0:T(8,128)} %coarse.3, f32[256,256]{1,0:T(8,128)} %basis_y.11, f32[256,256]{1,0:T(8,128)} %basis_z.7), custom_call_target="tpu_custom_call" | custom-call | flops 3221225472 | bytes 12582912 | tf_op jit(solution)/shard_map/forward/pallas_call | solution.py:75
  38.6 1.1 broadcast_multiply_fusion.shift
  39.8 28.7 %faces.1 = (f32[16,5,16,256]{3,2,1,0:T(8,128)}, f32[16,2,16,256]{3,2,1,0:T(8,128)}) custom-call(f32[1]{0:T(128)} %get-tuple-element.80.own_rho, f32[256]{0:T(256)} %broadcast_multiply_fusion.shift, f32[1,256]{1,0:T(1,128)} %bitcast.12, f32[1,256]{1,0:T(1,128)} %bitcast.13, f32[16,256]{1,0:T(8,128)} %constant_dynamic-slice_fusion.own_x, f32[256,256]{1,0:T(8,128)} %basis_z.7, ...), custom_call_target="tpu_custom_call" | custom-call | flops 16777216 | bytes 65536 | tf_op jit(solution)/shard_map/faces/pallas_call | solution.py:239
  68.5 0.7 fusion
  69.2 0.5 pad_maximum_fusion.ends
  69.7 1.4 add_multiply_fusion.base
  71.2 4.3 %collective-permute-done.4 = f32[16,2,16,256]{3,2,1,0:T(8,128)S(1)} collective-permute-done((f32[16,2,16,256]{3,2,1,0:T(8,128)}, f32[16,2,16,256]{3,2,1,0:T(8,128)S(1)}, u32[]{:S(2)}, u32[]{:S(2)}) %collective-permute-start.4) | collective-permute-done | bytes 524320 | tf_op jit(solution)/shard_map/ppermute | solution.py:402
  75.5 1.9 %slice_subtract_fusion = f32[16,2,16,256]{3,2,1,0:T(8,128)} fusion(f32[16,2,16,256]{3,2,1,0:T(8,128)S(1)} %collective-permute-done.4, f32[16,5,16,256]{3,2,1,0:T(8,128)} %get-tuple-element.44.pieces), kind=kLoop, calls=%fused_computation | loop fusion | flops 131072 | bytes 1572864 | tf_op jit(solution)/shard_map/sub | solution.py:454
  77.4 1.2 all-to-all-done.lines
  78.6 8.2 %all-to-all-start.1 = ((f32[16,2,16,256]{3,2,1,0:T(8,128)}), f32[16,2,16,256]{3,2,1,0:T(8,128)S(1)}, u32[]{:S(2)}, u32[]{:S(2)}) async-start(f32[16,2,16,256]{3,2,1,0:T(8,128)} %slice_subtract_fusion), calls=%async_computation.1 | async-start | bytes 1048576 | tf_op jit(solution)/shard_map/all_to_all | solution.py:418
  86.8 0.6 dynamic_slice.15.shift
  87.4 7.4 %middle.1 = f32[16,2,16,16,128]{4,3,2,1,0:T(8,128)} custom-call(f32[256,256]{1,0:T(8,128)} %add_multiply_fusion.base, f32[16]{0:T(128)} %dynamic_slice.15.shift, f32[256,256]{1,0:T(8,128)} %basis_x.3, f32[16,2,16,16,128]{4,3,2,1,0:T(8,128)} %all-to-all-done.lines), custom_call_target="tpu_custom_call" | custom-call | flops 3221225472 | bytes 8388608 | tf_op jit(solution)/shard_map/middle/pallas_call | solution.py:117
  94.8 3.2 %all-to-all-done.1 = f32[16,2,16,256]{3,2,1,0:T(8,128)S(1)} async-done(((f32[16,2,16,256]{3,2,1,0:T(8,128)}), f32[16,2,16,256]{3,2,1,0:T(8,128)S(1)}, u32[]{:S(2)}, u32[]{:S(2)}) %all-to-all-start.1) | async-done | bytes 524320 | tf_op jit(solution)/shard_map/all_to_all | solution.py:418
  98.1 0.1 broadcast_in_dim.25
  98.1 14.6 %all_to_all.20.jumps = f32[16,2,16,256]{3,2,1,0:T(8,128)} all-to-all(f32[16,2,16,256]{3,2,1,0:T(8,128)S(1)} %broadcast_in_dim.25), channel_id=1, replica_groups=mesh['sub'=8,'slab'=16] {'slab'}, dimensions={0} | all-to-all | bytes 1048576 | tf_op jit(solution)/shard_map/all_to_all | solution.py:418
  112.7 4.5 %all-to-all-start.3 = ((f32[16,2,16,16,128]{4,3,2,1,0:T(8,128)}), f32[16,2,16,16,128]{4,3,2,1,0:T(8,128)}, u32[]{:S(2)}, u32[]{:S(2)}) async-start(f32[16,2,16,16,128]{4,3,2,1,0:T(8,128)} %middle.1), calls=%async_computation.3 | async-start | bytes 8388608 | tf_op jit(solution)/shard_map/all_to_all | solution.py:418
  118.5 4.3 %chain0.1 = (f32[16,256]{1,0:T(8,128)}, f32[256,256]{1,0:T(8,128)}, f32[8,128]{1,0:T(8,128)}) custom-call(f32[1]{0:T(128)} %bitcast.2.scale, f32[16,2,16,256]{3,2,1,0:T(8,128)} %all_to_all.20.jumps, f32[256,256]{1,0:T(8,128)} %get-tuple-element.55.gram_x, f32[256,256]{1,0:T(8,128)} %get-tuple-element.56.gram_y, f32[256,256]{1,0:T(8,128)} %stiff.3, ...), custom_call_target="tpu_custom_call" | custom-call | flops 16777216 | bytes 65536 | tf_op jit(solution)/shard_map/chain0/pallas_call | solution.py:341
  124.1 1.0 collective-permute-start.6
  125.0 0.6 pad_maximum_fusion.1.scale
  125.6 0.9 collective-permute-start.10
  126.5 0.7 add.66
  127.2 1.6 collective-permute-done.5.before
  128.8 2.0 %collective-permute-start.9 = (f32[8,128]{1,0:T(8,128)S(1)}, f32[8,128]{1,0:T(8,128)S(1)}, u32[]{:S(2)}, u32[]{:S(2)}) collective-permute-start(f32[8,128]{1,0:T(8,128)S(1)} %add.66), channel_id=1, source_target_pairs={{0,96},{16,112},{32,64},{48,80},{64,32},{80,48},{96,0},{112,16},{1... | collective-permute-start | bytes 12296 | tf_op jit(solution)/shard_map/ppermute | solution.py:406
  130.8 0.9 collective-permute-start.8
  131.7 1.2 collective-permute-start.7
  132.9 9.7 %extra0.1.refs_0_ = f32[16,2,16,16,128]{4,3,2,1,0:T(8,128)} custom-call(f32[256,256]{1,0:T(8,128)} %add_multiply_fusion.base, f32[256]{0:T(256)} %broadcast_multiply_fusion.shift, f32[16,256]{1,0:T(8,128)} %constant_dynamic-slice_fusion.own_x, f32[2,256]{1,0:T(2,128)} %pad_maximum_fusion.ends, f32[256,256]{1,0:T(8,128)} %get-tuple-element.57.own.image, ...), custom_call_target="tpu_custom_call" | custom-call | flops 8999999488 | bytes 65536 | tf_op jit(solution)/shard_map/extra0/pallas_call | solution.py:283
  142.6 0.6 add_add_fusion.1.sums_in.sums0
  143.2 0.7 copy-done.1
  143.9 5.5 %chain1.1 = (f32[8,128]{1,0:T(8,128)}, f32[16,256]{1,0:T(8,128)}, f32[16,256]{1,0:T(8,128)}) custom-call(f32[2]{0:T(128)} %pad_maximum_fusion.1.scale, f32[8,128]{1,0:T(8,128)} %add_add_fusion.1.sums_in.sums0, f32[16,2,16,256]{3,2,1,0:T(8,128)} %all_to_all.20.jumps, f32[256,256]{1,0:T(8,128)} %get-tuple-element.57.own.image, f32[256,256]{1,0:T(8,128)} %copy-done, ...), custom_call_target="tpu_custom_call" | custom-call | flops 16777216 | bytes 65536 | tf_op jit(solution)/shard_map/chain1/pallas_call | solution.py:371
  149.4 8.4 %extra1.1.refs_0_ = f32[16,2,16,16,128]{4,3,2,1,0:T(8,128)} custom-call(f32[256,256]{1,0:T(8,128)} %add_multiply_fusion.base, f32[256]{0:T(256)} %broadcast_multiply_fusion.shift, f32[16,256]{1,0:T(8,128)} %constant_dynamic-slice_fusion.own_x, f32[2,256]{1,0:T(2,128)} %pad_maximum_fusion.ends, ...), custom_call_target="tpu_custom_call", output_to_operand_aliasing={{}: (6, {})} | custom-call | flops 7500000256 | bytes 65536 | tf_op jit(solution)/shard_map/extra1/pallas_call | solution.py:283
  157.8 2.1 %collective-permute-start.14 = (f32[8,128]{1,0:T(8,128)S(1)}, f32[8,128]{1,0:T(8,128)S(1)}, u32[]{:S(2)}, u32[]{:S(2)}) collective-permute-start(f32[8,128]{1,0:T(8,128)S(1)} %add.70), channel_id=1, source_target_pairs={{0,96},{16,112},{32,64},{48,80},{64,32},{80,48},{96,0},{112,16},{1... | collective-permute-start | bytes 12296 | tf_op jit(solution)/shard_map/ppermute | solution.py:406
  159.9 0.9 collective-permute-start.13
  160.8 1.2 collective-permute-start.12
  162.0 8.4 %extra2.1.extra = f32[16,2,16,16,128]{4,3,2,1,0:T(8,128)} custom-call(f32[256,256]{1,0:T(8,128)} %add_multiply_fusion.base, f32[256]{0:T(256)} %broadcast_multiply_fusion.shift, f32[16,256]{1,0:T(8,128)} %constant_dynamic-slice_fusion.own_x, f32[2,256]{1,0:T(2,128)} %pad_maximum_fusion.ends, ...), custom_call_target="tpu_custom_call", output_to_operand_aliasing={{}: (6, {})} | custom-call | flops 7500000256 | bytes 65536 | tf_op jit(solution)/shard_map/extra2/pallas_call | solution.py:283
  170.4 0.6 add_add_fusion.sums1
  171.0 9.3 %backward.1 = (f32[16,256,256]{2,1,0:T(8,128)}, f32[16,256]{1,0:T(8,128)}) custom-call(f32[8,128]{1,0:T(8,128)} %add_add_fusion.1.sums_in.sums0, f32[8,128]{1,0:T(8,128)} %add_add_fusion.sums1, f32[16,256]{1,0:T(8,128)} %get-tuple-element.70.first, f32[16,256]{1,0:T(8,128)} %get-tuple-element.71.change, f32[16,2,16,16,128]{4,3,2,1,0:T(8,128)} %all-to-all-done.3.field, ...), custom_call_target="tpu_custom_call" | custom-call | flops 3221225472 | bytes 12582912 | tf_op jit(solution)/shard_map/backward/pallas_call | solution.py:162
  (31 shorter events, 0.1 us)
Async XLA Ops:
  0.6 18.7 %collective-permute-start.3 = (f32[256]{0:T(256)}, f32[256]{0:T(256)S(1)}, u32[]{:S(2)}, u32[]{:S(2)}) collective-permute-start(f32[256]{0:T(256)} %param.16), channel_id=1, source_target_pairs={{4,0},{5,1},{6,2},{7,3},{8,4},{9,5},{10,6},{11,7},{12,8},{13,9},{1... | collective-permute-start | bytes 3080 | tf_op jit(solution)/shard_map/ppermute | solution.py:402
  3.7 15.6 %collective-permute-start = (f32[256]{0:T(256)}, f32[256]{0:T(256)S(1)}, u32[]{:S(2)}, u32[]{:S(2)}) collective-permute-start(f32[256]{0:T(256)} %param.16), channel_id=1, source_target_pairs={{15,0},{0,1},{1,2},{2,3},{3,4},{4,5},{5,6},{6,7},{7,8},{8,9},{9,10... | collective-permute-start | bytes 3080 | tf_op jit(solution)/shard_map/ppermute | solution.py:402
  5.6 13.7 %collective-permute-start.1 = (f32[256]{0:T(256)}, f32[256]{0:T(256)S(1)}, u32[]{:S(2)}, u32[]{:S(2)}) collective-permute-start(f32[256]{0:T(256)} %param.17), channel_id=1, source_target_pairs={{1,0},{2,1},{3,2},{4,3},{5,4},{6,5},{7,6},{8,7},{9,8},{10,9},{11,1... | collective-permute-start | bytes 3080 | tf_op jit(solution)/shard_map/ppermute | solution.py:402
  9.1 10.3 %collective-permute-start.2 = (f32[256]{0:T(256)}, f32[256]{0:T(256)S(1)}, u32[]{:S(2)}, u32[]{:S(2)}) collective-permute-start(f32[256]{0:T(256)} %param.18), channel_id=1, source_target_pairs={{12,0},{13,1},{14,2},{15,3},{0,4},{1,5},{2,6},{3,7},{4,8},{5,9},{6... | collective-permute-start | bytes 3080 | tf_op jit(solution)/shard_map/ppermute | solution.py:402
  19.3 7.3 %copy-start.4 = (f32[8]{0:T(128)S(1)}, f32[8]{0:T(128)}, u32[]{:S(2)}) copy-start(f32[8]{0:T(128)} %param.12) | copy-start | bytes 100
  19.3 4.7 %copy-start.6 = (f32[256]{0:T(256)}, f32[256]{0:T(256)S(1)}, u32[]{:S(2)}) copy-start(f32[256]{0:T(256)S(1)} %collective-permute-done) | copy-start | bytes 3076
  19.4 4.7 %copy-start.7 = (f32[256]{0:T(256)}, f32[256]{0:T(256)S(1)}, u32[]{:S(2)}) copy-start(f32[256]{0:T(256)S(1)} %collective-permute-done.2) | copy-start | bytes 3076
  19.4 59.2 %all-to-all-start = ((f32[16,2,16,16,128]{4,3,2,1,0:T(8,128)}), f32[16,2,16,16,128]{4,3,2,1,0:T(8,128)}, u32[]{:S(2)}, u32[]{:S(2)}) async-start(f32[16,2,16,16,128]{4,3,2,1,0:T(8,128)} %forward.2.part1), calls=%async_computation | async-start | bytes 8388608 | tf_op jit(solution)/shard_map/all_to_all | solution.py:418
  39.8 30.0 %copy-start.5 = (f32[256]{0:T(256)S(1)}, f32[256]{0:T(256)}, u32[]{:S(2)}) copy-start(f32[256]{0:T(256)} %param.18) | copy-start | bytes 3076
  39.8 47.0 %copy-start.3 = (f32[256]{0:T(256)S(1)}, f32[256]{0:T(256)}, u32[]{:S(2)}) copy-start(f32[256]{0:T(256)} %broadcast_multiply_fusion.shift) | copy-start | bytes 3076
  68.5 7.0 %collective-permute-start.4 = (f32[16,2,16,256]{3,2,1,0:T(8,128)}, f32[16,2,16,256]{3,2,1,0:T(8,128)S(1)}, u32[]{:S(2)}, u32[]{:S(2)}) collective-permute-start(f32[16,2,16,256]{3,2,1,0:T(8,128)} %get-tuple-element.45), channel_id=1, source_target_pairs={{16,0},{32,16},{48,32},{64,48},{80,64},{96,80},{112,96},{0,112},{1... | collective-permute-start | bytes 1572872 | tf_op jit(solution)/shard_map/ppermute | solution.py:402
  78.6 19.4 %all-to-all-start.1 = ((f32[16,2,16,256]{3,2,1,0:T(8,128)}), f32[16,2,16,256]{3,2,1,0:T(8,128)S(1)}, u32[]{:S(2)}, u32[]{:S(2)}) async-start(f32[16,2,16,256]{3,2,1,0:T(8,128)} %slice_subtract_fusion), calls=%async_computation.1 | async-start | bytes 1048576 | tf_op jit(solution)/shard_map/all_to_all | solution.py:418
  112.7 58.3 %all-to-all-start.3 = ((f32[16,2,16,16,128]{4,3,2,1,0:T(8,128)}), f32[16,2,16,16,128]{4,3,2,1,0:T(8,128)}, u32[]{:S(2)}, u32[]{:S(2)}) async-start(f32[16,2,16,16,128]{4,3,2,1,0:T(8,128)} %middle.1), calls=%async_computation.3 | async-start | bytes 8388608 | tf_op jit(solution)/shard_map/all_to_all | solution.py:418
  122.8 6.0 %collective-permute-start.5 = (f32[256,256]{1,0:T(8,128)}, f32[256,256]{1,0:T(8,128)S(1)}, u32[]{:S(2)}, u32[]{:S(2)}) collective-permute-start(f32[256,256]{1,0:T(8,128)} %get-tuple-element.57.own.image), channel_id=1, source_target_pairs={{112,0},{0,16},{16,32},{32,48},{48,64},{64,80},{80,96},{96,112},{1... | collective-permute-start | bytes 786440 | tf_op jit(solution)/shard_map/ppermute | solution.py:402
  124.1 2.4 %collective-permute-start.6 = (f32[8,128]{1,0:T(8,128)}, f32[8,128]{1,0:T(8,128)S(1)}, u32[]{:S(2)}, u32[]{:S(2)}) collective-permute-start(f32[8,128]{1,0:T(8,128)} %get-tuple-element.58), channel_id=1, source_target_pairs={{0,16},{16,0},{32,48},{48,32},{64,80},{80,64},{96,112},{112,96},{1... | collective-permute-start | bytes 12296 | tf_op jit(solution)/shard_map/ppermute | solution.py:406
  125.6 17.6 %collective-permute-start.10 = (f32[256,256]{1,0:T(8,128)}, f32[256,256]{1,0:T(8,128)S(1)}, u32[]{:S(2)}, u32[]{:S(2)}) collective-permute-start(f32[256,256]{1,0:T(8,128)} %get-tuple-element.57.own.image), channel_id=1, source_target_pairs={{16,0},{32,16},{48,32},{64,48},{80,64},{96,80},{112,96},{0,112},{1... | collective-permute-start | bytes 786440 | tf_op jit(solution)/shard_map/ppermute | solution.py:402
  128.8 4.1 %copy-start = (f32[256,256]{1,0:T(8,128)}, f32[256,256]{1,0:T(8,128)S(1)}, u32[]{:S(2)}) copy-start(f32[256,256]{1,0:T(8,128)S(1)} %collective-permute-done.5.before) | copy-start | bytes 786436
  128.8 13.8 %collective-permute-start.9 = (f32[8,128]{1,0:T(8,128)S(1)}, f32[8,128]{1,0:T(8,128)S(1)}, u32[]{:S(2)}, u32[]{:S(2)}) collective-permute-start(f32[8,128]{1,0:T(8,128)S(1)} %add.66), channel_id=1, source_target_pairs={{0,96},{16,112},{32,64},{48,80},{64,32},{80,48},{96,0},{112,16},{1... | collective-permute-start | bytes 12296 | tf_op jit(solution)/shard_map/ppermute | solution.py:406
  130.8 11.8 %collective-permute-start.8 = (f32[8,128]{1,0:T(8,128)S(1)}, f32[8,128]{1,0:T(8,128)S(1)}, u32[]{:S(2)}, u32[]{:S(2)}) collective-permute-start(f32[8,128]{1,0:T(8,128)S(1)} %add.66), channel_id=1, source_target_pairs={{0,64},{16,80},{32,96},{48,112},{64,0},{80,16},{96,32},{112,48},{1... | collective-permute-start | bytes 12296 | tf_op jit(solution)/shard_map/ppermute | solution.py:406
  131.7 10.9 %collective-permute-start.7 = (f32[8,128]{1,0:T(8,128)S(1)}, f32[8,128]{1,0:T(8,128)S(1)}, u32[]{:S(2)}, u32[]{:S(2)}) collective-permute-start(f32[8,128]{1,0:T(8,128)S(1)} %add.66), channel_id=1, source_target_pairs={{0,32},{16,48},{32,0},{48,16},{64,96},{80,112},{96,64},{112,80},{1... | collective-permute-start | bytes 12296 | tf_op jit(solution)/shard_map/ppermute | solution.py:406
  143.2 0.7 copy-start.1
  149.4 8.4 %copy-start.2 = (f32[8,128]{1,0:T(8,128)S(1)}, f32[8,128]{1,0:T(8,128)}, u32[]{:S(2)}) copy-start(f32[8,128]{1,0:T(8,128)} %get-tuple-element.65) | copy-start | bytes 12292
  149.4 8.4 %collective-permute-start.11 = (f32[8,128]{1,0:T(8,128)}, f32[8,128]{1,0:T(8,128)S(1)}, u32[]{:S(2)}, u32[]{:S(2)}) collective-permute-start(f32[8,128]{1,0:T(8,128)} %get-tuple-element.65), channel_id=1, source_target_pairs={{0,16},{16,0},{32,48},{48,32},{64,80},{80,64},{96,112},{112,96},{1... | collective-permute-start | bytes 12296 | tf_op jit(solution)/shard_map/ppermute | solution.py:406
  157.8 12.5 %collective-permute-start.14 = (f32[8,128]{1,0:T(8,128)S(1)}, f32[8,128]{1,0:T(8,128)S(1)}, u32[]{:S(2)}, u32[]{:S(2)}) collective-permute-start(f32[8,128]{1,0:T(8,128)S(1)} %add.70), channel_id=1, source_target_pairs={{0,96},{16,112},{32,64},{48,80},{64,32},{80,48},{96,0},{112,16},{1... | collective-permute-start | bytes 12296 | tf_op jit(solution)/shard_map/ppermute | solution.py:406
  159.9 10.5 %collective-permute-start.13 = (f32[8,128]{1,0:T(8,128)S(1)}, f32[8,128]{1,0:T(8,128)S(1)}, u32[]{:S(2)}, u32[]{:S(2)}) collective-permute-start(f32[8,128]{1,0:T(8,128)S(1)} %add.70), channel_id=1, source_target_pairs={{0,64},{16,80},{32,96},{48,112},{64,0},{80,16},{96,32},{112,48},{1... | collective-permute-start | bytes 12296 | tf_op jit(solution)/shard_map/ppermute | solution.py:406
  160.8 9.6 %collective-permute-start.12 = (f32[8,128]{1,0:T(8,128)S(1)}, f32[8,128]{1,0:T(8,128)S(1)}, u32[]{:S(2)}, u32[]{:S(2)}) collective-permute-start(f32[8,128]{1,0:T(8,128)S(1)} %add.70), channel_id=1, source_target_pairs={{0,32},{16,48},{32,0},{48,16},{64,96},{80,112},{96,64},{112,80},{1... | collective-permute-start | bytes 12296 | tf_op jit(solution)/shard_map/ppermute | solution.py:406

commit v10 on v7

--- a/solution.py
+++ b/solution.py
@@ -431,7 +431,10 @@
     start = slab_index * ROWS
     own_x = lax.dynamic_slice_in_dim(basis_x, start, ROWS, 0)
 
+    near_x = from_behind(eigen_x, "slab", 1)
+    near_z = from_behind(eigen_z, "slab", 4)
     part1 = forward(source, coarse, 1, basis_y, basis_z)
+    near_x, near_z, part1 = lax.optimization_barrier((near_x, near_z, part1))
     lines = exchange(part1)
 
     shift = own_rho * eigen_y
@@ -442,7 +445,7 @@
 
     part0 = forward(source, coarse, 0, basis_y, basis_z)
     pieces, near = faces(
-        own_rho.reshape(1), shift, eigen_x[None], eigen_z[None], own_x, basis_z, part0, part1
+        own_rho.reshape(1), shift, near_x[None], near_z[None], own_x, basis_z, part0, part1
     )
     shares = pieces[:, 0:2] - from_behind(near, "sub", -1)
     shares, lines, gram_x, gram_y, base_xz, ends = lax.optimization_barrier(

time: 188 us -> 182 us (0.968)
  waiting for transfers between devices: 17.5 us -> 9.07 us
  starting transfers between devices: 33.2 us -> 35.9 us
    all_to_all x3, waiting for transfers between devices: 14.2 us -> 3.14 us  [exchange(): lax.all_to_all(block, 'slab', split_axis=0, concat_axis=0, tiled=True)]
    ppermute x3 -> x5, starting transfers between devices: 1.25 us -> 4.7 us  [from_behind(): return lax.ppermute(block, axis, route)]
    ppermute x3 -> x5, waiting for transfers between devices: 3.24 us -> 5.91 us  [from_behind(): return lax.ppermute(block, axis, route)]
  transfers between devices with their start and end apart: 14 -> 16, of which waited for: 4 -> 4; matrix products, arithmetic and copies ran while one was open for 6% -> 6% of each run, Pallas kernels for 46% -> 53%
where the time goes in v10:
time: 182 us; the launch traced here: 179 us
  Pallas kernels  104 us (57%)
  starting transfers between devices  35.9 us (20%)
  blocking collectives  15.1 us (8%)
  waiting for transfers between devices  9.07 us (5%)
  other arithmetic  7.58 us (4%)
  local copies, waits for them, and re-layouts  4.06 us (2%)
  between operations  3.33 us (2%)
    pallas_call x1, Pallas kernels, faces(): pl.pallas_call(faces_kernel, grid=(SLABS,), in_specs=[smem(), smem(), who...  28.7 us
    pallas_call x3, Pallas kernels, extra(): pl.pallas_call(functools.partial(extra_kernel, part), grid=(stop - skip,)...  26.4 us
    all_to_all x3, starting transfers between devices, exchange(): lax.all_to_all(block, 'slab', split_axis=0, concat_axis=0, tiled=True)  22.2 us
    pallas_call x2, Pallas kernels, forward(): pl.pallas_call(forward_kernel, grid=(ROWS // GROUP,), in_specs=[pl.BlockS...  20.1 us
    all_to_all x1, blocking collectives, exchange(): lax.all_to_all(block, 'slab', split_axis=0, concat_axis=0, tiled=True)  15.1 us
    pallas_call x1, Pallas kernels, backward(): pl.pallas_call(backward_kernel, grid=(ROWS // GROUP,), in_specs=[whole((8...  9.28 us
    ppermute x8, starting transfers between devices, from_partner(): return lax.ppermute(sums, 'sub', [(i, i ^ bits) for i in range(8)])  8.98 us
    pallas_call x1, Pallas kernels, middle(): pl.pallas_call(middle_kernel, grid=(N // SLABS // GROUP,), in_specs=[whol...  7.39 us
  transfers between devices with their start and end apart: 16, of which 4 were waited for; matrix products, arithmetic and copies ran while one was open for 6% of the time, Pallas kernels for 53%

profile of v10, /device:TPU:6, one launch (start us, length us, event | category | flops | bytes accessed | tf_op | source)
XLA Modules:
  0.0 179.3 jit_solution(15397396645737202533)
XLA Ops:
  0.6 2.0 %collective-permute-start = (f32[256]{0:T(256)}, f32[256]{0:T(256)S(1)}, u32[]{:S(2)}, u32[]{:S(2)}) collective-permute-start(f32[256]{0:T(256)} %param.16), channel_id=1, source_target_pairs={{15,0},{0,1},{1,2},{2,3},{3,4},{4,5},{5,6},{6,7},{7,8},{8,9},{9,10... | collective-permute-start | bytes 3080 | tf_op jit(solution)/shard_map/ppermute | solution.py:402
  2.6 1.6 collective-permute-start.1
  4.2 10.1 %forward.2.part1 = f32[16,2,16,16,128]{4,3,2,1,0:T(8,128)} custom-call(f32[16,256,256]{2,1,0:T(8,128)} %bitcast.10, f32[2,1,16,256,256]{4,3,2,1,0:T(8,128)} %coarse.3, f32[256,256]{1,0:T(8,128)} %basis_y.11, f32[256,256]{1,0:T(8,128)} %basis_z.7), custom_call_target="tpu_custom_call" | custom-call | flops 3221225472 | bytes 12582912 | tf_op jit(solution)/shard_map/forward/pallas_call | solution.py:75
  14.3 0.0 collective-permute-done
  14.3 0.0 copy-start.8
  14.3 0.0 collective-permute-done.1
  14.3 7.4 %all-to-all-start = ((f32[16,2,16,16,128]{4,3,2,1,0:T(8,128)}), f32[16,2,16,16,128]{4,3,2,1,0:T(8,128)}, u32[]{:S(2)}, u32[]{:S(2)}) async-start(f32[16,2,16,16,128]{4,3,2,1,0:T(8,128)} %forward.2.part1), calls=%async_computation | async-start | bytes 8388608 | tf_op jit(solution)/shard_map/all_to_all | solution.py:418
  21.7 2.6 %grams.1 = (f32[256,256]{1,0:T(8,128)}, f32[256,256]{1,0:T(8,128)}) custom-call(f32[256,256]{1,0:T(8,128)} %basis_x.3, f32[256,256]{1,0:T(8,128)} %basis_y.11), custom_call_target="tpu_custom_call" | custom-call | tf_op jit(solution)/shard_map/grams/pallas_call | solution.py:394
  24.3 0.7 fusion.1
  24.9 1.3 constant_dynamic-slice_fusion.own_x
  26.3 1.1 broadcast_multiply_fusion.shift
  27.4 10.0 %forward.3.part0 = f32[16,2,16,16,128]{4,3,2,1,0:T(8,128)} custom-call(f32[16,256,256]{2,1,0:T(8,128)} %bitcast.11, f32[2,1,16,256,256]{4,3,2,1,0:T(8,128)} %coarse.3, f32[256,256]{1,0:T(8,128)} %basis_y.11, f32[256,256]{1,0:T(8,128)} %basis_z.7), custom_call_target="tpu_custom_call" | custom-call | flops 3221225472 | bytes 12582912 | tf_op jit(solution)/shard_map/forward/pallas_call | solution.py:75
  37.4 28.7 %faces.1 = (f32[16,5,16,256]{3,2,1,0:T(8,128)}, f32[16,2,16,256]{3,2,1,0:T(8,128)}) custom-call(f32[1]{0:T(128)} %get-tuple-element.76.own_rho, f32[256]{0:T(256)} %broadcast_multiply_fusion.shift, f32[1,256]{1,0:T(1,128)} %bitcast.12, f32[1,256]{1,0:T(1,128)} %bitcast.13, f32[16,256]{1,0:T(8,128)} %constant_dynamic-slice_fusion.own_x, f32[256,256]{1,0:T(8,128)} %basis_z.7, ...), custom_call_target="tpu_custom_call" | custom-call | flops 16777216 | bytes 65536 | tf_op jit(solution)/shard_map/faces/pallas_call | solution.py:239
  66.1 0.7 fusion
  66.9 0.5 pad_maximum_fusion.ends
  67.4 1.4 add_multiply_fusion.base
  68.8 4.3 %collective-permute-done.2 = f32[16,2,16,256]{3,2,1,0:T(8,128)S(1)} collective-permute-done((f32[16,2,16,256]{3,2,1,0:T(8,128)}, f32[16,2,16,256]{3,2,1,0:T(8,128)S(1)}, u32[]{:S(2)}, u32[]{:S(2)}) %collective-permute-start.2) | collective-permute-done | bytes 524320 | tf_op jit(solution)/shard_map/ppermute | solution.py:402
  73.1 1.9 %slice_subtract_fusion = f32[16,2,16,256]{3,2,1,0:T(8,128)} fusion(f32[16,2,16,256]{3,2,1,0:T(8,128)S(1)} %collective-permute-done.2, f32[16,5,16,256]{3,2,1,0:T(8,128)} %get-tuple-element.41.pieces), kind=kLoop, calls=%fused_computation | loop fusion | flops 131072 | bytes 1572864 | tf_op jit(solution)/shard_map/sub | solution.py:450
  75.1 1.0 all-to-all-done.lines
  76.1 10.1 %all-to-all-start.1 = ((f32[16,2,16,256]{3,2,1,0:T(8,128)}), f32[16,2,16,256]{3,2,1,0:T(8,128)S(1)}, u32[]{:S(2)}, u32[]{:S(2)}) async-start(f32[16,2,16,256]{3,2,1,0:T(8,128)} %slice_subtract_fusion), calls=%async_computation.1 | async-start | bytes 1048576 | tf_op jit(solution)/shard_map/all_to_all | solution.py:418
  86.3 0.6 dynamic_slice.15.shift
  86.9 7.4 %middle.1 = f32[16,2,16,16,128]{4,3,2,1,0:T(8,128)} custom-call(f32[256,256]{1,0:T(8,128)} %add_multiply_fusion.base, f32[16]{0:T(128)} %dynamic_slice.15.shift, f32[256,256]{1,0:T(8,128)} %basis_x.3, f32[16,2,16,16,128]{4,3,2,1,0:T(8,128)} %all-to-all-done.lines), custom_call_target="tpu_custom_call" | custom-call | flops 3221225472 | bytes 8388608 | tf_op jit(solution)/shard_map/middle/pallas_call | solution.py:117
  94.3 2.1 %all-to-all-done.1 = f32[16,2,16,256]{3,2,1,0:T(8,128)S(1)} async-done(((f32[16,2,16,256]{3,2,1,0:T(8,128)}), f32[16,2,16,256]{3,2,1,0:T(8,128)S(1)}, u32[]{:S(2)}, u32[]{:S(2)}) %all-to-all-start.1) | async-done | bytes 524320 | tf_op jit(solution)/shard_map/all_to_all | solution.py:418
  96.4 0.1 broadcast_in_dim.25
  96.5 15.1 %all_to_all.20.jumps = f32[16,2,16,256]{3,2,1,0:T(8,128)} all-to-all(f32[16,2,16,256]{3,2,1,0:T(8,128)S(1)} %broadcast_in_dim.25), channel_id=1, replica_groups=mesh['sub'=8,'slab'=16] {'slab'}, dimensions={0} | all-to-all | bytes 1048576 | tf_op jit(solution)/shard_map/all_to_all | solution.py:418
  111.6 4.7 %all-to-all-start.3 = ((f32[16,2,16,16,128]{4,3,2,1,0:T(8,128)}), f32[16,2,16,16,128]{4,3,2,1,0:T(8,128)}, u32[]{:S(2)}, u32[]{:S(2)}) async-start(f32[16,2,16,16,128]{4,3,2,1,0:T(8,128)} %middle.1), calls=%async_computation.3 | async-start | bytes 8388608 | tf_op jit(solution)/shard_map/all_to_all | solution.py:418
  117.5 4.3 %chain0.1 = (f32[16,256]{1,0:T(8,128)}, f32[256,256]{1,0:T(8,128)}, f32[8,128]{1,0:T(8,128)}) custom-call(f32[1]{0:T(128)} %bitcast.2.scale, f32[16,2,16,256]{3,2,1,0:T(8,128)} %all_to_all.20.jumps, f32[256,256]{1,0:T(8,128)} %get-tuple-element.51.gram_x, f32[256,256]{1,0:T(8,128)} %get-tuple-element.52.gram_y, f32[256,256]{1,0:T(8,128)} %stiff.3, ...), custom_call_target="tpu_custom_call" | custom-call | flops 16777216 | bytes 65536 | tf_op jit(solution)/shard_map/chain0/pallas_call | solution.py:341
  123.2 0.7 collective-permute-start.4
  123.9 0.6 pad_maximum_fusion.1.scale
  124.5 1.1 collective-permute-start.8
  125.6 0.0 collective-permute-done.4
  125.6 0.7 add.66
  126.3 1.6 collective-permute-done.3.before
  127.9 1.7 collective-permute-start.7
  129.6 1.2 collective-permute-start.6
  130.8 1.2 collective-permute-start.5
  132.0 9.7 %extra0.1.refs_0_ = f32[16,2,16,16,128]{4,3,2,1,0:T(8,128)} custom-call(f32[256,256]{1,0:T(8,128)} %add_multiply_fusion.base, f32[256]{0:T(256)} %broadcast_multiply_fusion.shift, f32[16,256]{1,0:T(8,128)} %constant_dynamic-slice_fusion.own_x, f32[2,256]{1,0:T(2,128)} %pad_maximum_fusion.ends, f32[256,256]{1,0:T(8,128)} %get-tuple-element.53.own.image, ...), custom_call_target="tpu_custom_call" | custom-call | flops 8999999488 | bytes 65536 | tf_op jit(solution)/shard_map/extra0/pallas_call | solution.py:283
  141.7 0.0 collective-permute-done.5
  141.7 0.6 add_add_fusion.1.sums_in.sums0
  142.3 0.7 copy-done.1
  143.0 5.5 %chain1.1 = (f32[8,128]{1,0:T(8,128)}, f32[16,256]{1,0:T(8,128)}, f32[16,256]{1,0:T(8,128)}) custom-call(f32[2]{0:T(128)} %pad_maximum_fusion.1.scale, f32[8,128]{1,0:T(8,128)} %add_add_fusion.1.sums_in.sums0, f32[16,2,16,256]{3,2,1,0:T(8,128)} %all_to_all.20.jumps, f32[256,256]{1,0:T(8,128)} %get-tuple-element.53.own.image, f32[256,256]{1,0:T(8,128)} %copy-done, ...), custom_call_target="tpu_custom_call" | custom-call | flops 16777216 | bytes 65536 | tf_op jit(solution)/shard_map/chain1/pallas_call | solution.py:371
  148.5 8.4 %extra1.1.refs_0_ = f32[16,2,16,16,128]{4,3,2,1,0:T(8,128)} custom-call(f32[256,256]{1,0:T(8,128)} %add_multiply_fusion.base, f32[256]{0:T(256)} %broadcast_multiply_fusion.shift, f32[16,256]{1,0:T(8,128)} %constant_dynamic-slice_fusion.own_x, f32[2,256]{1,0:T(2,128)} %pad_maximum_fusion.ends, ...), custom_call_target="tpu_custom_call", output_to_operand_aliasing={{}: (6, {})} | custom-call | flops 7500000256 | bytes 65536 | tf_op jit(solution)/shard_map/extra1/pallas_call | solution.py:283
  156.9 1.8 %collective-permute-start.12 = (f32[8,128]{1,0:T(8,128)S(1)}, f32[8,128]{1,0:T(8,128)S(1)}, u32[]{:S(2)}, u32[]{:S(2)}) collective-permute-start(f32[8,128]{1,0:T(8,128)S(1)} %add.70), channel_id=1, source_target_pairs={{0,96},{16,112},{32,64},{48,80},{64,32},{80,48},{96,0},{112,16},{1... | collective-permute-start | bytes 12296 | tf_op jit(solution)/shard_map/ppermute | solution.py:406
  158.7 1.2 collective-permute-start.11
  159.9 1.2 collective-permute-start.10
  161.1 8.4 %extra2.1.extra = f32[16,2,16,16,128]{4,3,2,1,0:T(8,128)} custom-call(f32[256,256]{1,0:T(8,128)} %add_multiply_fusion.base, f32[256]{0:T(256)} %broadcast_multiply_fusion.shift, f32[16,256]{1,0:T(8,128)} %constant_dynamic-slice_fusion.own_x, f32[2,256]{1,0:T(2,128)} %pad_maximum_fusion.ends, ...), custom_call_target="tpu_custom_call", output_to_operand_aliasing={{}: (6, {})} | custom-call | flops 7500000256 | bytes 65536 | tf_op jit(solution)/shard_map/extra2/pallas_call | solution.py:283
  169.5 0.6 add_add_fusion.sums1
  170.1 9.3 %backward.1 = (f32[16,256,256]{2,1,0:T(8,128)}, f32[16,256]{1,0:T(8,128)}) custom-call(f32[8,128]{1,0:T(8,128)} %add_add_fusion.1.sums_in.sums0, f32[8,128]{1,0:T(8,128)} %add_add_fusion.sums1, f32[16,256]{1,0:T(8,128)} %get-tuple-element.66.first, f32[16,256]{1,0:T(8,128)} %get-tuple-element.67.change, f32[16,2,16,16,128]{4,3,2,1,0:T(8,128)} %all-to-all-done.3.field, ...), custom_call_target="tpu_custom_call" | custom-call | flops 3221225472 | bytes 12582912 | tf_op jit(solution)/shard_map/backward/pallas_call | solution.py:162
  (31 shorter events, 0.1 us)
Async XLA Ops:
  0.6 13.7 %collective-permute-start = (f32[256]{0:T(256)}, f32[256]{0:T(256)S(1)}, u32[]{:S(2)}, u32[]{:S(2)}) collective-permute-start(f32[256]{0:T(256)} %param.16), channel_id=1, source_target_pairs={{15,0},{0,1},{1,2},{2,3},{3,4},{4,5},{5,6},{6,7},{7,8},{8,9},{9,10... | collective-permute-start | bytes 3080 | tf_op jit(solution)/shard_map/ppermute | solution.py:402
  2.6 11.7 %collective-permute-start.1 = (f32[256]{0:T(256)}, f32[256]{0:T(256)S(1)}, u32[]{:S(2)}, u32[]{:S(2)}) collective-permute-start(f32[256]{0:T(256)} %param.18), channel_id=1, source_target_pairs={{12,0},{13,1},{14,2},{15,3},{0,4},{1,5},{2,6},{3,7},{4,8},{5,9},{6... | collective-permute-start | bytes 3080 | tf_op jit(solution)/shard_map/ppermute | solution.py:402
  14.3 10.0 %copy-start.4 = (f32[8]{0:T(128)S(1)}, f32[8]{0:T(128)}, u32[]{:S(2)}) copy-start(f32[8]{0:T(128)} %param.12) | copy-start | bytes 100
  14.3 12.0 %copy-start.7 = (f32[256]{0:T(256)S(1)}, f32[256]{0:T(256)}, u32[]{:S(2)}) copy-start(f32[256]{0:T(256)} %param.17) | copy-start | bytes 3076
  14.3 7.4 %copy-start.8 = (f32[256]{0:T(256)}, f32[256]{0:T(256)S(1)}, u32[]{:S(2)}) copy-start(f32[256]{0:T(256)S(1)} %collective-permute-done) | copy-start | bytes 3076
  14.3 7.4 %copy-start.9 = (f32[256]{0:T(256)}, f32[256]{0:T(256)S(1)}, u32[]{:S(2)}) copy-start(f32[256]{0:T(256)S(1)} %collective-permute-done.1) | copy-start | bytes 3076
  14.3 61.8 %all-to-all-start = ((f32[16,2,16,16,128]{4,3,2,1,0:T(8,128)}), f32[16,2,16,16,128]{4,3,2,1,0:T(8,128)}, u32[]{:S(2)}, u32[]{:S(2)}) async-start(f32[16,2,16,16,128]{4,3,2,1,0:T(8,128)} %forward.2.part1), calls=%async_computation | async-start | bytes 8388608 | tf_op jit(solution)/shard_map/all_to_all | solution.py:418
  37.4 30.0 %copy-start.5 = (f32[256]{0:T(256)S(1)}, f32[256]{0:T(256)}, u32[]{:S(2)}) copy-start(f32[256]{0:T(256)} %param.16) | copy-start | bytes 3076
  37.4 30.0 %copy-start.6 = (f32[256]{0:T(256)S(1)}, f32[256]{0:T(256)}, u32[]{:S(2)}) copy-start(f32[256]{0:T(256)} %param.18) | copy-start | bytes 3076
  37.4 48.9 %copy-start.3 = (f32[256]{0:T(256)S(1)}, f32[256]{0:T(256)}, u32[]{:S(2)}) copy-start(f32[256]{0:T(256)} %broadcast_multiply_fusion.shift) | copy-start | bytes 3076
  66.1 7.0 %collective-permute-start.2 = (f32[16,2,16,256]{3,2,1,0:T(8,128)}, f32[16,2,16,256]{3,2,1,0:T(8,128)S(1)}, u32[]{:S(2)}, u32[]{:S(2)}) collective-permute-start(f32[16,2,16,256]{3,2,1,0:T(8,128)} %get-tuple-element.42), channel_id=1, source_target_pairs={{16,0},{32,16},{48,32},{64,48},{80,64},{96,80},{112,96},{0,112},{1... | collective-permute-start | bytes 1572872 | tf_op jit(solution)/shard_map/ppermute | solution.py:402
  76.1 20.3 %all-to-all-start.1 = ((f32[16,2,16,256]{3,2,1,0:T(8,128)}), f32[16,2,16,256]{3,2,1,0:T(8,128)S(1)}, u32[]{:S(2)}, u32[]{:S(2)}) async-start(f32[16,2,16,256]{3,2,1,0:T(8,128)} %slice_subtract_fusion), calls=%async_computation.1 | async-start | bytes 1048576 | tf_op jit(solution)/shard_map/all_to_all | solution.py:418
  111.6 58.5 %all-to-all-start.3 = ((f32[16,2,16,16,128]{4,3,2,1,0:T(8,128)}), f32[16,2,16,16,128]{4,3,2,1,0:T(8,128)}, u32[]{:S(2)}, u32[]{:S(2)}) async-start(f32[16,2,16,16,128]{4,3,2,1,0:T(8,128)} %middle.1), calls=%async_computation.3 | async-start | bytes 8388608 | tf_op jit(solution)/shard_map/all_to_all | solution.py:418
  121.9 6.0 %collective-permute-start.3 = (f32[256,256]{1,0:T(8,128)}, f32[256,256]{1,0:T(8,128)S(1)}, u32[]{:S(2)}, u32[]{:S(2)}) collective-permute-start(f32[256,256]{1,0:T(8,128)} %get-tuple-element.53.own.image), channel_id=1, source_target_pairs={{112,0},{0,16},{16,32},{32,48},{48,64},{64,80},{80,96},{96,112},{1... | collective-permute-start | bytes 786440 | tf_op jit(solution)/shard_map/ppermute | solution.py:402
  123.2 2.4 %collective-permute-start.4 = (f32[8,128]{1,0:T(8,128)}, f32[8,128]{1,0:T(8,128)S(1)}, u32[]{:S(2)}, u32[]{:S(2)}) collective-permute-start(f32[8,128]{1,0:T(8,128)} %get-tuple-element.54), channel_id=1, source_target_pairs={{0,16},{16,0},{32,48},{48,32},{64,80},{80,64},{96,112},{112,96},{1... | collective-permute-start | bytes 12296 | tf_op jit(solution)/shard_map/ppermute | solution.py:406
  124.5 17.9 %collective-permute-start.8 = (f32[256,256]{1,0:T(8,128)}, f32[256,256]{1,0:T(8,128)S(1)}, u32[]{:S(2)}, u32[]{:S(2)}) collective-permute-start(f32[256,256]{1,0:T(8,128)} %get-tuple-element.53.own.image), channel_id=1, source_target_pairs={{16,0},{32,16},{48,32},{64,48},{80,64},{96,80},{112,96},{0,112},{1... | collective-permute-start | bytes 786440 | tf_op jit(solution)/shard_map/ppermute | solution.py:402
  127.9 4.1 %copy-start = (f32[256,256]{1,0:T(8,128)}, f32[256,256]{1,0:T(8,128)S(1)}, u32[]{:S(2)}) copy-start(f32[256,256]{1,0:T(8,128)S(1)} %collective-permute-done.3.before) | copy-start | bytes 786436
  127.9 13.8 %collective-permute-start.7 = (f32[8,128]{1,0:T(8,128)S(1)}, f32[8,128]{1,0:T(8,128)S(1)}, u32[]{:S(2)}, u32[]{:S(2)}) collective-permute-start(f32[8,128]{1,0:T(8,128)S(1)} %add.66), channel_id=1, source_target_pairs={{0,96},{16,112},{32,64},{48,80},{64,32},{80,48},{96,0},{112,16},{1... | collective-permute-start | bytes 12296 | tf_op jit(solution)/shard_map/ppermute | solution.py:406
  129.6 12.1 %collective-permute-start.6 = (f32[8,128]{1,0:T(8,128)S(1)}, f32[8,128]{1,0:T(8,128)S(1)}, u32[]{:S(2)}, u32[]{:S(2)}) collective-permute-start(f32[8,128]{1,0:T(8,128)S(1)} %add.66), channel_id=1, source_target_pairs={{0,64},{16,80},{32,96},{48,112},{64,0},{80,16},{96,32},{112,48},{1... | collective-permute-start | bytes 12296 | tf_op jit(solution)/shard_map/ppermute | solution.py:406
  130.8 10.9 %collective-permute-start.5 = (f32[8,128]{1,0:T(8,128)S(1)}, f32[8,128]{1,0:T(8,128)S(1)}, u32[]{:S(2)}, u32[]{:S(2)}) collective-permute-start(f32[8,128]{1,0:T(8,128)S(1)} %add.66), channel_id=1, source_target_pairs={{0,32},{16,48},{32,0},{48,16},{64,96},{80,112},{96,64},{112,80},{1... | collective-permute-start | bytes 12296 | tf_op jit(solution)/shard_map/ppermute | solution.py:406
  142.3 0.7 copy-start.1
  148.5 8.4 %copy-start.2 = (f32[8,128]{1,0:T(8,128)S(1)}, f32[8,128]{1,0:T(8,128)}, u32[]{:S(2)}) copy-start(f32[8,128]{1,0:T(8,128)} %get-tuple-element.61) | copy-start | bytes 12292
  148.5 8.4 %collective-permute-start.9 = (f32[8,128]{1,0:T(8,128)}, f32[8,128]{1,0:T(8,128)S(1)}, u32[]{:S(2)}, u32[]{:S(2)}) collective-permute-start(f32[8,128]{1,0:T(8,128)} %get-tuple-element.61), channel_id=1, source_target_pairs={{0,16},{16,0},{32,48},{48,32},{64,80},{80,64},{96,112},{112,96},{1... | collective-permute-start | bytes 12296 | tf_op jit(solution)/shard_map/ppermute | solution.py:406
  156.9 12.5 %collective-permute-start.12 = (f32[8,128]{1,0:T(8,128)S(1)}, f32[8,128]{1,0:T(8,128)S(1)}, u32[]{:S(2)}, u32[]{:S(2)}) collective-permute-start(f32[8,128]{1,0:T(8,128)S(1)} %add.70), channel_id=1, source_target_pairs={{0,96},{16,112},{32,64},{48,80},{64,32},{80,48},{96,0},{112,16},{1... | collective-permute-start | bytes 12296 | tf_op jit(solution)/shard_map/ppermute | solution.py:406
  158.7 10.7 %collective-permute-start.11 = (f32[8,128]{1,0:T(8,128)S(1)}, f32[8,128]{1,0:T(8,128)S(1)}, u32[]{:S(2)}, u32[]{:S(2)}) collective-permute-start(f32[8,128]{1,0:T(8,128)S(1)} %add.70), channel_id=1, source_target_pairs={{0,64},{16,80},{32,96},{48,112},{64,0},{80,16},{96,32},{112,48},{1... | collective-permute-start | bytes 12296 | tf_op jit(solution)/shard_map/ppermute | solution.py:406
  159.9 9.6 %collective-permute-start.10 = (f32[8,128]{1,0:T(8,128)S(1)}, f32[8,128]{1,0:T(8,128)S(1)}, u32[]{:S(2)}, u32[]{:S(2)}) collective-permute-start(f32[8,128]{1,0:T(8,128)S(1)} %add.70), channel_id=1, source_target_pairs={{0,32},{16,48},{32,0},{48,16},{64,96},{80,112},{96,64},{112,80},{1... | collective-permute-start | bytes 12296 | tf_op jit(solution)/shard_map/ppermute | solution.py:406
